TPU v7x, 256 devices: a whole 4x4x8 slice. The times are simulated.
256 devices in a mesh: seq: 32 (over z, x), ch: 8 (over y, core).
Axes of the slice: x: 4, y: 4, z: 8, core: 2. Of those that a mesh axis runs over, the one named last changes fastest.
Arguments:
- grad_out: bfloat16 [16384, 4096], P('seq', 'ch'), may hold values from -6 to 6
- out_weight: bfloat16 [4096, 4096], P('seq', 'ch'), may hold values from -0.09375 to 0.09375
- gate_in: bfloat16 [4096, 16384], P('ch', 'seq'), may hold values from -6 to 6
- gate_out: bfloat16 [4096, 16384], P('ch', 'seq'), may hold values from -6 to 6
- values: bfloat16 [4096, 16384], P('ch', 'seq'), may hold values from -6 to 6
- conv_out: bfloat16 [4096, 16384], P('ch', 'seq'), may hold values from -6 to 6
- filters: float32 [4096, 16384], P('ch', 'seq'), may hold values from -1 to 1
- skip_scale: float32 [4096], P('ch'), may hold values from -4 to 4
Outputs:
- grad_gate_in: bfloat16 [4096, 16384], P('ch', 'seq')
- grad_values: bfloat16 [4096, 16384], P('ch', 'seq')
- grad_gate_out: bfloat16 [4096, 16384], P('ch', 'seq')
- grad_filters: float32 [4096, 16384], P('ch', 'seq')
All inputs are finite; a program needn't handle non-finite values.
Results may differ from a plain program's by a relative error of at most 0.0057.
Values may be sent and summed in bfloat16 or wider, within the bound.
A program may use at most 128 MiB of HBM per device.

v0:
```python
import math

import jax
import jax.numpy as jnp
from jax import lax
from jax.sharding import PartitionSpec as P


def angle_table(rows, cols, period):
    first = jnp.arange(rows, dtype=jnp.int32)
    second = jnp.arange(cols, dtype=jnp.int32)
    turns = first[:, None] * second[None, :] % period
    phase = turns.astype(jnp.float32) * (2.0 * math.pi / period)
    return (jnp.cos(phase), jnp.sin(phase))


def make_tables(total):
    power = total.bit_length() - 1
    outer = 2 ** (power // 2)
    inner = total // outer
    outer_cos, outer_sin = angle_table(outer // 2, outer, outer)
    twist_cos, twist_sin = angle_table(outer, inner, total)
    inner_cos, inner_sin = angle_table(inner, inner, inner)
    return (outer_cos, outer_sin, twist_cos, twist_sin, inner_cos, inner_sin)


def mult(form, left, right):
    return jnp.einsum(form, left, right, precision=lax.Precision.HIGHEST)


def forward(rows, tables):
    outer_cos, outer_sin, twist_cos, twist_sin, inner_cos, inner_sin = tables
    count = rows.shape[0]
    blocks = rows.reshape(count, outer_cos.shape[0], inner_cos.shape[0])
    first_real = mult("ak,cab->ckb", outer_cos, blocks)
    first_imag = -mult("ak,cab->ckb", outer_sin, blocks)
    turned_real = first_real * twist_cos + first_imag * twist_sin
    turned_imag = first_imag * twist_cos - first_real * twist_sin
    spec_real = mult("ckb,bj->ckj", turned_real, inner_cos) + mult(
        "ckb,bj->ckj", turned_imag, inner_sin
    )
    spec_imag = mult("ckb,bj->ckj", turned_imag, inner_cos) - mult(
        "ckb,bj->ckj", turned_real, inner_sin
    )
    return (spec_real, spec_imag)


def inverse(spec_real, spec_imag, tables):
    outer_cos, outer_sin, twist_cos, twist_sin, inner_cos, inner_sin = tables
    count = spec_real.shape[0]
    back_real = mult("ckj,jb->ckb", spec_real, inner_cos) - mult(
        "ckj,jb->ckb", spec_imag, inner_sin
    )
    back_imag = mult("ckj,jb->ckb", spec_imag, inner_cos) + mult(
        "ckj,jb->ckb", spec_real, inner_sin
    )
    turned_real = back_real * twist_cos - back_imag * twist_sin
    turned_imag = back_imag * twist_cos + back_real * twist_sin
    rows = mult("ak,ckb->cab", outer_cos, turned_real) - mult("ak,ckb->cab", outer_sin, turned_imag)
    half = outer_cos.shape[0]
    inner = inner_cos.shape[0]
    return rows.reshape(count, half * inner) / (2.0 * half * inner)


def shards(grad_out, out_weight, gate_in, gate_out, values, conv_out, filters, skip_scale):
    product = (gate_in.astype(jnp.float32) * values.astype(jnp.float32)).astype(jnp.bfloat16)
    weight_rows = lax.all_gather(out_weight, "seq", axis=0, tiled=True)
    back = lax.psum_scatter(
        lax.dot_general(
            weight_rows, grad_out, (((1,), (1,)), ((), ())), preferred_element_type=jnp.float32
        ),
        "ch",
        scatter_dimension=0,
        tiled=True,
    )
    grad_gate_out = (back * conv_out.astype(jnp.float32)).astype(jnp.bfloat16)
    gated = (back * gate_out.astype(jnp.float32)).astype(jnp.bfloat16)
    gated_rows, product_rows = (
        lax.all_to_all(gated, "seq", split_axis=0, concat_axis=1, tiled=True),
        lax.all_to_all(product, "seq", split_axis=0, concat_axis=1, tiled=True),
    )
    filter_rows = lax.all_to_all(filters, "seq", split_axis=0, concat_axis=1, tiled=True)
    length = gated_rows.shape[1]
    width = gated_rows.shape[0]
    tables = make_tables(2 * length)
    scale_rows = lax.dynamic_slice_in_dim(skip_scale, lax.axis_index("seq") * width, width, 0)
    gated_wide = gated_rows.astype(jnp.float32)
    grad_real, grad_imag = forward(gated_wide, tables)
    kern_real, kern_imag = forward(filter_rows, tables)
    mixed_rows = inverse(
        grad_real * kern_real + grad_imag * kern_imag,
        grad_imag * kern_real - grad_real * kern_imag,
        tables,
    )
    mixed_rows = (mixed_rows + scale_rows[:, None] * gated_wide).astype(jnp.bfloat16)
    prod_real, prod_imag = forward(product_rows.astype(jnp.float32), tables)
    filter_grad_rows = inverse(
        grad_real * prod_real + grad_imag * prod_imag,
        grad_imag * prod_real - grad_real * prod_imag,
        tables,
    )
    mixed = lax.all_to_all(mixed_rows, "seq", split_axis=1, concat_axis=0, tiled=True)
    grad_filters = lax.all_to_all(filter_grad_rows, "seq", split_axis=1, concat_axis=0, tiled=True)
    mixed_wide = mixed.astype(jnp.float32)
    grad_gate_in = (mixed_wide * values.astype(jnp.float32)).astype(jnp.bfloat16)
    grad_values = (mixed_wide * gate_in.astype(jnp.float32)).astype(jnp.bfloat16)
    return (grad_gate_in, grad_values, grad_gate_out, grad_filters)


def solution(mesh):
    placed = (
        P("seq", "ch"),
        P("seq", "ch"),
        P("ch", "seq"),
        P("ch", "seq"),
        P("ch", "seq"),
        P("ch", "seq"),
        P("ch", "seq"),
        P("ch"),
    )
    return jax.shard_map(
        shards,
        mesh=mesh,
        in_specs=placed,
        out_specs=(P("ch", "seq"), P("ch", "seq"), P("ch", "seq"), P("ch", "seq")),
        check_vma=False,
    )
```

profile of v0, /device:TPU:2, one launch (start us, length us, event | category | flops | bytes accessed | tf_op | source)
XLA Modules:
  0.0 317.8 jit_solution(10874490925379013492)
XLA Ops:
  8.0 86.2 %all-gather.2.cloned.1.call-done = bf16[4096,512]{1,0:T(8,128)(2,1)} async-done(((bf16[128,512]{1,0:T(8,128)(2,1)}), bf16[4096,512]{1,0:T(8,128)(2,1)}) %all-gather.2.cloned.1.call-update) | async-done | bytes 4194320 | tf_op jit(solution)/shard_map/all_gather | solution.py:67
  94.1 7.8 %fusion.290 = f32[4096,512]{1,0:T(8,128)} fusion(bf16[4096,512]{1,0:T(8,128)(2,1)} %all-gather.2.cloned.1.call-done, bf16[512,512]{1,0:T(8,128)(2,1)S(1)} %copy-done), kind=kOutput, calls=%fused_computation.273 | convolution fusion | flops 2147483648 | bytes 13107200 | tf_op jit(solution)/shard_map/dot_general | solution.py:69
  102.0 1.0 copy-done.11
  104.1 7.5 %all-to-all-start.3 = ((bf16[32,16,512]{2,1,0:T(8,128)(2,1)}), bf16[32,16,512]{2,1,0:T(8,128)(2,1)S(1)}, u32[]{:S(2)}, u32[]{:S(2)}) async-start(bf16[32,16,512]{2,1,0:T(8,128)(2,1)} %bitcast.16), calls=%async_computation.4 | async-start | bytes 1048576 | tf_op jit(solution)/shard_map/all_to_all | solution.py:80
  113.1 12.7 %all-to-all-done.3 = bf16[32,16,512]{2,1,0:T(8,128)(2,1)S(1)} async-done(((bf16[32,16,512]{2,1,0:T(8,128)(2,1)}), bf16[32,16,512]{2,1,0:T(8,128)(2,1)S(1)}, u32[]{:S(2)}, u32[]{:S(2)}) %all-to-all-start.3) | async-done | bytes 524320 | tf_op jit(solution)/shard_map/all_to_all | solution.py:80
  125.7 6.0 %all-to-all-start.1 = ((f32[32,16,512]{2,1,0:T(8,128)}), f32[32,16,512]{2,1,0:T(8,128)S(1)}, u32[]{:S(2)}, u32[]{:S(2)}) async-start(f32[32,16,512]{2,1,0:T(8,128)} %bitcast.8), calls=%async_computation.2 | async-start | bytes 2097152 | tf_op jit(solution)/shard_map/all_to_all | solution.py:82
  132.3 1.3 fusion.140
  133.6 1.3 fusion.148
  134.9 4.6 %fusion.74 = f32[16,128,256]{2,1,0:T(8,128)S(1)} fusion(f32[16,256,128]{2,1,0:T(8,128)S(1)} %fusion.148, f32[16,256,128]{2,1,0:T(8,128)S(1)} %fusion.140, f32[128,256]{0,1:T(8,128)S(1)} %get-tuple-element.14, f32[128,256]{0,1:T(8,128)S(1)} %get-tuple-element.15), kind=kOutput, calls=%fused_computation.79 | convolution fusion | flops 1613627392 | bytes 6553600 | tf_op jit(solution)/shard_map/ckb,bj->ckj/dot_general | solution.py:28
  139.5 4.8 %fusion.70 = f32[16,128,256]{2,1,0:T(8,128)S(1)} fusion(f32[16,256,128]{2,1,0:T(8,128)S(1)} %fusion.148, f32[16,256,128]{2,1,0:T(8,128)S(1)} %fusion.140, f32[128,256]{0,1:T(8,128)S(1)} %get-tuple-element.14, f32[128,256]{0,1:T(8,128)S(1)} %get-tuple-element.15), kind=kOutput, calls=%fused_computation.78 | convolution fusion | flops 1613627392 | bytes 6553600 | tf_op jit(solution)/shard_map/ckb,bj->ckj/dot_general | solution.py:28
  144.3 5.9 %convolution_add_fusion.1 = f32[16,128,256]{2,1,0:T(8,128)} fusion(f32[16,128,256]{2,1,0:T(8,128)S(1)} %fusion.74, f32[16,256,128]{2,1,0:T(8,128)S(1)} %fusion.148, f32[16,256,128]{2,1,0:T(8,128)S(1)} %fusion.140, f32[128,256]{0,1:T(8,128)S(1)} %get-tuple-element.14, f32[128,256]{0,1:T(8,128)S(1)} %get-tuple-element.15), kind=kOutput, calls=%fused_computation.47 | convolution fusion | flops 1614151680 | bytes 8650752 | tf_op jit(solution)/shard_map/ckb,bj->ckj/dot_general | solution.py:28
  150.1 5.9 %convolution_subtract_fusion.1 = f32[16,128,256]{2,1,0:T(8,128)} fusion(f32[16,128,256]{2,1,0:T(8,128)S(1)} %fusion.70, f32[16,256,128]{2,1,0:T(8,128)S(1)} %fusion.148, f32[16,256,128]{2,1,0:T(8,128)S(1)} %fusion.140, f32[128,256]{0,1:T(8,128)S(1)} %get-tuple-element.14, f32[128,256]{0,1:T(8,128)S(1)} %get-tuple-element.15), kind=kOutput, calls=%fused_computation.46 | convolution fusion | flops 1614151680 | bytes 8650752 | tf_op jit(solution)/shard_map/ckb,bj->ckj/dot_general | solution.py:28
  156.9 1.1 reshape.88
  158.1 3.3 %fusion.143 = f32[128,16,256]{2,0,1:T(8,128)S(1)} fusion(f32[16,64,256]{2,1,0:T(8,128)} %reshape.88), kind=kOutput, calls=%fused_computation.136 | convolution fusion | flops 402767872 | bytes 3145728 | tf_op jit(solution)/shard_map/ak,cab->ckb/dot_general | solution.py:28
  161.4 2.4 fusion.151
  163.8 1.3 copy-done.2
  165.1 4.3 %fusion.4 = f32[16,128,256]{2,1,0:T(8,128)} fusion(f32[128,16,256]{2,0,1:T(8,128)S(1)} %fusion.151, f32[128,16,256]{2,0,1:T(8,128)S(1)} %fusion.143, f32[128,256]{1,0:T(8,128)S(1)} %copy.44, f32[128,256]{1,0:T(8,128)S(1)} %copy.43), kind=kOutput, calls=%fused_computation.8 | convolution fusion | flops 1613627392 | bytes 6553600 | tf_op jit(solution)/shard_map/ckb,bj->ckj/dot_general | solution.py:28
  169.3 2.6 multiply_convert_fusion
  171.9 9.5 %all-to-all-start = ((bf16[32,16,512]{2,1,0:T(8,128)(2,1)}), bf16[32,16,512]{2,1,0:T(8,128)(2,1)S(1)}, u32[]{:S(2)}, u32[]{:S(2)}) async-start(bf16[32,16,512]{2,1,0:T(8,128)(2,1)} %bitcast.167), calls=%async_computation.1 | async-start | bytes 1048576 | tf_op jit(solution)/shard_map/all_to_all | solution.py:79
  181.4 4.7 %fusion.2 = f32[16,128,256]{2,1,0:T(8,128)S(1)} fusion(f32[128,16,256]{2,0,1:T(8,128)} %copy-done.2, f32[128,16,256]{2,0,1:T(8,128)S(1)} %fusion.143, f32[128,256]{1,0:T(8,128)S(1)} %copy.44, f32[128,256]{1,0:T(8,128)S(1)} %copy.43), kind=kOutput, calls=%fused_computation.6 | convolution fusion | flops 1613627392 | bytes 6553600 | tf_op jit(solution)/shard_map/ckb,bj->ckj/dot_general | solution.py:28
  186.1 4.3 %fusion.28 = f32[16,128,256]{2,1,0:T(8,128)} fusion(f32[16,128,256]{2,1,0:T(8,128)S(1)} %copy-done.10, f32[128,16,256]{2,0,1:T(8,128)S(1)} %copy-done.3, f32[128,16,256]{2,0,1:T(8,128)S(1)} %fusion.143, f32[128,256]{1,0:T(8,128)S(1)} %copy.44, f32[128,256]{1,0:T(8,128)S(1)} %copy.43), kind=kOutput, calls=%fused_computation.42 | convolution fusion | flops 1614151680 | bytes 8650752 | tf_op jit(solution)/shard_map/ckb,bj->ckj/dot_general | solution.py:28
  190.5 4.3 %fusion.31 = f32[16,128,256]{2,1,0:T(8,128)} fusion(f32[16,128,256]{2,1,0:T(8,128)S(1)} %fusion.2, f32[128,16,256]{2,0,1:T(8,128)S(1)} %copy-done.3, f32[128,16,256]{2,0,1:T(8,128)S(1)} %fusion.143, f32[128,256]{1,0:T(8,128)S(1)} %copy.44, f32[128,256]{1,0:T(8,128)S(1)} %copy.43), kind=kOutput, calls=%fused_computation.43 | convolution fusion | flops 1614151680 | bytes 8650752 | tf_op jit(solution)/shard_map/ckb,bj->ckj/dot_general | solution.py:28
  195.3 1.3 fusion.145
  196.6 1.5 fusion.153
  198.1 4.6 %fusion.64 = f32[16,128,256]{2,1,0:T(8,128)S(1)} fusion(f32[16,256,128]{2,1,0:T(8,128)S(1)} %fusion.153, f32[16,256,128]{2,1,0:T(8,128)S(1)} %fusion.145, f32[128,256]{0,1:T(8,128)S(1)} %get-tuple-element.14, f32[128,256]{0,1:T(8,128)S(1)} %get-tuple-element.15), kind=kOutput, calls=%fused_computation.76 | convolution fusion | flops 1613627392 | bytes 6553600 | tf_op jit(solution)/shard_map/ckb,bj->ckj/dot_general | solution.py:28
  202.7 4.6 %fusion.68 = f32[16,128,256]{2,1,0:T(8,128)S(1)} fusion(f32[16,256,128]{2,1,0:T(8,128)S(1)} %fusion.153, f32[16,256,128]{2,1,0:T(8,128)S(1)} %fusion.145, f32[128,256]{0,1:T(8,128)S(1)} %get-tuple-element.14, f32[128,256]{0,1:T(8,128)S(1)} %get-tuple-element.15), kind=kOutput, calls=%fused_computation.77 | convolution fusion | flops 1613627392 | bytes 6553600 | tf_op jit(solution)/shard_map/ckb,bj->ckj/dot_general | solution.py:28
  207.3 4.8 %convolution_subtract_fusion.3 = f32[16,128,256]{2,1,0:T(8,128)S(1)} fusion(f32[16,128,256]{2,1,0:T(8,128)S(1)} %fusion.64, f32[16,256,128]{2,1,0:T(8,128)S(1)} %fusion.153, f32[16,256,128]{2,1,0:T(8,128)S(1)} %fusion.145, f32[128,256]{0,1:T(8,128)S(1)} %get-tuple-element.14, f32[128,256]{0,1:T(8,128)S(1)} %get-tuple-element.15), kind=kOutput, calls=%fused_computation.50 | convolution fusion | flops 1614151680 | bytes 8650752 | tf_op jit(solution)/shard_map/ckb,bj->ckj/dot_general | solution.py:28
  212.1 5.6 %multiply_subtract_fusion = (f32[16,128,256]{2,1,0:T(8,128)S(1)}, f32[16,128,256]{2,1,0:T(8,128)S(1)}, f32[16,128,256]{2,1,0:T(8,128)S(1)}, f32[16,128,256]{2,1,0:T(8,128)S(1)}) fusion(f32[16,128,256]{2,1,0:T(8,128)S(1)} %copy-done.7, f32[16,128,256]{2,1,0:T(8,128)S(1)} %convolution_subtract_fusion.3, f32[16,128,256]{2,1,0:T(8,128)S(1)} %copy-done.6, ...), kind=kOutput, calls=%fused_computation.28 | convolution fusion | flops 1620443136 | bytes 25427968 | tf_op jit(solution)/shard_map/ckb,bj->ckj/dot_general | solution.py:28
  217.8 3.0 fusion.89
  220.8 4.7 %fusion.91 = f32[16,128,256]{1,2,0:T(8,128)} fusion(f32[16,128,256]{2,1,0:T(8,128)S(1)} %get-tuple-element.5), kind=kOutput, calls=%fused_computation.98 | convolution fusion | flops 1611530240 | bytes 4194304 | tf_op jit(solution)/shard_map/ckj,jb->ckb/dot_general | solution.py:28
  225.5 4.4 %convolution_add_fusion = f32[16,128,256]{1,2,0:T(8,128)} fusion(f32[16,128,256]{1,2,0:T(8,128)S(1)} %fusion.89, f32[16,128,256]{2,1,0:T(8,128)S(1)} %get-tuple-element.5), kind=kOutput, calls=%fused_computation.44 | convolution fusion | flops 1612054528 | bytes 6291456 | tf_op jit(solution)/shard_map/ckj,jb->ckb/dot_general | solution.py:28
  229.9 3.0 fusion.95
  232.9 3.0 fusion.97
  236.0 3.2 %convolution_add_fusion.2 = f32[16,128,256]{1,2,0:T(8,128)S(1)} fusion(f32[16,128,256]{1,2,0:T(8,128)S(1)} %fusion.95, f32[16,128,256]{2,1,0:T(8,128)S(1)} %get-tuple-element.8), kind=kOutput, calls=%fused_computation.48 | convolution fusion | flops 1612054528 | bytes 6291456 | tf_op jit(solution)/shard_map/ckj,jb->ckb/dot_general | solution.py:28
  239.2 3.0 convolution_subtract_fusion.2
  242.2 2.8 fusion.20
  245.0 3.8 %fusion.49 = f32[16,64,256]{2,1,0:T(8,128)} fusion(f32[16,256,64]{1,2,0:T(8,128)S(1)} %fusion.20, f32[16,128,256]{1,2,0:T(8,128)S(1)} %convolution_add_fusion.2, f32[16,128,256]{1,2,0:T(8,128)S(1)} %convolution_subtract_fusion.2, f32[128,256]{0,1:T(8,128)S(1)} %get-tuple-element.14, f32[128,256]{0,1:T(8,128)S(1)} %get-tuple-element.15), kind=kOutput, calls=%fused_computation.57 | convolution fusion | flops 404865024 | bytes 6553600 | tf_op jit(solution)/shard_map/ak,ckb->cab/dot_general | solution.py:28
  248.8 2.5 div.16
  251.3 2.7 fusion.55
  254.0 10.2 %all-to-all-start.2 = ((bf16[16,32,512]{2,0,1:T(8,128)(2,1)}), bf16[16,32,512]{2,0,1:T(8,128)(2,1)}, u32[]{:S(2)}, u32[]{:S(2)}) async-start(bf16[16,32,512]{2,0,1:T(8,128)(2,1)} %fusion.55), calls=%async_computation.3 | async-start | bytes 1048576 | tf_op jit(solution)/shard_map/all_to_all | solution.py:102
  264.2 4.8 %convolution_subtract_fusion = f32[16,128,256]{1,2,0:T(8,128)S(1)} fusion(f32[16,128,256]{1,2,0:T(8,128)} %fusion.91, f32[16,128,256]{2,1,0:T(8,128)S(1)} %get-tuple-element.4), kind=kOutput, calls=%fused_computation.45 | convolution fusion | flops 1612054528 | bytes 6291456 | tf_op jit(solution)/shard_map/ckj,jb->ckb/dot_general | solution.py:28
  269.1 2.8 fusion.12
  271.9 2.8 fusion.43
  275.0 1.6 copy.65
  276.7 9.8 %all-to-all-start.4 = ((f32[16,32,512]{2,0,1:T(8,128)}), f32[16,32,512]{2,0,1:T(8,128)S(1)}, u32[]{:S(2)}, u32[]{:S(2)}) async-start(f32[16,32,512]{2,0,1:T(8,128)} %copy.65), calls=%async_computation.5 | async-start | bytes 2097152 | tf_op jit(solution)/shard_map/all_to_all | solution.py:103
  286.5 2.3 fusion.53
  288.8 21.0 %all-to-all-done.4 = f32[16,32,512]{2,0,1:T(8,128)S(1)} async-done(((f32[16,32,512]{2,0,1:T(8,128)}), f32[16,32,512]{2,0,1:T(8,128)S(1)}, u32[]{:S(2)}, u32[]{:S(2)}) %all-to-all-start.4) | async-done | bytes 1048608 | tf_op jit(solution)/shard_map/all_to_all | solution.py:103
  309.8 1.0 copy.90
  (49 shorter events, 5.7 us)
Async XLA Ops:
  7.2 87.0 %copy-start = (bf16[512,512]{1,0:T(8,128)(2,1)S(1)}, bf16[512,512]{1,0:T(8,128)(2,1)}, u32[]{:S(2)}) copy-start(bf16[512,512]{1,0:T(8,128)(2,1)} %param.8) | copy-start | bytes 1572868
  7.2 86.9 %all-gather.2.cloned.1.call-start = ((), (), s32[]{:S(2)}) async-start(), calls=%async_computation.6 | async-start | bytes 4325376 | tf_op jit(solution)/shard_map/all_gather | solution.py:67
  7.9 161.4 %reduce-scatter.2.cloned.1.call-start = ((), (), s32[]{:S(2)}) async-start(), calls=%async_computation.7 | async-start | bytes 9437184 | tf_op jit(solution)/shard_map/reduce_scatter | solution.py:68
  102.0 1.0 copy-start.11
  102.0 1.2 copy-start.13
  104.1 21.7 %all-to-all-start.3 = ((bf16[32,16,512]{2,1,0:T(8,128)(2,1)}), bf16[32,16,512]{2,1,0:T(8,128)(2,1)S(1)}, u32[]{:S(2)}, u32[]{:S(2)}) async-start(bf16[32,16,512]{2,1,0:T(8,128)(2,1)} %bitcast.16), calls=%async_computation.4 | async-start | bytes 1048576 | tf_op jit(solution)/shard_map/all_to_all | solution.py:80
  125.7 30.6 %all-to-all-start.1 = ((f32[32,16,512]{2,1,0:T(8,128)}), f32[32,16,512]{2,1,0:T(8,128)S(1)}, u32[]{:S(2)}, u32[]{:S(2)}) async-start(f32[32,16,512]{2,1,0:T(8,128)} %bitcast.8), calls=%async_computation.2 | async-start | bytes 2097152 | tf_op jit(solution)/shard_map/all_to_all | solution.py:82
  158.1 3.3 %copy-start.5 = (f32[16,64,256]{2,1,0:T(8,128)S(1)}, f32[16,64,256]{2,1,0:T(8,128)}, u32[]{:S(2)}) copy-start(f32[16,64,256]{2,1,0:T(8,128)} %reshape.88) | copy-start | bytes 3145732
  163.7 1.3 copy-start.2
  165.1 4.3 %copy-start.15 = (bf16[512,512]{1,0:T(8,128)(2,1)S(1)}, bf16[512,512]{1,0:T(8,128)(2,1)}, u32[]{:S(2)}) copy-start(bf16[512,512]{1,0:T(8,128)(2,1)} %param.13) | copy-start | bytes 1572868
  171.9 22.9 %all-to-all-start = ((bf16[32,16,512]{2,1,0:T(8,128)(2,1)}), bf16[32,16,512]{2,1,0:T(8,128)(2,1)S(1)}, u32[]{:S(2)}, u32[]{:S(2)}) async-start(bf16[32,16,512]{2,1,0:T(8,128)(2,1)} %bitcast.167), calls=%async_computation.1 | async-start | bytes 1048576 | tf_op jit(solution)/shard_map/all_to_all | solution.py:79
  181.4 4.7 %copy-start.3 = (f32[128,16,256]{2,0,1:T(8,128)S(1)}, f32[128,16,256]{2,0,1:T(8,128)}, u32[]{:S(2)}) copy-start(f32[128,16,256]{2,0,1:T(8,128)} %copy-done.2) | copy-start | bytes 6291460
  181.4 4.7 %copy-start.10 = (f32[16,128,256]{2,1,0:T(8,128)S(1)}, f32[16,128,256]{2,1,0:T(8,128)}, u32[]{:S(2)}) copy-start(f32[16,128,256]{2,1,0:T(8,128)} %fusion.4) | copy-start | bytes 6291460
  207.3 4.9 %copy-start.6 = (f32[16,128,256]{2,1,0:T(8,128)S(1)}, f32[16,128,256]{2,1,0:T(8,128)}, u32[]{:S(2)}) copy-start(f32[16,128,256]{2,1,0:T(8,128)} %convolution_add_fusion.1) | copy-start | bytes 6291460
  207.3 4.9 %copy-start.7 = (f32[16,128,256]{2,1,0:T(8,128)S(1)}, f32[16,128,256]{2,1,0:T(8,128)}, u32[]{:S(2)}) copy-start(f32[16,128,256]{2,1,0:T(8,128)} %convolution_subtract_fusion.1) | copy-start | bytes 6291460
  207.3 4.9 %copy-start.8 = (f32[16,128,256]{2,1,0:T(8,128)S(1)}, f32[16,128,256]{2,1,0:T(8,128)}, u32[]{:S(2)}) copy-start(f32[16,128,256]{2,1,0:T(8,128)} %fusion.28) | copy-start | bytes 6291460
  207.3 4.9 %copy-start.9 = (f32[16,128,256]{2,1,0:T(8,128)S(1)}, f32[16,128,256]{2,1,0:T(8,128)}, u32[]{:S(2)}) copy-start(f32[16,128,256]{2,1,0:T(8,128)} %fusion.31) | copy-start | bytes 6291460
  254.0 22.8 %all-to-all-start.2 = ((bf16[16,32,512]{2,0,1:T(8,128)(2,1)}), bf16[16,32,512]{2,0,1:T(8,128)(2,1)}, u32[]{:S(2)}, u32[]{:S(2)}) async-start(bf16[16,32,512]{2,0,1:T(8,128)(2,1)} %fusion.55), calls=%async_computation.3 | async-start | bytes 1048576 | tf_op jit(solution)/shard_map/all_to_all | solution.py:102
  264.2 4.9 %copy-start.4 = (f32[16,128,256]{1,2,0:T(8,128)S(1)}, f32[16,128,256]{1,2,0:T(8,128)}, u32[]{:S(2)}) copy-start(f32[16,128,256]{1,2,0:T(8,128)} %convolution_add_fusion) | copy-start | bytes 6291460
  275.0 11.5 %copy-start.12 = (bf16[512,512]{1,0:T(8,128)(2,1)S(1)}, bf16[512,512]{1,0:T(8,128)(2,1)}, u32[]{:S(2)}) copy-start(bf16[512,512]{1,0:T(8,128)(2,1)} %param.10) | copy-start | bytes 1572868
  276.5 9.9 %copy-start.14 = (bf16[512,512]{1,0:T(8,128)(2,1)S(1)}, bf16[512,512]{1,0:T(8,128)(2,1)}, u32[]{:S(2)}) copy-start(bf16[512,512]{1,0:T(8,128)(2,1)} %param.12) | copy-start | bytes 1572868
  276.7 33.1 %all-to-all-start.4 = ((f32[16,32,512]{2,0,1:T(8,128)}), f32[16,32,512]{2,0,1:T(8,128)S(1)}, u32[]{:S(2)}, u32[]{:S(2)}) async-start(f32[16,32,512]{2,0,1:T(8,128)} %copy.65), calls=%async_computation.5 | async-start | bytes 2097152 | tf_op jit(solution)/shard_map/all_to_all | solution.py:103
  286.5 24.3 %copy-start.1 = (bf16[512,512]{1,0:T(8,128)(2,1)S(1)}, bf16[512,512]{1,0:T(8,128)(2,1)}, u32[]{:S(2)}) copy-start(bf16[512,512]{1,0:T(8,128)(2,1)} %param.8) | copy-start | bytes 1572868
Sparse Core Ops, SparseCore 0:
  10.6 83.4 all-gather.1
  102.1 53.6 reduce-scatter.1
where the time goes:
time: 322 us; the launch traced here: 318 us
  waiting for transfers between devices  121 us (38%)
  matrix products  119 us (37%)
  starting transfers between devices  43 us (13%)
  between operations  14.7 us (5%)
  local copies, waits for them, and re-layouts  11.6 us (4%)
  other arithmetic  8.98 us (3%)
    dot_general x30, matrix products, mult(): return jnp.einsum(form, left, right, precision=lax.Precision.HIGHEST)  111 us
    all_gather x1, waiting for transfers between devices, shards(): weight_rows = lax.all_gather(out_weight, 'seq', axis=0, tiled=True)  86.2 us
    all_to_all x1, waiting for transfers between devices, shards(): lax.all_to_all(filter_grad_rows, 'seq', split_axis=1, concat_axis=0, tile...  21 us
    all_to_all x1, waiting for transfers between devices, shards(): lax.all_to_all(product, 'seq', split_axis=0, concat_axis=1, tiled=True)  12.7 us
    all_to_all x1, starting transfers between devices, shards(): lax.all_to_all(mixed_rows, 'seq', split_axis=1, concat_axis=0, tiled=True)  10.2 us
    all_to_all x1, starting transfers between devices, shards(): lax.all_to_all(filter_grad_rows, 'seq', split_axis=1, concat_axis=0, tile...  9.76 us
    all_to_all x1, starting transfers between devices, shards(): lax.all_to_all(gated, 'seq', split_axis=0, concat_axis=1, tiled=True)  9.47 us
    dot_general x1, matrix products, shards(): lax.dot_general(weight_rows, grad_out, (((1,), (1,)), ((), ())), preferre...  7.84 us
  transfers between devices with their start and end apart: 7, of which 5 were waited for; matrix products, arithmetic and copies ran while one was open for 21% of the time, Pallas kernels for 0%

commit v1 on v0

v1 whole, which is shorter than its diff:
```python
import functools
import math

import jax
import jax.numpy as jnp
import ml_dtypes
import numpy as np
from jax import lax
from jax.experimental import pallas as pl
from jax.experimental.pallas import tpu as pltpu
from jax.sharding import PartitionSpec as P

OUTER = 64
CHUNK = 256


def split_pair(table):
    high = table.astype(np.float32).astype(ml_dtypes.bfloat16)
    low = (table - high.astype(np.float64)).astype(np.float32).astype(ml_dtypes.bfloat16)
    return high, low


def make_tables(blocks, width, inner):
    total = OUTER * inner
    half = OUTER // 2 + 1
    k = np.arange(half)
    a = np.arange(blocks)
    b = np.arange(inner)
    first = 2.0 * np.pi * (np.outer(k, a) % OUTER) / OUTER
    eye = np.eye(width)
    k_cos = np.kron(np.cos(first), eye)
    k_sin = np.kron(np.sin(first), eye)
    into = np.concatenate([k_cos, -k_sin], 0)
    weight = np.full((half, 1), 2.0)
    weight[0] = 1.0
    weight[-1] = 1.0
    weight = weight / total
    back_cos = np.kron((weight * np.cos(first)).T, eye)
    back_sin = np.kron((weight * np.sin(first)).T, eye)
    out_of = np.concatenate([back_cos, back_sin], 1)
    turn = 2.0 * np.pi * (np.outer(k, b) % total) / total
    turn = np.repeat(turn, width, axis=0)
    second = 2.0 * np.pi * (np.outer(b, b) % inner) / inner
    c, s = np.cos(second), np.sin(second)
    across = np.concatenate([np.concatenate([c, -s], 1), np.concatenate([s, c], 1)], 0)
    return (
        split_pair(into),
        split_pair(out_of),
        np.cos(turn).astype(np.float32),
        np.sin(turn).astype(np.float32),
        split_pair(across),
    )


def dot(left, right):
    return jnp.dot(left, right, preferred_element_type=jnp.float32)


def turned(real, imag, cos, sin):
    return real * cos + imag * sin, imag * cos - real * sin


def spread(x_ref, into, twist, z_ref):
    rows = z_ref.shape[0]
    inner = x_ref.shape[1]

    @pl.loop(0, inner // CHUNK)
    def _(i):
        at = pl.ds(pl.multiple_of(i * CHUNK, CHUNK), CHUNK)
        block = x_ref[:, at]
        y = dot(into[0][...], block) + dot(into[1][...], block)
        real, imag = turned(y[:rows], y[rows:], twist[0][:, at], twist[1][:, at])
        z_ref[:, at] = real.astype(jnp.bfloat16)
        z_ref[:, pl.ds(pl.multiple_of(inner + i * CHUNK, CHUNK), CHUNK)] = imag.astype(jnp.bfloat16)


def across_columns(z_ref, across, out_ref):
    @pl.loop(0, z_ref.shape[1] // CHUNK)
    def _(i):
        at = pl.ds(pl.multiple_of(i * CHUNK, CHUNK), CHUNK)
        z = z_ref[...]
        out_ref[:, at] = dot(z, across[0][:, at]) + dot(z, across[1][:, at])


def combine(grad_ref, other_ref, z_ref, inner):
    @pl.loop(0, inner // CHUNK)
    def _(i):
        at = pl.ds(pl.multiple_of(i * CHUNK, CHUNK), CHUNK)
        far = pl.ds(pl.multiple_of(inner + i * CHUNK, CHUNK), CHUNK)
        g_re, g_im = grad_ref[:, at], grad_ref[:, far]
        o_re, o_im = other_ref[:, at], other_ref[:, far]
        z_ref[:, at] = (g_re * o_re + g_im * o_im).astype(jnp.bfloat16)
        z_ref[:, far] = (g_re * o_im - g_im * o_re).astype(jnp.bfloat16)


def gather_up(spec_ref, out_of, twist, u_ref, inner, store):
    rows = spec_ref.shape[0]

    @pl.loop(0, inner // CHUNK)
    def _(i):
        at = pl.ds(pl.multiple_of(i * CHUNK, CHUNK), CHUNK)
        far = pl.ds(pl.multiple_of(inner + i * CHUNK, CHUNK), CHUNK)
        real, imag = turned(spec_ref[:, at], spec_ref[:, far], twist[0][:, at], twist[1][:, at])
        u_ref[:rows, :] = real.astype(jnp.bfloat16)
        u_ref[rows:, :] = imag.astype(jnp.bfloat16)
        u = u_ref[...]
        store(at, dot(out_of[0][...], u) + dot(out_of[1][...], u))


def forward_kernel(x_ref, in_hi, in_lo, cos, sin, ac_hi, ac_lo, out_ref, z_ref):
    for i in range(2):
        spread(x_ref.at[i], (in_hi, in_lo), (cos, sin), z_ref)
        across_columns(z_ref, (ac_hi, ac_lo), out_ref.at[i])


def inverse_kernel(
    g_ref, other_ref, skip_ref, in_hi, in_lo, of_hi, of_lo, cos, sin, ac_hi, ac_lo, out_ref,
    z_ref, grad_ref, spec_ref, u_ref,
):
    inner = g_ref.shape[1]
    across = (ac_hi, ac_lo)
    spread(g_ref, (in_hi, in_lo), (cos, sin), z_ref)
    across_columns(z_ref, across, grad_ref)
    for i in range(2):
        combine(grad_ref, other_ref.at[i], z_ref, inner)
        across_columns(z_ref, across, spec_ref)

        def store(at, value):
            if i == 1:
                value = value + skip_ref[...] * g_ref[:, at].astype(jnp.float32)
            out_ref[i, :, at] = value.astype(jnp.bfloat16)

        gather_up(spec_ref, (of_hi, of_lo), (cos, sin), u_ref, inner, store)


VMEM = pl.BlockSpec(memory_space=pltpu.VMEM)


def shards(grad_out, out_weight, gate_in, gate_out, values, conv_out, filters, skip_scale):
    blocks = lax.axis_size("seq")
    rows, inner = gate_in.shape
    width = rows // blocks
    into, out_of, cos, sin, across = make_tables(blocks, width, inner)
    spec_rows = cos.shape[0]
    params = pltpu.CompilerParams(vmem_limit_bytes=50 * 1024 * 1024)

    product = (gate_in.astype(jnp.float32) * values.astype(jnp.float32)).astype(jnp.bfloat16)
    sent = jnp.stack(
        [product.reshape(blocks, width, inner), filters.astype(jnp.bfloat16).reshape(blocks, width, inner)], 1
    )
    landed = lax.all_to_all(sent, "seq", split_axis=0, concat_axis=0, tiled=True)
    landed = landed.transpose(1, 0, 2, 3).reshape(2, rows, inner)
    weight_rows = lax.all_gather(out_weight, "seq", axis=0, tiled=True)
    others = pl.pallas_call(
        forward_kernel,
        out_shape=jax.ShapeDtypeStruct((2, spec_rows, 2 * inner), jnp.float32),
        in_specs=[VMEM] * 7,
        out_specs=VMEM,
        scratch_shapes=[pltpu.VMEM((spec_rows, 2 * inner), jnp.bfloat16)],
        compiler_params=params,
        cost_estimate=pl.CostEstimate(flops=7 * 10**9, bytes_accessed=16 * 10**6, transcendentals=0),
    )(landed, *into, cos, sin, *across)

    back = lax.psum_scatter(
        lax.dot_general(
            weight_rows, grad_out, (((1,), (1,)), ((), ())), preferred_element_type=jnp.float32
        ),
        "ch",
        scatter_dimension=0,
        tiled=True,
    )
    grad_gate_out = (back * conv_out.astype(jnp.float32)).astype(jnp.bfloat16)
    gated = (back * gate_out.astype(jnp.float32)).astype(jnp.bfloat16)
    gated = lax.all_to_all(
        gated.reshape(blocks, width, inner), "seq", split_axis=0, concat_axis=0, tiled=True
    ).reshape(rows, inner)
    scale = lax.dynamic_slice_in_dim(skip_scale, lax.axis_index("seq") * width, width, 0)
    scale = jnp.tile(scale, blocks)[:, None]
    both = pl.pallas_call(
        inverse_kernel,
        out_shape=jax.ShapeDtypeStruct((2, rows, inner), jnp.bfloat16),
        in_specs=[VMEM] * 11,
        out_specs=VMEM,
        scratch_shapes=[
            pltpu.VMEM((spec_rows, 2 * inner), jnp.bfloat16),
            pltpu.VMEM((spec_rows, 2 * inner), jnp.float32),
            pltpu.VMEM((spec_rows, 2 * inner), jnp.float32),
            pltpu.VMEM((2 * spec_rows, CHUNK), jnp.bfloat16),
        ],
        compiler_params=params,
        cost_estimate=pl.CostEstimate(flops=10 * 10**9, bytes_accessed=20 * 10**6, transcendentals=0),
    )(gated, others, scale, *into, *out_of, cos, sin, *across)
    mixed = lax.all_to_all(
        both[1].reshape(blocks, width, inner), "seq", split_axis=0, concat_axis=0, tiled=True
    ).reshape(rows, inner)
    grad_filters = lax.all_to_all(
        both[0].reshape(blocks, width, inner), "seq", split_axis=0, concat_axis=0, tiled=True
    ).reshape(rows, inner)
    mixed_wide = mixed.astype(jnp.float32)
    grad_gate_in = (mixed_wide * values.astype(jnp.float32)).astype(jnp.bfloat16)
    grad_values = (mixed_wide * gate_in.astype(jnp.float32)).astype(jnp.bfloat16)
    return (grad_gate_in, grad_values, grad_gate_out, grad_filters.astype(jnp.float32))


def solution(mesh):
    placed = (
        P("seq", "ch"),
        P("seq", "ch"),
        P("ch", "seq"),
        P("ch", "seq"),
        P("ch", "seq"),
        P("ch", "seq"),
        P("ch", "seq"),
        P("ch"),
    )
    return jax.shard_map(
        shards,
        mesh=mesh,
        in_specs=placed,
        out_specs=(P("ch", "seq"), P("ch", "seq"), P("ch", "seq"), P("ch", "seq")),
        check_vma=False,
    )
```

time: 322 us -> 261 us (0.81)
  the two profiles are of different devices: /device:TPU:2 before, /device:TPU:1 now
where the time goes in v1:
time: 261 us; the launch traced here: 257 us
  waiting for transfers between devices  146 us (56%)
  Pallas kernels  33.4 us (13%)
  blocking collectives  23.9 us (9%)
  starting transfers between devices  21.7 us (8%)
  between operations  14.2 us (5%)
  matrix products  7.82 us (3%)
  other arithmetic  6.07 us (2%)
  local copies, waits for them, and re-layouts  4.54 us (2%)
    all_gather x1, waiting for transfers between devices, shards(): weight_rows = lax.all_gather(out_weight, 'seq', axis=0, tiled=True)  85.6 us
    reduce_scatter x1, waiting for transfers between devices, shards(): lax.psum_scatter(lax.dot_general(weight_rows, grad_out, (((1,), (1,)), ((...  46.1 us
    all_to_all x1, blocking collectives, shards(): lax.all_to_all(both[1].reshape(blocks, width, inner), 'seq', split_axis=0...  23.9 us
    pallas_call x1, Pallas kernels, shards(): pl.pallas_call(inverse_kernel, out_shape=jax.ShapeDtypeStruct((2, rows, i...  19.5 us
    pallas_call x1, Pallas kernels, shards(): pl.pallas_call(forward_kernel, out_shape=jax.ShapeDtypeStruct((2, spec_ro...  13.9 us
    all_to_all x1, waiting for transfers between devices, shards(): lax.all_to_all(both[0].reshape(blocks, width, inner), 'seq', split_axis=0...  13.3 us
    all_to_all x1, starting transfers between devices, shards(): lax.all_to_all(gated.reshape(blocks, width, inner), 'seq', split_axis=0,...  9.68 us
    dot_general x1, matrix products, shards(): lax.dot_general(weight_rows, grad_out, (((1,), (1,)), ((), ())), preferre...  7.82 us
  transfers between devices with their start and end apart: 5, of which 3 were waited for; matrix products, arithmetic and copies ran while one was open for 3% of the time, Pallas kernels for 5%

profile of v1, /device:TPU:1, one launch (start us, length us, event | category | flops | bytes accessed | tf_op | source)
XLA Modules:
  0.0 257.4 jit_solution(4614235687166424876)
XLA Ops:
  7.2 0.0 copy-start
  7.2 0.0 all-gather.2.cloned.1.call-start
  7.2 0.7 all-gather.2.cloned.1.call-update
  7.9 0.0 reduce-scatter.2.cloned.1.call-start
  8.0 85.6 %all-gather.2.cloned.1.call-done = bf16[4096,512]{1,0:T(8,128)(2,1)} async-done(((bf16[128,512]{1,0:T(8,128)(2,1)}), bf16[4096,512]{1,0:T(8,128)(2,1)}) %all-gather.2.cloned.1.call-update) | async-done | bytes 4194320 | tf_op jit(solution)/shard_map/all_gather | solution.py:153
  93.6 0.0 copy-done
  93.6 7.8 %fusion.4 = f32[4096,512]{1,0:T(8,128)} fusion(bf16[4096,512]{1,0:T(8,128)(2,1)} %all-gather.2.cloned.1.call-done, bf16[512,512]{1,0:T(8,128)(2,1)S(1)} %copy-done), kind=kOutput, calls=%fused_computation.11 | convolution fusion | flops 2147483648 | bytes 13107200 | tf_op jit(solution)/shard_map/dot_general | solution.py:165
  101.4 0.0 copy-start.7
  101.4 0.0 copy-start.3
  101.4 0.0 copy-start.5
  101.4 0.0 reduce-scatter.2.cloned.1.call-update
  101.4 1.2 copy-done.7
  102.6 0.1 convert_element_type.49
  102.7 0.1 copy-done.3
  102.7 0.2 copy-done.5
  102.9 0.1 fusion
  103.0 0.0 copy-start.8
  103.1 0.0 copy-start.9
  103.1 1.1 pad_maximum_fusion
  104.1 5.7 %all-to-all-start.1 = ((bf16[32,2,16,512]{3,2,1,0:T(8,128)(2,1)}), bf16[32,2,16,512]{3,2,1,0:T(8,128)(2,1)}, u32[]{:S(2)}, u32[]{:S(2)}) async-start(bf16[32,2,16,512]{3,2,1,0:T(8,128)(2,1)} %pad_maximum_fusion), calls=%async_computation.2 | async-start | bytes 2097152 | tf_op jit(solution)/shard_map/all_to_all | solution.py:151
  109.9 46.1 %reduce-scatter.2.cloned.1.call-done = f32[512,512]{1,0:T(8,128)} async-done(((f32[4096,512]{1,0:T(8,128)}), f32[512,512]{1,0:T(8,128)}) %reduce-scatter.2.cloned.1.call-update) | async-done | bytes 1048592 | tf_op jit(solution)/shard_map/reduce_scatter | solution.py:164
  156.0 0.0 copy-done.8
  156.0 0.0 copy-done.9
  156.0 2.4 multiply_convert_fusion
  158.4 0.0 copy-start.1
  158.5 0.0 copy-start.2
  158.5 0.0 all-to-all-done.1
  158.5 9.7 %all-to-all-start = ((bf16[32,16,512]{2,1,0:T(8,128)(2,1)}), bf16[32,16,512]{2,1,0:T(8,128)(2,1)S(1)}, u32[]{:S(2)}, u32[]{:S(2)}) async-start(bf16[32,16,512]{2,1,0:T(8,128)(2,1)} %bitcast.21), calls=%async_computation.1 | async-start | bytes 1048576 | tf_op jit(solution)/shard_map/all_to_all | solution.py:174
  168.2 0.8 dynamic_slice.3
  168.9 0.2 broadcast_in_dim_tile.4.skip_ref
  169.1 1.3 copy.21
  170.4 0.0 copy-done.1
  170.4 0.0 copy-done.2
  170.4 13.9 %shard_map.183.other_ref = f32[2,528,1024]{2,1,0:T(8,128)} custom-call(bf16[2,512,512]{2,1,0:T(8,128)(2,1)S(1)} %bitcast.17, bf16[1056,512]{1,0:T(8,128)(2,1)S(1)} %copy-done.1, bf16[1056,512]{1,0:T(8,128)(2,1)S(1)} %copy-done.2, f32[528,512]{1,0:T(8,128)} %constant.30.clone.cos, f32[528,512]{1,0:T(8,128)} %constant.31.clone.sin, ...), custom_call_target="tpu_custom_call" | custom-call | flops 7000000000 | bytes 16000000 | tf_op jit(solution)/shard_map/pallas_call | solution.py:154
  184.3 0.0 all-to-all-done
  184.3 19.5 %shard_map.184 = bf16[2,512,512]{2,1,0:T(8,128)(2,1)S(1)} custom-call(bf16[512,512]{1,0:T(8,128)(2,1)S(1)} %bitcast.18, f32[2,528,1024]{2,1,0:T(8,128)} %shard_map.183.other_ref, f32[512,1]{1,0:T(8,128)S(1)} %broadcast_in_dim_tile.4.skip_ref, bf16[1056,512]{1,0:T(8,128)(2,1)S(1)} %copy-done.1, bf16[1056,512]{1,0:T(8,128)(2,1)S(1)} %copy-done.2, ...), custom_call_target="tpu_custom_call" | custom-call | flops 10000000000 | bytes 20000000 | tf_op jit(solution)/shard_map/pallas_call | solution.py:179
  203.8 0.0 copy-start.4
  203.8 0.0 copy-start.6
  203.9 0.9 fusion.3
  204.7 23.9 %all_to_all.20 = bf16[32,16,512]{2,1,0:T(8,128)(2,1)S(1)} all-to-all(bf16[32,16,512]{2,1,0:T(8,128)(2,1)S(1)} %bitcast.22), channel_id=1, replica_groups=mesh['seq'=32,'ch'=8] {'seq'}, dimensions={0} | all-to-all | bytes 1048576 | tf_op jit(solution)/shard_map/all_to_all | solution.py:193
  228.6 6.2 %all-to-all-start.3 = ((bf16[32,16,512]{2,1,0:T(8,128)(2,1)}), bf16[32,16,512]{2,1,0:T(8,128)(2,1)S(1)}, u32[]{:S(2)}, u32[]{:S(2)}) async-start(bf16[32,16,512]{2,1,0:T(8,128)(2,1)} %bitcast.9), calls=%async_computation.4 | async-start | bytes 1048576 | tf_op jit(solution)/shard_map/all_to_all | solution.py:196
  234.8 0.0 copy-done.4
  234.8 0.0 copy-done.6
  234.8 1.2 fusion.2
  236.1 13.3 %all-to-all-done.3 = bf16[32,16,512]{2,1,0:T(8,128)(2,1)S(1)} async-done(((bf16[32,16,512]{2,1,0:T(8,128)(2,1)}), bf16[32,16,512]{2,1,0:T(8,128)(2,1)S(1)}, u32[]{:S(2)}, u32[]{:S(2)}) %all-to-all-start.3) | async-done | bytes 524320 | tf_op jit(solution)/shard_map/all_to_all | solution.py:196
  249.4 1.1 bitcast_convert_fusion
  (1 shorter events, 0.0 us)
Async XLA Ops:
  7.2 86.4 %copy-start = (bf16[512,512]{1,0:T(8,128)(2,1)S(1)}, bf16[512,512]{1,0:T(8,128)(2,1)}, u32[]{:S(2)}) copy-start(bf16[512,512]{1,0:T(8,128)(2,1)} %param.16) | copy-start | bytes 1572868
  7.2 86.4 %all-gather.2.cloned.1.call-start = ((), (), s32[]{:S(2)}) async-start(), calls=%async_computation.5 | async-start | bytes 4325376 | tf_op jit(solution)/shard_map/all_gather | solution.py:153
  7.9 148.1 %reduce-scatter.2.cloned.1.call-start = ((), (), s32[]{:S(2)}) async-start(), calls=%async_computation.6 | async-start | bytes 9437184 | tf_op jit(solution)/shard_map/reduce_scatter | solution.py:164
  101.4 1.2 copy-start.7
  101.4 1.4 copy-start.3
  101.4 1.5 copy-start.5
  103.0 53.0 %copy-start.8 = (bf16[512,512]{1,0:T(8,128)(2,1)S(1)}, bf16[512,512]{1,0:T(8,128)(2,1)}, u32[]{:S(2)}) copy-start(bf16[512,512]{1,0:T(8,128)(2,1)} %param.21) | copy-start | bytes 1572868
  103.1 53.0 %copy-start.9 = (bf16[512,512]{1,0:T(8,128)(2,1)S(1)}, bf16[512,512]{1,0:T(8,128)(2,1)}, u32[]{:S(2)}) copy-start(bf16[512,512]{1,0:T(8,128)(2,1)} %param.19) | copy-start | bytes 1572868
  104.1 54.3 %all-to-all-start.1 = ((bf16[32,2,16,512]{3,2,1,0:T(8,128)(2,1)}), bf16[32,2,16,512]{3,2,1,0:T(8,128)(2,1)}, u32[]{:S(2)}, u32[]{:S(2)}) async-start(bf16[32,2,16,512]{3,2,1,0:T(8,128)(2,1)} %pad_maximum_fusion), calls=%async_computation.2 | async-start | bytes 2097152 | tf_op jit(solution)/shard_map/all_to_all | solution.py:151
  158.4 11.9 %copy-start.1 = (bf16[1056,512]{1,0:T(8,128)(2,1)S(1)}, bf16[1056,512]{1,0:T(8,128)(2,1)}, u32[]{:S(2)}) copy-start(bf16[1056,512]{1,0:T(8,128)(2,1)} %constant.28.clone.in_hi) | copy-start | bytes 3244036
  158.5 12.0 %copy-start.2 = (bf16[1056,512]{1,0:T(8,128)(2,1)S(1)}, bf16[1056,512]{1,0:T(8,128)(2,1)}, u32[]{:S(2)}) copy-start(bf16[1056,512]{1,0:T(8,128)(2,1)} %constant.29.clone.in_lo) | copy-start | bytes 3244036
  158.5 25.9 %all-to-all-start = ((bf16[32,16,512]{2,1,0:T(8,128)(2,1)}), bf16[32,16,512]{2,1,0:T(8,128)(2,1)S(1)}, u32[]{:S(2)}, u32[]{:S(2)}) async-start(bf16[32,16,512]{2,1,0:T(8,128)(2,1)} %bitcast.21), calls=%async_computation.1 | async-start | bytes 1048576 | tf_op jit(solution)/shard_map/all_to_all | solution.py:174
  203.8 31.0 %copy-start.4 = (bf16[512,512]{1,0:T(8,128)(2,1)S(1)}, bf16[512,512]{1,0:T(8,128)(2,1)}, u32[]{:S(2)}) copy-start(bf16[512,512]{1,0:T(8,128)(2,1)} %param.18) | copy-start | bytes 1572868
  203.8 31.0 %copy-start.6 = (bf16[512,512]{1,0:T(8,128)(2,1)S(1)}, bf16[512,512]{1,0:T(8,128)(2,1)}, u32[]{:S(2)}) copy-start(bf16[512,512]{1,0:T(8,128)(2,1)} %param.20) | copy-start | bytes 1572868
  228.6 20.8 %all-to-all-start.3 = ((bf16[32,16,512]{2,1,0:T(8,128)(2,1)}), bf16[32,16,512]{2,1,0:T(8,128)(2,1)S(1)}, u32[]{:S(2)}, u32[]{:S(2)}) async-start(bf16[32,16,512]{2,1,0:T(8,128)(2,1)} %bitcast.9), calls=%async_computation.4 | async-start | bytes 1048576 | tf_op jit(solution)/shard_map/all_to_all | solution.py:196
Sparse Core Ops, SparseCore 0:
  10.6 82.9 all-gather.1
  101.5 54.4 reduce-scatter.1

commit v2 on v1

--- a/solution.py
+++ b/solution.py
@@ -136,21 +136,238 @@
 VMEM = pl.BlockSpec(memory_space=pltpu.VMEM)
 
 
+ZS, XS, YS = 8, 4, 4
+MESH = pl.DeviceIdType.MESH
+
+
+def project_kernel(
+    w_ref, g_ref, gate_in_ref, values_ref, gate_out_ref, filters_ref,
+    gated_out, pair_out, home_out,
+    w_ring, w_mine, w_other, g_ring, g_other, own, part, sums, near_gate, back_bf, gated, stage, crossed,
+    send_sems, recv_sems,
+):
+    s, h = lax.axis_index("seq"), lax.axis_index("ch")
+    z, x = s // XS, s % XS
+    y, core = h // 2, h % 2
+
+    def at_z(d):
+        return (lax.rem(z + d + ZS, ZS) * XS + x, h)
+
+    def at_x(d):
+        return (z * XS + lax.rem(x + d + XS, XS), h)
+
+    def at_y(d):
+        return (s, lax.rem(y + d, YS) * 2 + core)
+
+    sibling = (s, y * 2 + 1 - core)
+    peers = [at_z(d) for d in range(1, ZS)] + [at_x(d) for d in range(1, XS)]
+    peers += [at_y(d) for d in range(1, YS)] + [sibling]
+
+    barrier = pltpu.get_barrier_semaphore()
+    for peer in peers:
+        pl.semaphore_signal(barrier, inc=1, device_id=peer, device_id_type=MESH)
+    pl.semaphore_wait(barrier, len(peers))
+
+    copies = []
+
+    def send(src, dst, device):
+        k = len(copies)
+        copy = pltpu.make_async_remote_copy(
+            src_ref=src, dst_ref=dst, send_sem=send_sems.at[k], recv_sem=recv_sems.at[k],
+            device_id=device, device_id_type=MESH,
+        )
+        copy.start()
+        copies.append(copy)
+        return copy
+
+    def zmod(d):
+        return lax.rem(z + d + ZS, ZS)
+
+    def xmod(d):
+        return lax.rem(x + d + XS, XS)
+
+    half_w = w_ref.shape[0] // 2
+    half_g = g_ref.shape[0] // 2
+    top, low = pl.ds(0, half_g), pl.ds(half_g, half_g)
+
+    up = send(w_ref, w_ring.at[z], at_z(1))
+    down = send(w_ref, w_ring.at[z], at_z(-1))
+    right_top = send(g_ref.at[top], g_ring.at[x, top], at_x(1))
+    left_low = send(g_ref.at[low], g_ring.at[x, low], at_x(-1))
+    right_low = send(g_ref.at[low], g_ring.at[x, low], at_x(1))
+    left_top = send(g_ref.at[top], g_ring.at[x, top], at_x(-1))
+    shared = [send(g_ref, g_other.at[0], sibling)]
+    w_ring[z] = w_ref[...]
+    for i in range(XS):
+        product = gate_in_ref[i].astype(jnp.float32) * values_ref[i].astype(jnp.float32)
+        stage[0, i] = product.astype(jnp.bfloat16)
+        stage[1, i] = filters_ref[i].astype(jnp.bfloat16)
+
+    up.wait_recv()
+    up = send(w_ring.at[zmod(-1)], w_ring.at[zmod(-1)], at_z(1))
+    down.wait_recv()
+    down = send(w_ring.at[zmod(1)], w_ring.at[zmod(1)], at_z(-1))
+    right_top.wait_recv()
+    far_top = send(g_ring.at[xmod(-1), top], g_ring.at[xmod(-1), top], at_x(1))
+    left_low.wait_recv()
+    far_low = send(g_ring.at[xmod(1), low], g_ring.at[xmod(1), low], at_x(-1))
+    gates = [send(gate_out_ref.at[xmod(d)], near_gate.at[d], at_x(d)) for d in range(1, XS)]
+    near_gate[0] = gate_out_ref[x]
+    up.wait_recv()
+    up = send(w_ring.at[zmod(-2)], w_ring.at[zmod(-2)], at_z(1))
+    down.wait_recv()
+    down = send(w_ring.at[zmod(2)], w_ring.at[zmod(2)], at_z(-1))
+    up.wait_recv()
+    first, second = pl.ds(0, half_w), pl.ds(half_w, half_w)
+    up = send(w_ring.at[zmod(-3), first], w_ring.at[zmod(-3), first], at_z(1))
+    down.wait_recv()
+    down = send(w_ring.at[zmod(3), second], w_ring.at[zmod(3), second], at_z(-1))
+    pairs = [
+        send(stage.at[:, :, zmod(d)], crossed.at[:, z], at_z(d)) for d in range(1, ZS)
+    ]
+    crossed[:, z] = stage[:, :, z]
+    up.wait_recv()
+    down.wait_recv()
+
+    def rows_for(d, of_core):
+        return lax.rem(y + d, YS) * 2 + of_core
+
+    w_shared = [
+        send(w_ring.at[rows_for(d, 1 - core)], w_other.at[d], sibling) for d in range(YS)
+    ]
+    for d in range(YS):
+        w_mine[d] = w_ring[rows_for(d, core)]
+    right_low.wait_recv()
+    shared.append(send(g_ring.at[xmod(-1)], g_other.at[1], sibling))
+    left_top.wait_recv()
+    shared.append(send(g_ring.at[xmod(1)], g_other.at[2], sibling))
+    for copy in w_shared:
+        copy.wait_recv()
+
+    offsets = (0, -1, 1, 2)
+    parts = []
+    wide = (YS * w_ref.shape[0], w_ref.shape[1])
+    tile = 256
+    for n, off in enumerate(offsets):
+        if n == 3:
+            far_top.wait_recv()
+            far_low.wait_recv()
+            shared.append(send(g_ring.at[xmod(2)], g_other.at[3], sibling))
+        shared[n].wait_recv()
+
+        @pl.loop(0, g_ref.shape[0] // tile)
+        def _(i, n=n, off=off):
+            at = pl.ds(pl.multiple_of(i * tile, tile), tile)
+            near = g_ref[at, :] if n == 0 else g_ring[xmod(off), at, :]
+            form = (((1,), (1,)), ((), ()))
+            total = lax.dot_general(
+                w_mine[...].reshape(wide), near, form, preferred_element_type=jnp.float32
+            ) + lax.dot_general(
+                w_other[...].reshape(wide), g_other[n, at, :], form, preferred_element_type=jnp.float32
+            )
+            total = total.reshape(YS, w_ref.shape[0], tile)
+            own[n, :, at] = total[0]
+            part[n, :, :, at] = total[1:].astype(jnp.bfloat16)
+
+        parts.append([send(part.at[n, d - 1], sums.at[n, d - 1], at_y(d)) for d in range(1, YS)])
+
+    for copy in pairs:
+        copy.wait_recv()
+    tails = [
+        send(crossed.at[:, :, xmod(d)], pair_out.at[:, :, x], at_x(d)) for d in range(1, XS)
+    ]
+    pair_out[:, :, x] = crossed[:, :, x]
+
+    arrivals = []
+    for n, off in enumerate(offsets):
+        for copy in parts[n]:
+            copy.wait_recv()
+        back = own[n]
+        for d in range(1, YS):
+            back = back + sums[n, d - 1].astype(jnp.float32)
+        result = back * near_gate_value(near_gate, gates, off)
+        gated[n] = result.astype(jnp.bfloat16).reshape(gated.shape[1:])
+        for d in range(1, ZS):
+            arrivals.append(send(gated.at[n, zmod(d)], gated_out.at[z, xmod(off)], at_z(d)))
+        gated_out[z, xmod(off)] = gated[n, z]
+        back_bf[n] = back.astype(jnp.bfloat16)
+        if n == 0:
+            home_out[x] = back_bf[n]
+        else:
+            arrivals.append(send(back_bf.at[n], home_out.at[x], at_x(off)))
+
+    for copy in tails + arrivals:
+        copy.wait_recv()
+    for copy in copies:
+        copy.wait_send()
+
+
+def near_gate_value(near_gate, gates, off):
+    d = -off % XS
+    if d:
+        gates[d - 1].wait_recv()
+    return near_gate[d].astype(jnp.float32)
+
+
+def project(grad_out, out_weight, gate_in, gate_out, values, filters):
+    rows, inner = gate_in.shape
+    deep, wide = out_weight.shape
+    width = rows // (ZS * XS)
+    bf = jnp.bfloat16
+    split = (XS, ZS, width, inner)
+    count = 2 + 4 + 1 + 2 + 2 + 3 + 2 + 2 + 7 + 4 + 3 + 12 + 3 + 28 + 3
+    return pl.pallas_call(
+        project_kernel,
+        out_shape=[
+            jax.ShapeDtypeStruct((ZS, XS, width, inner), bf),
+            jax.ShapeDtypeStruct((2, ZS, XS, width, inner), bf),
+            jax.ShapeDtypeStruct((XS, deep, inner), bf),
+        ],
+        in_specs=[VMEM] * 6,
+        out_specs=[VMEM] * 3,
+        scratch_shapes=[
+            pltpu.VMEM((ZS, deep, wide), bf),
+            pltpu.VMEM((YS, deep, wide), bf),
+            pltpu.VMEM((YS, deep, wide), bf),
+            pltpu.VMEM((XS,) + grad_out.shape, bf),
+            pltpu.VMEM((XS,) + grad_out.shape, bf),
+            pltpu.VMEM((XS, deep, inner), jnp.float32),
+            pltpu.VMEM((XS, YS - 1, deep, inner), bf),
+            pltpu.VMEM((XS, YS - 1, deep, inner), bf),
+            pltpu.VMEM((XS, deep, inner), bf),
+            pltpu.VMEM((XS, deep, inner), bf),
+            pltpu.VMEM((XS, ZS, width, inner), bf),
+            pltpu.VMEM((2,) + split, bf),
+            pltpu.VMEM((2, ZS, XS, width, inner), bf),
+            pltpu.SemaphoreType.DMA((count,)),
+            pltpu.SemaphoreType.DMA((count,)),
+        ],
+        compiler_params=pltpu.CompilerParams(
+            collective_id=0, has_side_effects=True, vmem_limit_bytes=50 * 1024 * 1024
+        ),
+        cost_estimate=pl.CostEstimate(flops=3 * 10**9, bytes_accessed=6 * 10**6, transcendentals=0),
+    )(
+        out_weight,
+        grad_out,
+        gate_in.reshape(split),
+        values.reshape(split),
+        gate_out.reshape(XS, deep, inner),
+        filters.reshape(split),
+    )
+
+
 def shards(grad_out, out_weight, gate_in, gate_out, values, conv_out, filters, skip_scale):
-    blocks = lax.axis_size("seq")
     rows, inner = gate_in.shape
+    blocks = ZS * XS
     width = rows // blocks
     into, out_of, cos, sin, across = make_tables(blocks, width, inner)
     spec_rows = cos.shape[0]
     params = pltpu.CompilerParams(vmem_limit_bytes=50 * 1024 * 1024)
 
-    product = (gate_in.astype(jnp.float32) * values.astype(jnp.float32)).astype(jnp.bfloat16)
-    sent = jnp.stack(
-        [product.reshape(blocks, width, inner), filters.astype(jnp.bfloat16).reshape(blocks, width, inner)], 1
-    )
-    landed = lax.all_to_all(sent, "seq", split_axis=0, concat_axis=0, tiled=True)
-    landed = landed.transpose(1, 0, 2, 3).reshape(2, rows, inner)
-    weight_rows = lax.all_gather(out_weight, "seq", axis=0, tiled=True)
+    gated, pair, home = project(grad_out, out_weight, gate_in, gate_out, values, filters)
+    grad_gate_out = (
+        home.reshape(rows, inner).astype(jnp.float32) * conv_out.astype(jnp.float32)
+    ).astype(jnp.bfloat16)
     others = pl.pallas_call(
         forward_kernel,
         out_shape=jax.ShapeDtypeStruct((2, spec_rows, 2 * inner), jnp.float32),
@@ -159,22 +376,10 @@
         scratch_shapes=[pltpu.VMEM((spec_rows, 2 * inner), jnp.bfloat16)],
         compiler_params=params,
         cost_estimate=pl.CostEstimate(flops=7 * 10**9, bytes_accessed=16 * 10**6, transcendentals=0),
-    )(landed, *into, cos, sin, *across)
-
-    back = lax.psum_scatter(
-        lax.dot_general(
-            weight_rows, grad_out, (((1,), (1,)), ((), ())), preferred_element_type=jnp.float32
-        ),
-        "ch",
-        scatter_dimension=0,
-        tiled=True,
-    )
-    grad_gate_out = (back * conv_out.astype(jnp.float32)).astype(jnp.bfloat16)
-    gated = (back * gate_out.astype(jnp.float32)).astype(jnp.bfloat16)
-    gated = lax.all_to_all(
-        gated.reshape(blocks, width, inner), "seq", split_axis=0, concat_axis=0, tiled=True
-    ).reshape(rows, inner)
-    scale = lax.dynamic_slice_in_dim(skip_scale, lax.axis_index("seq") * width, width, 0)
+    )(pair.reshape(2, rows, inner), *into, cos, sin, *across)
+    place = lax.axis_index("seq")
+    start = (place % XS) * (rows // XS) + (place // XS) * width
+    scale = lax.dynamic_slice_in_dim(skip_scale, start, width, 0)
     scale = jnp.tile(scale, blocks)[:, None]
     both = pl.pallas_call(
         inverse_kernel,
@@ -189,17 +394,17 @@
         ],
         compiler_params=params,
         cost_estimate=pl.CostEstimate(flops=10 * 10**9, bytes_accessed=20 * 10**6, transcendentals=0),
-    )(gated, others, scale, *into, *out_of, cos, sin, *across)
-    mixed = lax.all_to_all(
-        both[1].reshape(blocks, width, inner), "seq", split_axis=0, concat_axis=0, tiled=True
-    ).reshape(rows, inner)
-    grad_filters = lax.all_to_all(
-        both[0].reshape(blocks, width, inner), "seq", split_axis=0, concat_axis=0, tiled=True
-    ).reshape(rows, inner)
-    mixed_wide = mixed.astype(jnp.float32)
+    )(gated.reshape(rows, inner), others, scale, *into, *out_of, cos, sin, *across)
+    landed = [
+        lax.all_to_all(
+            both[i].reshape(blocks, width, inner), "seq", split_axis=0, concat_axis=0, tiled=True
+        ).reshape(ZS, XS, width, inner).transpose(1, 0, 2, 3).reshape(rows, inner)
+        for i in (1, 0)
+    ]
+    mixed_wide = landed[0].astype(jnp.float32)
     grad_gate_in = (mixed_wide * values.astype(jnp.float32)).astype(jnp.bfloat16)
     grad_values = (mixed_wide * gate_in.astype(jnp.float32)).astype(jnp.bfloat16)
-    return (grad_gate_in, grad_values, grad_gate_out, grad_filters.astype(jnp.float32))
+    return (grad_gate_in, grad_values, grad_gate_out, landed[1].astype(jnp.float32))
 
 
 def solution(mesh):

time: 261 us -> 156 us (0.60)
  waiting for transfers between devices: 146 us -> 14 us
  Pallas kernels: 33.4 us -> 101 us
  starting transfers between devices: 21.7 us -> 4.97 us
  between operations: 14.2 us -> 0.76 us
  matrix products: 7.82 us -> 0 us
  local copies, waits for them, and re-layouts: 4.54 us -> 9.31 us
  other arithmetic: 6.07 us -> 1.49 us
    all_gather x1 -> x0, waiting for transfers between devices: 85.6 us -> none  [shards(): weight_rows = lax.all_gather(out_weight, 'seq', axis=0, tiled=True)]
    pallas_call x0 -> x1, Pallas kernels: none -> 67.9 us  [project(): pl.pallas_call(project_kernel, out_shape=[jax.ShapeDtypeStruct((ZS, XS, w...]
    reduce_scatter x1 -> x0, waiting for transfers between devices: 46.1 us -> none  [shards(): lax.psum_scatter(lax.dot_general(weight_rows, grad_out, (((1,), (1,)), ((...]
    all_to_all x3 -> x1, starting transfers between devices: 21.6 us -> 4.97 us  [shards(): lax.all_to_all(both[i].reshape(blocks, width, inner), 'seq', split_axis=0...]
    dot_general x1 -> x0, matrix products: 7.82 us -> none  [shards(): lax.dot_general(weight_rows, grad_out, (((1,), (1,)), ((), ())), preferre...]
    unnamed x20 -> x22, local copies, waits for them, and re-layouts: 1.46 us -> 6.3 us
    convert_element_type x4 -> x0, other arithmetic: 3.77 us -> none  [the longest x1 2.43 us: shards(): grad_gate_out = (back * conv_out.astype(jnp.float32)).astype(jnp.bfloat16)]
    all_to_all x3 -> x1, waiting for transfers between devices: 13.3 us -> 14 us  [shards(): lax.all_to_all(both[i].reshape(blocks, width, inner), 'seq', split_axis=0...]
  transfers between devices with their start and end apart: 5 -> 1, of which waited for: 3 -> 1; matrix products, arithmetic and copies ran while one was open for 3% -> 1% of each run, Pallas kernels for 5% -> 0%
where the time goes in v2:
time: 156 us; the launch traced here: 154 us
  Pallas kernels  101 us (65%)
  blocking collectives  22 us (14%)
  waiting for transfers between devices  14 us (9%)
  local copies, waits for them, and re-layouts  9.31 us (6%)
  starting transfers between devices  4.97 us (3%)
    pallas_call x1, Pallas kernels, project(): pl.pallas_call(project_kernel, out_shape=[jax.ShapeDtypeStruct((ZS, XS, w...  67.9 us
    all_to_all x1, blocking collectives, shards(): lax.all_to_all(both[i].reshape(blocks, width, inner), 'seq', split_axis=0...  22 us
    pallas_call x1, Pallas kernels, shards(): pl.pallas_call(inverse_kernel, out_shape=jax.ShapeDtypeStruct((2, rows, i...  19.5 us
    all_to_all x1, waiting for transfers between devices, shards(): lax.all_to_all(both[i].reshape(blocks, width, inner), 'seq', split_axis=0...  14 us
    pallas_call x1, Pallas kernels, shards(): pl.pallas_call(forward_kernel, out_shape=jax.ShapeDtypeStruct((2, spec_ro...  13.9 us
    unnamed x22, local copies, waits for them, and re-layouts  6.3 us
    all_to_all x1, starting transfers between devices, shards(): lax.all_to_all(both[i].reshape(blocks, width, inner), 'seq', split_axis=0...  4.97 us
  transfers between devices with their start and end apart: 1, of which 1 were waited for; matrix products, arithmetic and copies ran while one was open for 1% of the time, Pallas kernels for 0%

profile of v2, /device:TPU:1, one launch (start us, length us, event | category | flops | bytes accessed | tf_op | source)
XLA Modules:
  0.0 153.8 jit_solution(15577429645865912607)
XLA Ops:
  0.7 0.8 dynamic_slice.3
  1.4 0.2 broadcast_in_dim_tile.4.skip_ref
  1.6 0.0 copy-start
  1.6 1.0 copy-done
  2.6 0.0 copy-start.2
  2.6 1.0 copy-done.2
  3.7 0.0 copy-start.4
  3.7 1.0 copy-done.4
  4.7 0.0 copy-start.5
  4.7 1.0 copy-done.5
  5.8 0.0 copy-start.6
  5.8 0.9 copy-done.6
  6.7 0.0 copy-start.7
  6.7 0.0 copy-start.8
  6.7 67.9 %shard_map.183 = (bf16[8,4,16,512]{3,2,1,0:T(8,128)(2,1)S(1)}, bf16[2,8,4,16,512]{4,3,2,1,0:T(8,128)(2,1)}, bf16[4,128,512]{2,1,0:T(8,128)(2,1)S(1)}) custom-call(bf16[128,512]{1,0:T(8,128)(2,1)S(1)} %copy-done.6, bf16[512,512]{1,0:T(8,128)(2,1)S(1)} %copy-done.4, bf16[4,8,16,512]{3,2,1,0:T(8,128)(2,1)S(1)} %bitcast.27, ...), custom_call_target="tpu_custom_call" | custom-call | flops 3000000000 | bytes 6000000 | tf_op jit(solution)/shard_map/pallas_call | solution.py:319
  74.6 0.0 copy-done.7
  74.6 0.0 copy-done.8
  74.6 0.0 copy-start.9
  74.7 1.2 copy-done.9
  75.9 13.9 %shard_map.184.other_ref = f32[2,528,1024]{2,1,0:T(8,128)} custom-call(bf16[2,512,512]{2,1,0:T(8,128)(2,1)S(1)} %bitcast.30, bf16[1056,512]{1,0:T(8,128)(2,1)S(1)} %copy-done.8, bf16[1056,512]{1,0:T(8,128)(2,1)S(1)} %copy-done.7, f32[528,512]{1,0:T(8,128)} %constant.57.clone.cos, f32[528,512]{1,0:T(8,128)} %constant.58.clone.sin, ...), custom_call_target="tpu_custom_call" | custom-call | flops 7000000000 | bytes 16000000 | tf_op jit(solution)/shard_map/pallas_call | solution.py:371
  89.7 19.5 %shard_map.185 = bf16[2,512,512]{2,1,0:T(8,128)(2,1)S(1)} custom-call(bf16[512,512]{1,0:T(8,128)(2,1)S(1)} %bitcast.31, f32[2,528,1024]{2,1,0:T(8,128)} %shard_map.184.other_ref, f32[512,1]{1,0:T(8,128)S(1)} %broadcast_in_dim_tile.4.skip_ref, bf16[1056,512]{1,0:T(8,128)(2,1)S(1)} %copy-done.8, bf16[1056,512]{1,0:T(8,128)(2,1)S(1)} %copy-done.7, ...), custom_call_target="tpu_custom_call" | custom-call | flops 10000000000 | bytes 20000000 | tf_op jit(solution)/shard_map/pallas_call | solution.py:384
  109.3 0.9 fusion.3
  110.1 22.0 %all_to_all.10 = bf16[32,16,512]{2,1,0:T(8,128)(2,1)S(1)} all-to-all(bf16[32,16,512]{2,1,0:T(8,128)(2,1)S(1)} %bitcast.34), channel_id=1, replica_groups=mesh['seq'=32,'ch'=8] {'seq'}, dimensions={0} | all-to-all | bytes 1048576 | tf_op jit(solution)/shard_map/all_to_all | solution.py:399
  132.1 5.0 %all-to-all-start = ((bf16[32,16,512]{2,1,0:T(8,128)(2,1)}), bf16[32,16,512]{2,1,0:T(8,128)(2,1)S(1)}, u32[]{:S(2)}, u32[]{:S(2)}) async-start(bf16[32,16,512]{2,1,0:T(8,128)(2,1)} %bitcast.6), calls=%async_computation | async-start | bytes 1048576 | tf_op jit(solution)/shard_map/all_to_all | solution.py:399
  137.1 1.1 copy.24
  138.2 0.0 copy-start.1
  138.2 0.0 copy-start.3
  138.2 0.0 copy-start.10
  138.2 14.0 %all-to-all-done = bf16[32,16,512]{2,1,0:T(8,128)(2,1)S(1)} async-done(((bf16[32,16,512]{2,1,0:T(8,128)(2,1)}), bf16[32,16,512]{2,1,0:T(8,128)(2,1)S(1)}, u32[]{:S(2)}, u32[]{:S(2)}) %all-to-all-start) | async-done | bytes 524320 | tf_op jit(solution)/shard_map/all_to_all | solution.py:399
  152.2 0.1 copy.23
  152.3 0.0 copy-done.1
  152.3 0.0 copy-done.3
  152.3 0.0 copy-done.10
  152.3 1.5 fusion.2
  (1 shorter events, 0.0 us)
Async XLA Ops:
  1.6 1.0 copy-start
  2.6 1.0 copy-start.2
  3.7 1.0 copy-start.4
  4.7 1.0 copy-start.5
  5.8 0.9 copy-start.6
  6.7 68.0 %copy-start.7 = (bf16[1056,512]{1,0:T(8,128)(2,1)S(1)}, bf16[1056,512]{1,0:T(8,128)(2,1)}, u32[]{:S(2)}) copy-start(bf16[1056,512]{1,0:T(8,128)(2,1)} %constant.56.clone.in_lo) | copy-start | bytes 3244036
  6.7 68.0 %copy-start.8 = (bf16[1056,512]{1,0:T(8,128)(2,1)S(1)}, bf16[1056,512]{1,0:T(8,128)(2,1)}, u32[]{:S(2)}) copy-start(bf16[1056,512]{1,0:T(8,128)(2,1)} %constant.55.clone.in_hi) | copy-start | bytes 3244036
  74.6 1.2 copy-start.9
  132.1 20.1 %all-to-all-start = ((bf16[32,16,512]{2,1,0:T(8,128)(2,1)}), bf16[32,16,512]{2,1,0:T(8,128)(2,1)S(1)}, u32[]{:S(2)}, u32[]{:S(2)}) async-start(bf16[32,16,512]{2,1,0:T(8,128)(2,1)} %bitcast.6), calls=%async_computation | async-start | bytes 1048576 | tf_op jit(solution)/shard_map/all_to_all | solution.py:399
  138.2 14.2 %copy-start.1 = (bf16[512,512]{1,0:T(8,128)(2,1)S(1)}, bf16[512,512]{1,0:T(8,128)(2,1)}, u32[]{:S(2)}) copy-start(bf16[512,512]{1,0:T(8,128)(2,1)} %param.18) | copy-start | bytes 1572868
  138.2 14.2 %copy-start.3 = (bf16[512,512]{1,0:T(8,128)(2,1)S(1)}, bf16[512,512]{1,0:T(8,128)(2,1)}, u32[]{:S(2)}) copy-start(bf16[512,512]{1,0:T(8,128)(2,1)} %param.20) | copy-start | bytes 1572868
  138.2 14.2 %copy-start.10 = (bf16[512,512]{1,0:T(8,128)(2,1)S(1)}, bf16[512,512]{1,0:T(8,128)(2,1)}, u32[]{:S(2)}) copy-start(bf16[512,512]{1,0:T(8,128)(2,1)} %param.21) | copy-start | bytes 1572868

commit v3 on v2

v3 whole, which is shorter than its diff:
```python
import jax
import jax.numpy as jnp
import ml_dtypes
import numpy as np
from jax import lax
from jax.experimental import pallas as pl
from jax.experimental.pallas import tpu as pltpu
from jax.sharding import PartitionSpec as P

OUTER = 64
CHUNK = 256


def split_pair(table):
    high = table.astype(np.float32).astype(ml_dtypes.bfloat16)
    low = (table - high.astype(np.float64)).astype(np.float32).astype(ml_dtypes.bfloat16)
    return high, low


def make_tables(blocks, width, inner):
    total = OUTER * inner
    half = OUTER // 2 + 1
    k = np.arange(half)
    a = np.arange(blocks)
    b = np.arange(inner)
    first = 2.0 * np.pi * (np.outer(k, a) % OUTER) / OUTER
    eye = np.eye(width)
    k_cos = np.kron(np.cos(first), eye)
    k_sin = np.kron(np.sin(first), eye)
    into = np.concatenate([k_cos, -k_sin], 0)
    weight = np.full((half, 1), 2.0)
    weight[0] = 1.0
    weight[-1] = 1.0
    weight = weight / total
    back_cos = np.kron((weight * np.cos(first)).T, eye)
    back_sin = np.kron((weight * np.sin(first)).T, eye)
    out_of = np.concatenate([back_cos, back_sin], 1)
    turn = 2.0 * np.pi * (np.outer(k, b) % total) / total
    turn = np.repeat(turn, width, axis=0)
    second = 2.0 * np.pi * (np.outer(b, b) % inner) / inner
    c, s = np.cos(second), np.sin(second)
    across = np.concatenate([np.concatenate([c, -s], 1), np.concatenate([s, c], 1)], 0)
    return (
        split_pair(into),
        split_pair(out_of),
        np.cos(turn).astype(np.float32),
        np.sin(turn).astype(np.float32),
        split_pair(across),
    )


def dot(left, right):
    return jnp.dot(left, right, preferred_element_type=jnp.float32)


def turned(real, imag, cos, sin):
    return real * cos + imag * sin, imag * cos - real * sin


ZS, XS, YS = 8, 4, 4
VMEM = pl.BlockSpec(memory_space=pltpu.VMEM)
MESH = pl.DeviceIdType.MESH
BF = jnp.bfloat16


def spread(block_of, into, twist, z_ref, inner):
    rows = z_ref.shape[0]

    @pl.loop(0, inner // CHUNK)
    def _(i):
        at = pl.ds(pl.multiple_of(i * CHUNK, CHUNK), CHUNK)
        block = block_of(at)
        y = dot(into[0][...], block) + dot(into[1][...], block)
        real, imag = turned(y[:rows], y[rows:], twist[0][:, at], twist[1][:, at])
        z_ref[:, at] = real.astype(BF)
        z_ref[:, pl.ds(pl.multiple_of(inner + i * CHUNK, CHUNK), CHUNK)] = imag.astype(BF)


def across_columns(z_ref, across, out_ref):
    @pl.loop(0, z_ref.shape[1] // CHUNK)
    def _(i):
        at = pl.ds(pl.multiple_of(i * CHUNK, CHUNK), CHUNK)
        z = z_ref[...]
        out_ref[:, at] = dot(z, across[0][:, at]) + dot(z, across[1][:, at])


def combine(grad_ref, other_ref, z_ref, inner):
    @pl.loop(0, inner // CHUNK)
    def _(i):
        at = pl.ds(pl.multiple_of(i * CHUNK, CHUNK), CHUNK)
        far = pl.ds(pl.multiple_of(inner + i * CHUNK, CHUNK), CHUNK)
        g_re, g_im = grad_ref[:, at], grad_ref[:, far]
        o_re, o_im = other_ref[:, at], other_ref[:, far]
        z_ref[:, at] = (g_re * o_re + g_im * o_im).astype(BF)
        z_ref[:, far] = (g_re * o_im - g_im * o_re).astype(BF)


def layer_kernel(
    w_hbm, g_hbm, gate_in_hbm, values_hbm, gate_out_hbm, filters_hbm, skip_ref,
    in_hi_h, in_lo_h, of_hi_h, of_lo_h, cos_h, sin_h, ac_hi_h, ac_lo_h,
    home_out, result_out,
    gate_in, values, filters, in_hi, in_lo, of_hi, of_lo, cos, sin, ac_hi, ac_lo,
    w_ring, w_mine, w_other, g_ring, g_other, own, hold, part, inbox, relay, final,
    near_gate, back_bf, gated, gated_in, stage, crossed, pair_in,
    z_ref, u_ref, spec_g, spec_p, spec_f, leaving, landed,
    send_sems, recv_sems, local_sems,
):
    s, h = lax.axis_index("seq"), lax.axis_index("ch")
    z, x = s // XS, s % XS
    y, core = h // 2, h % 2

    def zmod(d):
        return lax.rem(z + d + ZS, ZS)

    def xmod(d):
        return lax.rem(x + d + XS, XS)

    def at_z(d):
        return (zmod(d) * XS + x, h)

    def at_x(d):
        return (z * XS + xmod(d), h)

    def at_y(d):
        return (s, lax.rem(y + d + YS, YS) * 2 + core)

    sibling = (s, y * 2 + 1 - core)
    peers = [at_z(d) for d in range(1, ZS)] + [at_x(d) for d in range(1, XS)]
    peers += [at_y(d) for d in (1, -1)] + [sibling]

    barrier = pltpu.get_barrier_semaphore()
    for peer in peers:
        pl.semaphore_signal(barrier, inc=1, device_id=peer, device_id_type=MESH)

    loads = []

    def load(src, dst):
        copy = pltpu.make_async_copy(src, dst, local_sems.at[len(loads)])
        copy.start()
        loads.append(copy)
        return copy

    w_load = load(w_hbm, w_ring.at[z])
    g_load = load(g_hbm, g_ring.at[x])
    pair_loads = [load(gate_in_hbm, gate_in), load(values_hbm, values), load(filters_hbm, filters)]
    gate_load = load(gate_out_hbm.at[x], near_gate.at[0])
    table_loads = [
        load(src, dst)
        for src, dst in (
            (in_hi_h, in_hi), (in_lo_h, in_lo), (ac_hi_h, ac_hi), (ac_lo_h, ac_lo),
            (cos_h, cos), (sin_h, sin), (of_hi_h, of_hi), (of_lo_h, of_lo),
        )
    ]
    pl.semaphore_wait(barrier, len(peers))

    copies = []

    def send(src, dst, device):
        k = len(copies)
        copy = pltpu.make_async_remote_copy(
            src_ref=src, dst_ref=dst, send_sem=send_sems.at[k], recv_sem=recv_sems.at[k],
            device_id=device, device_id_type=MESH,
        )
        copy.start()
        copies.append(copy)
        return copy

    half_w = w_ring.shape[1] // 2
    half_g = g_ring.shape[1] // 2
    first, second = pl.ds(0, half_w), pl.ds(half_w, half_w)
    top, low = pl.ds(0, half_g), pl.ds(half_g, half_g)

    up = send(w_hbm, w_ring.at[z], at_z(1))
    down = send(w_hbm, w_ring.at[z], at_z(-1))
    right_top = send(g_hbm.at[top], g_ring.at[x, top], at_x(1))
    left_low = send(g_hbm.at[low], g_ring.at[x, low], at_x(-1))
    right_low = send(g_hbm.at[low], g_ring.at[x, low], at_x(1))
    left_top = send(g_hbm.at[top], g_ring.at[x, top], at_x(-1))
    shared = [send(g_hbm, g_other.at[0], sibling)]
    for copy in pair_loads:
        copy.wait()
    for i in range(XS):
        product = gate_in[i].astype(jnp.float32) * values[i].astype(jnp.float32)
        stage[0, i] = product.astype(BF)
        stage[1, i] = filters[i].astype(BF)

    up.wait_recv()
    up = send(w_ring.at[zmod(-1)], w_ring.at[zmod(-1)], at_z(1))
    down.wait_recv()
    down = send(w_ring.at[zmod(1)], w_ring.at[zmod(1)], at_z(-1))
    right_top.wait_recv()
    far_top = send(g_ring.at[xmod(-1), top], g_ring.at[xmod(-1), top], at_x(1))
    left_low.wait_recv()
    far_low = send(g_ring.at[xmod(1), low], g_ring.at[xmod(1), low], at_x(-1))
    gates = [send(gate_out_hbm.at[xmod(d)], near_gate.at[d], at_x(d)) for d in range(1, XS)]
    up.wait_recv()
    up = send(w_ring.at[zmod(-2)], w_ring.at[zmod(-2)], at_z(1))
    down.wait_recv()
    down = send(w_ring.at[zmod(2)], w_ring.at[zmod(2)], at_z(-1))
    up.wait_recv()
    up = send(w_ring.at[zmod(-3), first], w_ring.at[zmod(-3), first], at_z(1))
    down.wait_recv()
    down = send(w_ring.at[zmod(3), second], w_ring.at[zmod(3), second], at_z(-1))
    pairs = [
        send(stage.at[:, :, zmod(d)], crossed.at[:, z], at_z(d)) for d in range(1, ZS)
    ]
    crossed[:, z] = stage[:, :, z]
    w_load.wait()
    g_load.wait()
    up.wait_recv()
    down.wait_recv()

    def rows_for(d, of_core):
        return lax.rem(y + d, YS) * 2 + of_core

    w_shared = [
        send(w_ring.at[rows_for(d, 1 - core)], w_other.at[d], sibling) for d in range(YS)
    ]
    for d in range(YS):
        w_mine[d] = w_ring[rows_for(d, core)]
    right_low.wait_recv()
    shared.append(send(g_ring.at[xmod(-1)], g_other.at[1], sibling))
    left_top.wait_recv()
    shared.append(send(g_ring.at[xmod(1)], g_other.at[2], sibling))
    for copy in w_shared:
        copy.wait_recv()

    offsets = (0, -1, 1, 2)
    parts = []
    passed = []
    deep = w_ring.shape[1]
    wide = (YS * deep, w_ring.shape[2])

    def pass_on(n):
        for side in range(2):
            parts[n][side].wait_recv()
            relay[n, side] = (hold[n, side] + inbox[n, side, 0].astype(jnp.float32)).astype(BF)
            passed.append(send(relay.at[n, side], final.at[n, side], at_y(1 - 2 * side)))

    for n, off in enumerate(offsets):
        if n == 3:
            far_top.wait_recv()
            far_low.wait_recv()
            shared.append(send(g_ring.at[xmod(2)], g_other.at[3], sibling))
        shared[n].wait_recv()

        @pl.loop(0, g_ring.shape[1] // CHUNK)
        def _(i, n=n, off=off):
            at = pl.ds(pl.multiple_of(i * CHUNK, CHUNK), CHUNK)
            form = (((1,), (1,)), ((), ()))
            total = lax.dot_general(
                w_mine[...].reshape(wide), g_ring[xmod(off), at, :], form,
                preferred_element_type=jnp.float32,
            ) + lax.dot_general(
                w_other[...].reshape(wide), g_other[n, at, :], form,
                preferred_element_type=jnp.float32,
            )
            total = total.reshape(YS, deep, CHUNK)
            own[n, :, at] = total[0]
            hold[n, 0, :, at] = total[1, :half_w]
            hold[n, 1, :, at] = total[3, half_w:]
            part[n, 0, 0, :, at] = total[2, :half_w].astype(BF)
            part[n, 0, 1, :, at] = total[1, half_w:].astype(BF)
            part[n, 1, 0, :, at] = total[2, half_w:].astype(BF)
            part[n, 1, 1, :, at] = total[3, :half_w].astype(BF)

        parts.append([send(part.at[n, side], inbox.at[n, side], at_y(1 - 2 * side)) for side in range(2)])
        if n:
            pass_on(n - 1)

    for copy in pairs:
        copy.wait_recv()
    tails = [
        send(crossed.at[:, :, xmod(d)], pair_in.at[:, :, x], at_x(d)) for d in range(1, XS)
    ]
    pair_in[:, :, x] = crossed[:, :, x]
    pass_on(len(offsets) - 1)

    gate_load.wait()
    arrivals = []
    homes = []
    for n, off in enumerate(offsets):
        for copy in passed[2 * n : 2 * n + 2]:
            copy.wait_recv()
        d = -off % XS
        if d:
            gates[d - 1].wait_recv()
        upper = own[n, :half_w] + final[n, 0].astype(jnp.float32) + inbox[n, 1, 1].astype(jnp.float32)
        lower = own[n, half_w:] + final[n, 1].astype(jnp.float32) + inbox[n, 0, 1].astype(jnp.float32)
        back = jnp.concatenate([upper, lower], 0)
        result = back * near_gate[d].astype(jnp.float32)
        gated[n] = result.astype(BF).reshape(gated.shape[1:])
        for d in range(1, ZS):
            arrivals.append(send(gated.at[n, zmod(d)], gated_in.at[z, xmod(off)], at_z(d)))
        gated_in[z, xmod(off)] = gated[n, z]
        back_bf[n] = back.astype(BF)
        if n == 0:
            home_out[x] = back_bf[n]
        else:
            homes.append(send(back_bf.at[n], home_out.at[x], at_x(off)))

    inner = g_ring.shape[2]
    rows = g_ring.shape[1]
    into, twist, across = (in_hi, in_lo), (cos, sin), (ac_hi, ac_lo)
    for copy in table_loads:
        copy.wait()
    for copy in tails:
        copy.wait_recv()
    for i, spec in ((1, spec_f), (0, spec_p)):
        spread(lambda at, i=i: pair_in[i, :, :, :, at].reshape(rows, CHUNK), into, twist, z_ref, inner)
        across_columns(z_ref, across, spec)
    for copy in arrivals:
        copy.wait_recv()
    spread(lambda at: gated_in[:, :, :, at].reshape(rows, CHUNK), into, twist, z_ref, inner)
    across_columns(z_ref, across, spec_g)

    width = gated_in.shape[2]
    lanes = skip_ref.shape[1]
    pick = lax.broadcasted_iota(jnp.int32, (width, lanes), 1) == z * width + lax.broadcasted_iota(
        jnp.int32, (width, lanes), 0
    )
    scale = jnp.sum(jnp.where(pick, skip_ref[pl.ds(x, 1), :], 0.0), axis=1, keepdims=True)
    spec_rows = z_ref.shape[0]
    gone = []
    turns = []

    def turn_x(k):
        for copy in gone[k]:
            copy.wait_recv()
        turns.extend(
            send(landed.at[k, :, xmod(d)], result_out.at[k, x], at_x(d)) for d in range(1, XS)
        )
        result_out[k, x] = landed[k, :, x]

    for k in range(4):
        which, c = divmod(k, 2)
        if c == 0:
            combine(spec_g, (spec_p, spec_f)[which], z_ref, inner)
        at, far = pl.ds(c * CHUNK, CHUNK), pl.ds(inner + c * CHUNK, CHUNK)
        values_z = z_ref[...]
        real = dot(values_z, ac_hi[:, at]) + dot(values_z, ac_lo[:, at])
        imag = dot(values_z, ac_hi[:, far]) + dot(values_z, ac_lo[:, far])
        real, imag = turned(real, imag, cos[:, at], sin[:, at])
        u_ref[:spec_rows, :] = real.astype(BF)
        u_ref[spec_rows:, :] = imag.astype(BF)
        u = u_ref[...]
        out = (dot(of_hi[...], u) + dot(of_lo[...], u)).reshape(leaving.shape[1:])
        if which == 1:
            out = out + scale * gated_in[:, :, :, at].astype(jnp.float32)
        leaving[k] = out.astype(BF)
        gone.append(
            [send(leaving.at[k, zmod(d)], landed.at[k, z], at_z(d)) for d in range(1, ZS)]
        )
        landed[k, z] = leaving[k, z]
        if k >= 2:
            turn_x(k - 2)
    turn_x(2)
    turn_x(3)
    for copy in homes + turns:
        copy.wait_recv()
    for copy in copies:
        copy.wait_send()


def layer(grad_out, out_weight, gate_in, gate_out, values, filters, skip_scale):
    rows, inner = gate_in.shape
    deep, wide = out_weight.shape
    width = rows // (ZS * XS)
    into, out_of, cos, sin, across = make_tables(ZS * XS, width, inner)
    tables = (*into, *out_of, cos, sin, *across)
    spec_rows = cos.shape[0]
    split = (XS, ZS, width, inner)
    parts = inner // CHUNK
    count = 122

    def vmem(shape, dtype=BF):
        return pltpu.VMEM(shape, dtype)

    spec = vmem((spec_rows, 2 * inner), jnp.float32)
    return pl.pallas_call(
        layer_kernel,
        out_shape=[
            jax.ShapeDtypeStruct((XS, deep, inner), BF),
            jax.ShapeDtypeStruct((2 * parts, XS, ZS, width, CHUNK), BF),
        ],
        in_specs=[pl.BlockSpec(memory_space=pl.ANY)] * 6
        + [VMEM]
        + [pl.BlockSpec(memory_space=pl.ANY)] * len(tables),
        out_specs=[VMEM] * 2,
        scratch_shapes=[
            vmem(split),
            vmem(split),
            vmem(split, jnp.float32),
            *[vmem(t.shape, t.dtype) for t in tables],
            vmem((ZS, deep, wide)),
            vmem((YS, deep, wide)),
            vmem((YS, deep, wide)),
            vmem((XS,) + grad_out.shape),
            vmem((XS,) + grad_out.shape),
            vmem((XS, deep, inner), jnp.float32),
            vmem((XS, 2, deep // 2, inner), jnp.float32),
            vmem((XS, 2, 2, deep // 2, inner)),
            vmem((XS, 2, 2, deep // 2, inner)),
            vmem((XS, 2, deep // 2, inner)),
            vmem((XS, 2, deep // 2, inner)),
            vmem((XS, deep, inner)),
            vmem((XS, deep, inner)),
            vmem((XS, ZS, width, inner)),
            vmem((ZS, XS, width, inner)),
            vmem((2,) + split),
            vmem((2, ZS, XS, width, inner)),
            vmem((2, ZS, XS, width, inner)),
            vmem((spec_rows, 2 * inner)),
            vmem((2 * spec_rows, CHUNK)),
            spec,
            spec,
            spec,
            vmem((2 * parts, ZS, XS, width, CHUNK)),
            vmem((2 * parts, ZS, XS, width, CHUNK)),
            pltpu.SemaphoreType.DMA((count,)),
            pltpu.SemaphoreType.DMA((count,)),
            pltpu.SemaphoreType.DMA((14,)),
        ],
        compiler_params=pltpu.CompilerParams(
            collective_id=0, has_side_effects=True, vmem_limit_bytes=58 * 1024 * 1024
        ),
        cost_estimate=pl.CostEstimate(flops=20 * 10**9, bytes_accessed=20 * 10**6, transcendentals=0),
    )(
        out_weight,
        grad_out,
        gate_in.reshape(split),
        values.reshape(split),
        gate_out.reshape(XS, deep, inner),
        filters.reshape(split),
        skip_scale.reshape(XS, deep),
        *tables,
    )


def shards(grad_out, out_weight, gate_in, gate_out, values, conv_out, filters, skip_scale):
    rows, inner = gate_in.shape
    home, result = layer(grad_out, out_weight, gate_in, gate_out, values, filters, skip_scale)
    back = home.reshape(rows, inner).astype(jnp.float32)
    grad_gate_out = (back * conv_out.astype(jnp.float32)).astype(BF)
    result = result.reshape(2, inner // CHUNK, rows, CHUNK).transpose(0, 2, 1, 3)
    result = result.reshape(2, rows, inner).astype(jnp.float32)
    grad_gate_in = (result[1] * values.astype(jnp.float32)).astype(BF)
    grad_values = (result[1] * gate_in.astype(jnp.float32)).astype(BF)
    return (grad_gate_in, grad_values, grad_gate_out, result[0])


def solution(mesh):
    placed = (
        P("seq", "ch"),
        P("seq", "ch"),
        P("ch", "seq"),
        P("ch", "seq"),
        P("ch", "seq"),
        P("ch", "seq"),
        P("ch", "seq"),
        P("ch"),
    )
    return jax.shard_map(
        shards,
        mesh=mesh,
        in_specs=placed,
        out_specs=(P("ch", "seq"), P("ch", "seq"), P("ch", "seq"), P("ch", "seq")),
        check_vma=False,
    )
```

time: 156 us -> 119 us (0.76); the launches traced: 154 us -> 119 us
  blocking collectives: 22 us -> 0 us
  waiting for transfers between devices: 14 us -> 0 us
  Pallas kernels: 101 us -> 111 us
  local copies, waits for them, and re-layouts: 9.31 us -> 4.28 us
  starting transfers between devices: 4.97 us -> 0 us
    all_to_all x1 -> x0, blocking collectives: 22 us -> none  [shards(): lax.all_to_all(both[i].reshape(blocks, width, inner), 'seq', split_axis=0...]
    all_to_all x1 -> x0, waiting for transfers between devices: 14 us -> none  [shards(): lax.all_to_all(both[i].reshape(blocks, width, inner), 'seq', split_axis=0...]
    pallas_call x3 -> x1, Pallas kernels: 101 us -> 111 us  [layer(): pl.pallas_call(layer_kernel, out_shape=[jax.ShapeDtypeStruct((XS, deep, i...]
    all_to_all x1 -> x0, starting transfers between devices: 4.97 us -> none  [shards(): lax.all_to_all(both[i].reshape(blocks, width, inner), 'seq', split_axis=0...]
    unnamed x22 -> x10, local copies, waits for them, and re-layouts: 6.3 us -> 2.52 us
  transfers between devices with their start and end apart: 1 -> 0, of which waited for: 1 -> 0; matrix products, arithmetic and copies ran while one was open for 1% -> 0% of each run, Pallas kernels for 0% -> 0%
where the time goes in v3:
time: 119 us
  Pallas kernels  111 us (93%)
  local copies, waits for them, and re-layouts  4.28 us (4%)
  other arithmetic  2.86 us (2%)
    pallas_call x1, Pallas kernels, layer(): pl.pallas_call(layer_kernel, out_shape=[jax.ShapeDtypeStruct((XS, deep, i...  111 us
    unnamed x10, local copies, waits for them, and re-layouts  2.52 us

profile of v3, /device:TPU:1, one launch (start us, length us, event | category | flops | bytes accessed | tf_op | source)
XLA Modules:
  0.0 119.0 jit_solution(3373099724639896441)
XLA Ops:
  0.6 111.2 %shard_map.183 = (bf16[4,128,512]{2,1,0:T(8,128)(2,1)}, bf16[4,4,8,16,256]{4,3,2,1,0:T(8,128)(2,1)}) custom-call(bf16[128,512]{1,0:T(8,128)(2,1)} %w_hbm.1, bf16[512,512]{1,0:T(8,128)(2,1)} %g_hbm.1, bf16[4,8,16,512]{3,2,1,0:T(8,128)(2,1)} %bitcast.23, bf16[4,8,16,512]{3,2,1,0:T(8,128)(2,1)} %bitcast.24, bf16[4,128,512]{2,1,0:T(8,128)(2,1)} %bitcast.26, ...), custom_call_target="tpu_custom_call" | custom-call | flops 20000000000 | bytes 20000000 | tf_op jit(solution)/shard_map/pallas_call | solution.py:380
  111.8 1.4 %convert_bitcast_fusion = f32[2,512,2,256]{3,1,2,0:T(8,128)S(1)} fusion(bf16[2,2,512,256]{3,2,1,0:T(8,128)(2,1)} %bitcast.21), kind=kLoop, calls=%fused_computation | loop fusion | flops 524288 | bytes 3145728 | tf_op jit(solution)/shard_map/convert_element_type | solution.py:446
  113.2 0.1 fusion.1
  113.4 0.8 copy.21
  114.2 1.0 copy.23
  115.2 0.8 copy.20
  116.0 0.0 copy-start
  116.1 0.0 copy-start.1
  116.1 0.0 copy-start.2
  116.1 0.0 copy-start.3
  116.1 0.1 copy.22
  116.2 0.9 copy-done
  117.1 0.2 copy-done.1
  117.2 0.2 copy-done.2
  117.4 0.2 copy-done.3
  117.6 1.5 %multiply_convert_fusion = (bf16[512,512]{1,0:T(8,128)(2,1)}, bf16[512,512]{1,0:T(8,128)(2,1)}, bf16[512,512]{1,0:T(8,128)(2,1)}) fusion(f32[512,512]{1,0:T(8,128)S(1)} %bitcast.20, bf16[512,512]{1,0:T(8,128)(2,1)S(1)} %copy-done, bf16[512,512]{1,0:T(8,128)(2,1)S(1)} %copy-done.1, bf16[512,512]{1,0:T(8,128)(2,1)S(1)} %copy-done.2, ...), kind=kLoop, calls=%fused_computation.3 | loop fusion | flops 2621440 | bytes 4718592 | tf_op jit(solution)/shard_map/convert_element_type | solution.py:448
Async XLA Ops:
  116.0 1.0 copy-start
  116.1 1.2 %copy-start.1 = (bf16[512,512]{1,0:T(8,128)(2,1)S(1)}, bf16[512,512]{1,0:T(8,128)(2,1)}, u32[]{:S(2)}) copy-start(bf16[512,512]{1,0:T(8,128)(2,1)} %param.20) | copy-start | bytes 1572868
  116.1 1.3 %copy-start.2 = (bf16[512,512]{1,0:T(8,128)(2,1)S(1)}, bf16[512,512]{1,0:T(8,128)(2,1)}, u32[]{:S(2)}) copy-start(bf16[512,512]{1,0:T(8,128)(2,1)} %param.21) | copy-start | bytes 1572868
  116.1 1.5 %copy-start.3 = (bf16[4,128,512]{2,1,0:T(8,128)(2,1)S(1)}, bf16[4,128,512]{2,1,0:T(8,128)(2,1)}, u32[]{:S(2)}) copy-start(bf16[4,128,512]{2,1,0:T(8,128)(2,1)} %get-tuple-element.7) | copy-start | bytes 1572868

commit v4 on v3

--- a/solution.py
+++ b/solution.py
@@ -1,3 +1,5 @@
+import functools
+
 import jax
 import jax.numpy as jnp
 import ml_dtypes
@@ -63,25 +65,26 @@
 BF = jnp.bfloat16
 
 
-def spread(block_of, into, twist, z_ref, inner):
+def forward_pieces(block_of, into, twist, across, z_ref, out_ref):
     rows = z_ref.shape[0]
-
-    @pl.loop(0, inner // CHUNK)
-    def _(i):
-        at = pl.ds(pl.multiple_of(i * CHUNK, CHUNK), CHUNK)
+    inner = z_ref.shape[1] // 2
+
+    def spread(c):
+        at = pl.ds(c * CHUNK, CHUNK)
         block = block_of(at)
-        y = dot(into[0][...], block) + dot(into[1][...], block)
+        y = sum(dot(table[...], block) for table in into)
         real, imag = turned(y[:rows], y[rows:], twist[0][:, at], twist[1][:, at])
         z_ref[:, at] = real.astype(BF)
-        z_ref[:, pl.ds(pl.multiple_of(inner + i * CHUNK, CHUNK), CHUNK)] = imag.astype(BF)
-
-
-def across_columns(z_ref, across, out_ref):
-    @pl.loop(0, z_ref.shape[1] // CHUNK)
-    def _(i):
-        at = pl.ds(pl.multiple_of(i * CHUNK, CHUNK), CHUNK)
+        z_ref[:, pl.ds(inner + c * CHUNK, CHUNK)] = imag.astype(BF)
+
+    def columns(c):
+        at = pl.ds(c * CHUNK, CHUNK)
         z = z_ref[...]
-        out_ref[:, at] = dot(z, across[0][:, at]) + dot(z, across[1][:, at])
+        out_ref[:, at] = sum(dot(z, table[:, at]) for table in across)
+
+    pieces = [functools.partial(spread, c) for c in range(inner // CHUNK)]
+    pieces += [functools.partial(columns, c) for c in range(2 * inner // CHUNK)]
+    return pieces
 
 
 def combine(grad_ref, other_ref, z_ref, inner):
@@ -98,7 +101,7 @@
 def layer_kernel(
     w_hbm, g_hbm, gate_in_hbm, values_hbm, gate_out_hbm, filters_hbm, skip_ref,
     in_hi_h, in_lo_h, of_hi_h, of_lo_h, cos_h, sin_h, ac_hi_h, ac_lo_h,
-    home_out, result_out,
+    home_out, filters_out, mixed_out,
     gate_in, values, filters, in_hi, in_lo, of_hi, of_lo, cos, sin, ac_hi, ac_lo,
     w_ring, w_mine, w_other, g_ring, g_other, own, hold, part, inbox, relay, final,
     near_gate, back_bf, gated, gated_in, stage, crossed, pair_in,
@@ -197,18 +200,33 @@
     up = send(w_ring.at[zmod(-2)], w_ring.at[zmod(-2)], at_z(1))
     down.wait_recv()
     down = send(w_ring.at[zmod(2)], w_ring.at[zmod(2)], at_z(-1))
+    over_z = {}
+    over_x = {}
+
+    def pair_z(i):
+        over_z[i] = [
+            send(stage.at[i, :, zmod(d)], crossed.at[i, z], at_z(d)) for d in range(1, ZS)
+        ]
+        crossed[i, z] = stage[i, :, z]
+
+    def pair_x(i):
+        for copy in over_z[i]:
+            copy.wait_recv()
+        over_x[i] = [
+            send(crossed.at[i, :, xmod(d)], pair_in.at[i, :, x], at_x(d)) for d in range(1, XS)
+        ]
+        pair_in[i, :, x] = crossed[i, :, x]
+
+    pair_z(1)
     up.wait_recv()
     up = send(w_ring.at[zmod(-3), first], w_ring.at[zmod(-3), first], at_z(1))
     down.wait_recv()
     down = send(w_ring.at[zmod(3), second], w_ring.at[zmod(3), second], at_z(-1))
-    pairs = [
-        send(stage.at[:, :, zmod(d)], crossed.at[:, z], at_z(d)) for d in range(1, ZS)
-    ]
-    crossed[:, z] = stage[:, :, z]
     w_load.wait()
     g_load.wait()
     up.wait_recv()
     down.wait_recv()
+    pair_z(0)
 
     def rows_for(d, of_core):
         return lax.rem(y + d, YS) * 2 + of_core
@@ -265,26 +283,19 @@
             part[n, 1, 1, :, at] = total[3, :half_w].astype(BF)
 
         parts.append([send(part.at[n, side], inbox.at[n, side], at_y(1 - 2 * side)) for side in range(2)])
-        if n:
-            pass_on(n - 1)
-
-    for copy in pairs:
-        copy.wait_recv()
-    tails = [
-        send(crossed.at[:, :, xmod(d)], pair_in.at[:, :, x], at_x(d)) for d in range(1, XS)
-    ]
-    pair_in[:, :, x] = crossed[:, :, x]
-    pass_on(len(offsets) - 1)
-
-    gate_load.wait()
+
     arrivals = []
     homes = []
-    for n, off in enumerate(offsets):
+
+    def total_up(n):
+        off = offsets[n]
         for copy in passed[2 * n : 2 * n + 2]:
             copy.wait_recv()
         d = -off % XS
         if d:
             gates[d - 1].wait_recv()
+        else:
+            gate_load.wait()
         upper = own[n, :half_w] + final[n, 0].astype(jnp.float32) + inbox[n, 1, 1].astype(jnp.float32)
         lower = own[n, half_w:] + final[n, 1].astype(jnp.float32) + inbox[n, 0, 1].astype(jnp.float32)
         back = jnp.concatenate([upper, lower], 0)
@@ -294,25 +305,48 @@
             arrivals.append(send(gated.at[n, zmod(d)], gated_in.at[z, xmod(off)], at_z(d)))
         gated_in[z, xmod(off)] = gated[n, z]
         back_bf[n] = back.astype(BF)
-        if n == 0:
-            home_out[x] = back_bf[n]
-        else:
-            homes.append(send(back_bf.at[n], home_out.at[x], at_x(off)))
 
     inner = g_ring.shape[2]
     rows = g_ring.shape[1]
     into, twist, across = (in_hi, in_lo), (cos, sin), (ac_hi, ac_lo)
+
+    def pair_block(i):
+        return lambda at: pair_in[i, :, :, :, at].reshape(rows, CHUNK)
+
+    pass_on(0)
+    pass_on(1)
+    pair_x(1)
+    pass_on(2)
+    total_up(0)
+    pass_on(3)
+    total_up(1)
     for copy in table_loads:
         copy.wait()
-    for copy in tails:
+    for copy in over_x[1]:
         copy.wait_recv()
-    for i, spec in ((1, spec_f), (0, spec_p)):
-        spread(lambda at, i=i: pair_in[i, :, :, :, at].reshape(rows, CHUNK), into, twist, z_ref, inner)
-        across_columns(z_ref, across, spec)
+    pieces = forward_pieces(pair_block(1), into, twist, across, z_ref, spec_f)
+    for piece in pieces[:2]:
+        piece()
+    total_up(2)
+    pieces[2]()
+    total_up(3)
+    pair_x(0)
+    for piece in pieces[3:]:
+        piece()
+    for copy in over_x[0]:
+        copy.wait_recv()
+    for piece in forward_pieces(pair_block(0), into, twist, across, z_ref, spec_p):
+        piece()
+    home_out[x] = back_bf[0]
+    for n, off in enumerate(offsets):
+        if n:
+            homes.append(send(back_bf.at[n], home_out.at[x], at_x(off)))
     for copy in arrivals:
         copy.wait_recv()
-    spread(lambda at: gated_in[:, :, :, at].reshape(rows, CHUNK), into, twist, z_ref, inner)
-    across_columns(z_ref, across, spec_g)
+    for piece in forward_pieces(
+        lambda at: gated_in[:, :, :, at].reshape(rows, CHUNK), into, twist, across[:1], z_ref, spec_g
+    ):
+        piece()
 
     width = gated_in.shape[2]
     lanes = skip_ref.shape[1]
@@ -327,10 +361,14 @@
     def turn_x(k):
         for copy in gone[k]:
             copy.wait_recv()
+        which, c = divmod(k, 2)
+        result = (filters_out, mixed_out)[which]
+        at = pl.ds(c * CHUNK, CHUNK)
         turns.extend(
-            send(landed.at[k, :, xmod(d)], result_out.at[k, x], at_x(d)) for d in range(1, XS)
+            send(landed.at[k, :, xmod(d)], result.at[x, :, :, at], at_x(d))
+            for d in range(1, XS)
         )
-        result_out[k, x] = landed[k, :, x]
+        result[x, :, :, at] = landed[k, :, x]
 
     for k in range(4):
         which, c = divmod(k, 2)
@@ -371,7 +409,7 @@
     spec_rows = cos.shape[0]
     split = (XS, ZS, width, inner)
     parts = inner // CHUNK
-    count = 122
+    count = 132
 
     def vmem(shape, dtype=BF):
         return pltpu.VMEM(shape, dtype)
@@ -381,12 +419,13 @@
         layer_kernel,
         out_shape=[
             jax.ShapeDtypeStruct((XS, deep, inner), BF),
-            jax.ShapeDtypeStruct((2 * parts, XS, ZS, width, CHUNK), BF),
+            jax.ShapeDtypeStruct(split, BF),
+            jax.ShapeDtypeStruct(split, BF),
         ],
         in_specs=[pl.BlockSpec(memory_space=pl.ANY)] * 6
         + [VMEM]
         + [pl.BlockSpec(memory_space=pl.ANY)] * len(tables),
-        out_specs=[VMEM] * 2,
+        out_specs=[VMEM] * 3,
         scratch_shapes=[
             vmem(split),
             vmem(split),
@@ -439,14 +478,17 @@
 
 def shards(grad_out, out_weight, gate_in, gate_out, values, conv_out, filters, skip_scale):
     rows, inner = gate_in.shape
-    home, result = layer(grad_out, out_weight, gate_in, gate_out, values, filters, skip_scale)
-    back = home.reshape(rows, inner).astype(jnp.float32)
-    grad_gate_out = (back * conv_out.astype(jnp.float32)).astype(BF)
-    result = result.reshape(2, inner // CHUNK, rows, CHUNK).transpose(0, 2, 1, 3)
-    result = result.reshape(2, rows, inner).astype(jnp.float32)
-    grad_gate_in = (result[1] * values.astype(jnp.float32)).astype(BF)
-    grad_values = (result[1] * gate_in.astype(jnp.float32)).astype(BF)
-    return (grad_gate_in, grad_values, grad_gate_out, result[0])
+    home, grad_filters, mixed = layer(
+        grad_out, out_weight, gate_in, gate_out, values, filters, skip_scale
+    )
+
+    def wide(block):
+        return block.reshape(rows, inner).astype(jnp.float32)
+
+    grad_gate_out = (wide(home) * wide(conv_out)).astype(BF)
+    grad_gate_in = (wide(mixed) * wide(values)).astype(BF)
+    grad_values = (wide(mixed) * wide(gate_in)).astype(BF)
+    return (grad_gate_in, grad_values, grad_gate_out, wide(grad_filters))
 
 
 def solution(mesh):

time: 119 us -> 117 us (0.983)
  local copies, waits for them, and re-layouts: 4.28 us -> 0.02 us
  Pallas kernels: 111 us -> 113 us
    unnamed x10 -> x8, local copies, waits for them, and re-layouts: 2.52 us -> 0.02 us
    slice x3 -> x0, local copies, waits for them, and re-layouts: 1.76 us -> none  [the longest x2 0.95 us: shards(): return (grad_gate_in, grad_values, grad_gate_out, result[0])]
    pallas_call x1, Pallas kernels: 111 us -> 113 us  [layer(): pl.pallas_call(layer_kernel, out_shape=[jax.ShapeDtypeStruct((XS, deep, i...]
where the time goes in v4:
time: 117 us
  Pallas kernels  113 us (97%)
  other arithmetic  3.79 us (3%)
    pallas_call x1, Pallas kernels, layer(): pl.pallas_call(layer_kernel, out_shape=[jax.ShapeDtypeStruct((XS, deep, i...  113 us
    convert_element_type x1, other arithmetic, shards(): grad_values = (wide(mixed) * wide(gate_in)).astype(BF)  2.65 us

profile of v4, /device:TPU:1, one launch (start us, length us, event | category | flops | bytes accessed | tf_op | source)
XLA Modules:
  0.0 117.3 jit_solution(16603706293417865175)
XLA Ops:
  0.6 0.0 copy-start.1
  0.6 0.0 copy-start.2
  0.7 0.0 copy-start.3
  0.7 112.8 %shard_map.183 = (bf16[4,128,512]{2,1,0:T(8,128)(2,1)}, bf16[4,8,16,512]{3,2,1,0:T(8,128)(2,1)}, bf16[4,8,16,512]{3,2,1,0:T(8,128)(2,1)}) custom-call(bf16[128,512]{1,0:T(8,128)(2,1)} %w_hbm.1, bf16[512,512]{1,0:T(8,128)(2,1)} %g_hbm.1, bf16[4,8,16,512]{3,2,1,0:T(8,128)(2,1)} %bitcast.15, bf16[4,8,16,512]{3,2,1,0:T(8,128)(2,1)} %bitcast.16, ...), custom_call_target="tpu_custom_call" | custom-call | flops 20000000000 | bytes 20000000 | tf_op jit(solution)/shard_map/pallas_call | solution.py:418
  113.5 0.0 copy-done.1
  113.5 0.0 copy-done.2
  113.5 0.0 copy-done.3
  113.5 0.0 copy-start
  113.5 2.6 %fusion.1 = (bf16[512,512]{1,0:T(8,128)(2,1)}, bf16[512,512]{1,0:T(8,128)(2,1)}, bf16[512,512]{1,0:T(8,128)(2,1)}) fusion(bf16[512,512]{1,0:T(8,128)(2,1)S(1)} %copy-done.1, bf16[4,8,16,512]{3,2,1,0:T(8,128)(2,1)} %get-tuple-element.7, bf16[512,512]{1,0:T(8,128)(2,1)S(1)} %copy-done.2, bf16[512,512]{1,0:T(8,128)(2,1)S(1)} %copy-done.3, ...), kind=kLoop, calls=%fused_computation.3 | loop fusion | flops 2883584 | bytes 4194304 | tf_op jit(solution)/shard_map/convert_element_type | solution.py:490
  116.2 0.0 copy-done
  116.2 1.1 bitcast_convert_fusion
Async XLA Ops:
  0.6 112.9 %copy-start.1 = (bf16[512,512]{1,0:T(8,128)(2,1)S(1)}, bf16[512,512]{1,0:T(8,128)(2,1)}, u32[]{:S(2)}) copy-start(bf16[512,512]{1,0:T(8,128)(2,1)} %param.18) | copy-start | bytes 1572868
  0.6 112.9 %copy-start.2 = (bf16[512,512]{1,0:T(8,128)(2,1)S(1)}, bf16[512,512]{1,0:T(8,128)(2,1)}, u32[]{:S(2)}) copy-start(bf16[512,512]{1,0:T(8,128)(2,1)} %param.20) | copy-start | bytes 1572868
  0.7 112.9 %copy-start.3 = (bf16[512,512]{1,0:T(8,128)(2,1)S(1)}, bf16[512,512]{1,0:T(8,128)(2,1)}, u32[]{:S(2)}) copy-start(bf16[512,512]{1,0:T(8,128)(2,1)} %param.21) | copy-start | bytes 1572868
  113.5 2.7 %copy-start = (bf16[4,8,16,512]{3,2,1,0:T(8,128)(2,1)S(1)}, bf16[4,8,16,512]{3,2,1,0:T(8,128)(2,1)}, u32[]{:S(2)}) copy-start(bf16[4,8,16,512]{3,2,1,0:T(8,128)(2,1)} %get-tuple-element.9) | copy-start | bytes 1572868

commit v5 on v4

--- a/solution.py
+++ b/solution.py
@@ -203,11 +203,12 @@
     over_z = {}
     over_x = {}
 
-    def pair_z(i):
-        over_z[i] = [
-            send(stage.at[i, :, zmod(d)], crossed.at[i, z], at_z(d)) for d in range(1, ZS)
-        ]
-        crossed[i, z] = stage[i, :, z]
+    def pair_z(i, start, size):
+        at = pl.ds(start, size)
+        over_z.setdefault(i, []).extend(
+            send(stage.at[i, at, zmod(d)], crossed.at[i, z, at], at_z(d)) for d in range(1, ZS)
+        )
+        crossed[i, z, at] = stage[i, at, z]
 
     def pair_x(i):
         for copy in over_z[i]:
@@ -217,7 +218,7 @@
         ]
         pair_in[i, :, x] = crossed[i, :, x]
 
-    pair_z(1)
+    pair_z(1, 0, XS)
     up.wait_recv()
     up = send(w_ring.at[zmod(-3), first], w_ring.at[zmod(-3), first], at_z(1))
     down.wait_recv()
@@ -226,7 +227,7 @@
     g_load.wait()
     up.wait_recv()
     down.wait_recv()
-    pair_z(0)
+    pair_z(0, 0, XS // 2)
 
     def rows_for(d, of_core):
         return lax.rem(y + d, YS) * 2 + of_core
@@ -330,17 +331,10 @@
     total_up(2)
     pieces[2]()
     total_up(3)
-    pair_x(0)
+    pair_z(0, XS // 2, XS // 2)
     for piece in pieces[3:]:
         piece()
-    for copy in over_x[0]:
-        copy.wait_recv()
-    for piece in forward_pieces(pair_block(0), into, twist, across, z_ref, spec_p):
-        piece()
     home_out[x] = back_bf[0]
-    for n, off in enumerate(offsets):
-        if n:
-            homes.append(send(back_bf.at[n], home_out.at[x], at_x(off)))
     for copy in arrivals:
         copy.wait_recv()
     for piece in forward_pieces(
@@ -362,7 +356,7 @@
         for copy in gone[k]:
             copy.wait_recv()
         which, c = divmod(k, 2)
-        result = (filters_out, mixed_out)[which]
+        result = (mixed_out, filters_out)[which]
         at = pl.ds(c * CHUNK, CHUNK)
         turns.extend(
             send(landed.at[k, :, xmod(d)], result.at[x, :, :, at], at_x(d))
@@ -370,10 +364,10 @@
         )
         result[x, :, :, at] = landed[k, :, x]
 
-    for k in range(4):
+    def leave(k):
         which, c = divmod(k, 2)
         if c == 0:
-            combine(spec_g, (spec_p, spec_f)[which], z_ref, inner)
+            combine(spec_g, (spec_f, spec_p)[which], z_ref, inner)
         at, far = pl.ds(c * CHUNK, CHUNK), pl.ds(inner + c * CHUNK, CHUNK)
         values_z = z_ref[...]
         real = dot(values_z, ac_hi[:, at]) + dot(values_z, ac_lo[:, at])
@@ -383,15 +377,28 @@
         u_ref[spec_rows:, :] = imag.astype(BF)
         u = u_ref[...]
         out = (dot(of_hi[...], u) + dot(of_lo[...], u)).reshape(leaving.shape[1:])
-        if which == 1:
+        if which == 0:
             out = out + scale * gated_in[:, :, :, at].astype(jnp.float32)
         leaving[k] = out.astype(BF)
         gone.append(
             [send(leaving.at[k, zmod(d)], landed.at[k, z], at_z(d)) for d in range(1, ZS)]
         )
         landed[k, z] = leaving[k, z]
-        if k >= 2:
-            turn_x(k - 2)
+
+    leave(0)
+    pair_x(0)
+    leave(1)
+    for n, off in enumerate(offsets):
+        if n:
+            homes.append(send(back_bf.at[n], home_out.at[x], at_x(off)))
+    for copy in over_x[0]:
+        copy.wait_recv()
+    for piece in forward_pieces(pair_block(0), into, twist, across, z_ref, spec_p):
+        piece()
+    leave(2)
+    turn_x(0)
+    leave(3)
+    turn_x(1)
     turn_x(2)
     turn_x(3)
     for copy in homes + turns:
@@ -409,7 +416,7 @@
     spec_rows = cos.shape[0]
     split = (XS, ZS, width, inner)
     parts = inner // CHUNK
-    count = 132
+    count = 139
 
     def vmem(shape, dtype=BF):
         return pltpu.VMEM(shape, dtype)

time: 117 us -> 115 us (0.983)
  Pallas kernels: 113 us -> 111 us
    pallas_call x1, Pallas kernels: 113 us -> 111 us  [layer(): pl.pallas_call(layer_kernel, out_shape=[jax.ShapeDtypeStruct((XS, deep, i...]
where the time goes in v5:
time: 115 us
  Pallas kernels  111 us (97%)
  other arithmetic  3.79 us (3%)
    pallas_call x1, Pallas kernels, layer(): pl.pallas_call(layer_kernel, out_shape=[jax.ShapeDtypeStruct((XS, deep, i...  111 us
    convert_element_type x1, other arithmetic, shards(): grad_values = (wide(mixed) * wide(gate_in)).astype(BF)  2.65 us

profile of v5, /device:TPU:1, one launch (start us, length us, event | category | flops | bytes accessed | tf_op | source)
XLA Modules:
  0.0 115.1 jit_solution(9125718405526456791)
XLA Ops:
  0.6 0.0 copy-start.1
  0.6 0.0 copy-start.2
  0.7 0.0 copy-start.3
  0.7 110.6 %shard_map.183 = (bf16[4,128,512]{2,1,0:T(8,128)(2,1)}, bf16[4,8,16,512]{3,2,1,0:T(8,128)(2,1)}, bf16[4,8,16,512]{3,2,1,0:T(8,128)(2,1)}) custom-call(bf16[128,512]{1,0:T(8,128)(2,1)} %w_hbm.1, bf16[512,512]{1,0:T(8,128)(2,1)} %g_hbm.1, bf16[4,8,16,512]{3,2,1,0:T(8,128)(2,1)} %bitcast.15, bf16[4,8,16,512]{3,2,1,0:T(8,128)(2,1)} %bitcast.16, ...), custom_call_target="tpu_custom_call" | custom-call | flops 20000000000 | bytes 20000000 | tf_op jit(solution)/shard_map/pallas_call | solution.py:425
  111.3 0.0 copy-done.1
  111.3 0.0 copy-done.2
  111.3 0.0 copy-done.3
  111.3 0.0 copy-start
  111.4 2.6 %fusion.1 = (bf16[512,512]{1,0:T(8,128)(2,1)}, bf16[512,512]{1,0:T(8,128)(2,1)}, bf16[512,512]{1,0:T(8,128)(2,1)}) fusion(bf16[512,512]{1,0:T(8,128)(2,1)S(1)} %copy-done.1, bf16[4,8,16,512]{3,2,1,0:T(8,128)(2,1)} %get-tuple-element.7, bf16[512,512]{1,0:T(8,128)(2,1)S(1)} %copy-done.2, bf16[512,512]{1,0:T(8,128)(2,1)S(1)} %copy-done.3, ...), kind=kLoop, calls=%fused_computation.3 | loop fusion | flops 2883584 | bytes 4194304 | tf_op jit(solution)/shard_map/convert_element_type | solution.py:497
  114.0 0.0 copy-done
  114.0 1.1 bitcast_convert_fusion
Async XLA Ops:
  0.6 110.7 %copy-start.1 = (bf16[512,512]{1,0:T(8,128)(2,1)S(1)}, bf16[512,512]{1,0:T(8,128)(2,1)}, u32[]{:S(2)}) copy-start(bf16[512,512]{1,0:T(8,128)(2,1)} %param.18) | copy-start | bytes 1572868
  0.6 110.7 %copy-start.2 = (bf16[512,512]{1,0:T(8,128)(2,1)S(1)}, bf16[512,512]{1,0:T(8,128)(2,1)}, u32[]{:S(2)}) copy-start(bf16[512,512]{1,0:T(8,128)(2,1)} %param.20) | copy-start | bytes 1572868
  0.7 110.7 %copy-start.3 = (bf16[512,512]{1,0:T(8,128)(2,1)S(1)}, bf16[512,512]{1,0:T(8,128)(2,1)}, u32[]{:S(2)}) copy-start(bf16[512,512]{1,0:T(8,128)(2,1)} %param.21) | copy-start | bytes 1572868
  111.3 2.7 %copy-start = (bf16[4,8,16,512]{3,2,1,0:T(8,128)(2,1)S(1)}, bf16[4,8,16,512]{3,2,1,0:T(8,128)(2,1)}, u32[]{:S(2)}) copy-start(bf16[4,8,16,512]{3,2,1,0:T(8,128)(2,1)} %get-tuple-element.9) | copy-start | bytes 1572868

commit v6 on v5

--- a/solution.py
+++ b/solution.py
@@ -195,7 +195,6 @@
     far_top = send(g_ring.at[xmod(-1), top], g_ring.at[xmod(-1), top], at_x(1))
     left_low.wait_recv()
     far_low = send(g_ring.at[xmod(1), low], g_ring.at[xmod(1), low], at_x(-1))
-    gates = [send(gate_out_hbm.at[xmod(d)], near_gate.at[d], at_x(d)) for d in range(1, XS)]
     up.wait_recv()
     up = send(w_ring.at[zmod(-2)], w_ring.at[zmod(-2)], at_z(1))
     down.wait_recv()
@@ -218,11 +217,15 @@
         ]
         pair_in[i, :, x] = crossed[i, :, x]
 
-    pair_z(1, 0, XS)
     up.wait_recv()
     up = send(w_ring.at[zmod(-3), first], w_ring.at[zmod(-3), first], at_z(1))
     down.wait_recv()
     down = send(w_ring.at[zmod(3), second], w_ring.at[zmod(3), second], at_z(-1))
+    pair_z(1, 0, XS)
+    right_low.wait_recv()
+    shared.append(send(g_ring.at[xmod(-1)], g_other.at[1], sibling))
+    left_top.wait_recv()
+    shared.append(send(g_ring.at[xmod(1)], g_other.at[2], sibling))
     w_load.wait()
     g_load.wait()
     up.wait_recv()
@@ -237,16 +240,13 @@
     ]
     for d in range(YS):
         w_mine[d] = w_ring[rows_for(d, core)]
-    right_low.wait_recv()
-    shared.append(send(g_ring.at[xmod(-1)], g_other.at[1], sibling))
-    left_top.wait_recv()
-    shared.append(send(g_ring.at[xmod(1)], g_other.at[2], sibling))
     for copy in w_shared:
         copy.wait_recv()
 
     offsets = (0, -1, 1, 2)
     parts = []
     passed = []
+    gates = []
     deep = w_ring.shape[1]
     wide = (YS * deep, w_ring.shape[2])
 
@@ -260,6 +260,9 @@
         if n == 3:
             far_top.wait_recv()
             far_low.wait_recv()
+            gates.extend(
+                send(gate_out_hbm.at[xmod(d)], near_gate.at[d], at_x(d)) for d in range(1, XS)
+            )
             shared.append(send(g_ring.at[xmod(2)], g_other.at[3], sibling))
         shared[n].wait_recv()
 
@@ -316,23 +319,19 @@
 
     pass_on(0)
     pass_on(1)
-    pair_x(1)
     pass_on(2)
     total_up(0)
     pass_on(3)
     total_up(1)
+    total_up(2)
+    pair_x(1)
+    total_up(3)
+    pair_z(0, XS // 2, XS // 2)
     for copy in table_loads:
         copy.wait()
     for copy in over_x[1]:
         copy.wait_recv()
-    pieces = forward_pieces(pair_block(1), into, twist, across, z_ref, spec_f)
-    for piece in pieces[:2]:
-        piece()
-    total_up(2)
-    pieces[2]()
-    total_up(3)
-    pair_z(0, XS // 2, XS // 2)
-    for piece in pieces[3:]:
+    for piece in forward_pieces(pair_block(1), into, twist, across, z_ref, spec_f):
         piece()
     home_out[x] = back_bf[0]
     for copy in arrivals:

time: 115 us -> 111 us (0.965)
  Pallas kernels: 111 us -> 107 us
    pallas_call x1, Pallas kernels: 111 us -> 107 us  [layer(): pl.pallas_call(layer_kernel, out_shape=[jax.ShapeDtypeStruct((XS, deep, i...]
where the time goes in v6:
time: 111 us
  Pallas kernels  107 us (96%)
  other arithmetic  3.79 us (3%)
    pallas_call x1, Pallas kernels, layer(): pl.pallas_call(layer_kernel, out_shape=[jax.ShapeDtypeStruct((XS, deep, i...  107 us
    convert_element_type x1, other arithmetic, shards(): grad_values = (wide(mixed) * wide(gate_in)).astype(BF)  2.65 us

profile of v6, /device:TPU:1, one launch (start us, length us, event | category | flops | bytes accessed | tf_op | source)
XLA Modules:
  0.0 111.1 jit_solution(8438211927987346126)
XLA Ops:
  0.6 0.0 copy-start.1
  0.6 0.0 copy-start.2
  0.7 0.0 copy-start.3
  0.7 106.6 %shard_map.183 = (bf16[4,128,512]{2,1,0:T(8,128)(2,1)}, bf16[4,8,16,512]{3,2,1,0:T(8,128)(2,1)}, bf16[4,8,16,512]{3,2,1,0:T(8,128)(2,1)}) custom-call(bf16[128,512]{1,0:T(8,128)(2,1)} %w_hbm.1, bf16[512,512]{1,0:T(8,128)(2,1)} %g_hbm.1, bf16[4,8,16,512]{3,2,1,0:T(8,128)(2,1)} %bitcast.15, bf16[4,8,16,512]{3,2,1,0:T(8,128)(2,1)} %bitcast.16, ...), custom_call_target="tpu_custom_call" | custom-call | flops 20000000000 | bytes 20000000 | tf_op jit(solution)/shard_map/pallas_call | solution.py:424
  107.3 0.0 copy-done.1
  107.3 0.0 copy-done.2
  107.3 0.0 copy-done.3
  107.3 0.0 copy-start
  107.3 2.6 %fusion.1 = (bf16[512,512]{1,0:T(8,128)(2,1)}, bf16[512,512]{1,0:T(8,128)(2,1)}, bf16[512,512]{1,0:T(8,128)(2,1)}) fusion(bf16[512,512]{1,0:T(8,128)(2,1)S(1)} %copy-done.1, bf16[4,8,16,512]{3,2,1,0:T(8,128)(2,1)} %get-tuple-element.7, bf16[512,512]{1,0:T(8,128)(2,1)S(1)} %copy-done.2, bf16[512,512]{1,0:T(8,128)(2,1)S(1)} %copy-done.3, ...), kind=kLoop, calls=%fused_computation.3 | loop fusion | flops 2883584 | bytes 4194304 | tf_op jit(solution)/shard_map/convert_element_type | solution.py:496
  109.9 0.0 copy-done
  109.9 1.1 %bitcast_convert_fusion = f32[512,512]{1,0:T(8,128)} fusion(bf16[4,8,16,512]{3,2,1,0:T(8,128)(2,1)S(1)} %copy-done), kind=kLoop, calls=%fused_computation.6 | loop fusion | flops 262144 | bytes 1572864 | tf_op jit(solution)/shard_map/convert_element_type | solution.py:492
Async XLA Ops:
  0.6 106.6 %copy-start.1 = (bf16[512,512]{1,0:T(8,128)(2,1)S(1)}, bf16[512,512]{1,0:T(8,128)(2,1)}, u32[]{:S(2)}) copy-start(bf16[512,512]{1,0:T(8,128)(2,1)} %param.18) | copy-start | bytes 1572868
  0.6 106.6 %copy-start.2 = (bf16[512,512]{1,0:T(8,128)(2,1)S(1)}, bf16[512,512]{1,0:T(8,128)(2,1)}, u32[]{:S(2)}) copy-start(bf16[512,512]{1,0:T(8,128)(2,1)} %param.20) | copy-start | bytes 1572868
  0.7 106.6 %copy-start.3 = (bf16[512,512]{1,0:T(8,128)(2,1)S(1)}, bf16[512,512]{1,0:T(8,128)(2,1)}, u32[]{:S(2)}) copy-start(bf16[512,512]{1,0:T(8,128)(2,1)} %param.21) | copy-start | bytes 1572868
  107.3 2.7 %copy-start = (bf16[4,8,16,512]{3,2,1,0:T(8,128)(2,1)S(1)}, bf16[4,8,16,512]{3,2,1,0:T(8,128)(2,1)}, u32[]{:S(2)}) copy-start(bf16[4,8,16,512]{3,2,1,0:T(8,128)(2,1)} %get-tuple-element.9) | copy-start | bytes 1572868

commit v7 on v6

--- a/solution.py
+++ b/solution.py
@@ -105,7 +105,7 @@
     gate_in, values, filters, in_hi, in_lo, of_hi, of_lo, cos, sin, ac_hi, ac_lo,
     w_ring, w_mine, w_other, g_ring, g_other, own, hold, part, inbox, relay, final,
     near_gate, back_bf, gated, gated_in, stage, crossed, pair_in,
-    z_ref, u_ref, spec_g, spec_p, spec_f, leaving, landed,
+    z_ref, u_ref, spec_g, spec_p, spec_f, leaving, landed, way_pair, way_gated, way_out,
     send_sems, recv_sems, local_sems,
 ):
     s, h = lax.axis_index("seq"), lax.axis_index("ch")
@@ -202,15 +202,41 @@
     over_z = {}
     over_x = {}
 
+    def ring_z(source, target, halves, way, sides=(0, 1)):
+        hops = {}
+        for side in sides:
+            block = source(ZS // 2, halves[side])
+            hops[side] = send(block, way.at[side], at_z(2 - 4 * side))
+        there = [send(source(d, None), target(z, None), at_z(d)) for d in (3, -3, 2, -2, 1, -1)]
+
+        def forward():
+            for side in sides:
+                hops[side].wait_recv()
+                turn = 2 - 4 * side
+                there.append(send(way.at[side], target(zmod(-turn), halves[side]), at_z(turn)))
+
+        return there, forward
+
     def pair_z(i, start, size):
         at = pl.ds(start, size)
-        over_z.setdefault(i, []).extend(
-            send(stage.at[i, at, zmod(d)], crossed.at[i, z, at], at_z(d)) for d in range(1, ZS)
+        half = size // 2
+
+        def source(d, part):
+            return stage.at[i, at if part is None else part, zmod(d)]
+
+        def target(origin, part):
+            return crossed.at[i, origin, at if part is None else part]
+
+        there, forward = ring_z(
+            source, target, (pl.ds(start, half), pl.ds(start + half, half)),
+            way_pair.at[i, :, pl.ds(start // 2, half)],
         )
+        over_z.setdefault(i, []).append(there)
         crossed[i, z, at] = stage[i, at, z]
+        return forward
 
     def pair_x(i):
-        for copy in over_z[i]:
+        for copy in sum(over_z[i], []):
             copy.wait_recv()
         over_x[i] = [
             send(crossed.at[i, :, xmod(d)], pair_in.at[i, :, x], at_x(d)) for d in range(1, XS)
@@ -221,7 +247,7 @@
     up = send(w_ring.at[zmod(-3), first], w_ring.at[zmod(-3), first], at_z(1))
     down.wait_recv()
     down = send(w_ring.at[zmod(3), second], w_ring.at[zmod(3), second], at_z(-1))
-    pair_z(1, 0, XS)
+    filters_on = pair_z(1, 0, XS)
     right_low.wait_recv()
     shared.append(send(g_ring.at[xmod(-1)], g_other.at[1], sibling))
     left_top.wait_recv()
@@ -230,7 +256,7 @@
     g_load.wait()
     up.wait_recv()
     down.wait_recv()
-    pair_z(0, 0, XS // 2)
+    product_on = pair_z(0, 0, XS // 2)
 
     def rows_for(d, of_core):
         return lax.rem(y + d, YS) * 2 + of_core
@@ -242,6 +268,7 @@
         w_mine[d] = w_ring[rows_for(d, core)]
     for copy in w_shared:
         copy.wait_recv()
+    filters_on()
 
     offsets = (0, -1, 1, 2)
     parts = []
@@ -289,6 +316,7 @@
         parts.append([send(part.at[n, side], inbox.at[n, side], at_y(1 - 2 * side)) for side in range(2)])
 
     arrivals = []
+    gated_on = []
     homes = []
 
     def total_up(n):
@@ -305,8 +333,13 @@
         back = jnp.concatenate([upper, lower], 0)
         result = back * near_gate[d].astype(jnp.float32)
         gated[n] = result.astype(BF).reshape(gated.shape[1:])
-        for d in range(1, ZS):
-            arrivals.append(send(gated.at[n, zmod(d)], gated_in.at[z, xmod(off)], at_z(d)))
+        there, forward = ring_z(
+            lambda d, part: gated.at[n, zmod(d)],
+            lambda origin, part: gated_in.at[origin, xmod(off)],
+            (None, None), way_gated.at[n], (n % 2,),
+        )
+        arrivals.append(there)
+        gated_on.append(forward)
         gated_in[z, xmod(off)] = gated[n, z]
         back_bf[n] = back.astype(BF)
 
@@ -319,22 +352,31 @@
 
     pass_on(0)
     pass_on(1)
+    product_on()
     pass_on(2)
     total_up(0)
     pass_on(3)
     total_up(1)
+    gated_on[0]()
     total_up(2)
+    gated_on[1]()
     pair_x(1)
     total_up(3)
-    pair_z(0, XS // 2, XS // 2)
+    gated_on[2]()
+    product_on = pair_z(0, XS // 2, XS // 2)
     for copy in table_loads:
         copy.wait()
+    gated_on[3]()
     for copy in over_x[1]:
         copy.wait_recv()
-    for piece in forward_pieces(pair_block(1), into, twist, across, z_ref, spec_f):
+    pieces = forward_pieces(pair_block(1), into, twist, across, z_ref, spec_f)
+    for piece in pieces[:2]:
+        piece()
+    product_on()
+    for piece in pieces[2:]:
         piece()
     home_out[x] = back_bf[0]
-    for copy in arrivals:
+    for copy in sum(arrivals, []):
         copy.wait_recv()
     for piece in forward_pieces(
         lambda at: gated_in[:, :, :, at].reshape(rows, CHUNK), into, twist, across[:1], z_ref, spec_g
@@ -349,6 +391,7 @@
     scale = jnp.sum(jnp.where(pick, skip_ref[pl.ds(x, 1), :], 0.0), axis=1, keepdims=True)
     spec_rows = z_ref.shape[0]
     gone = []
+    gone_on = []
     turns = []
 
     def turn_x(k):
@@ -379,25 +422,41 @@
         if which == 0:
             out = out + scale * gated_in[:, :, :, at].astype(jnp.float32)
         leaving[k] = out.astype(BF)
-        gone.append(
-            [send(leaving.at[k, zmod(d)], landed.at[k, z], at_z(d)) for d in range(1, ZS)]
-        )
+
+
+        def source(d, part):
+            return leaving.at[k, zmod(d)] if part is None else leaving.at[k, zmod(d), part]
+
+        def target(origin, part):
+            return landed.at[k, origin] if part is None else landed.at[k, origin, part]
+
+        half = XS // 2
+        there, forward = ring_z(source, target, (pl.ds(0, half), pl.ds(half, half)), way_out.at[k])
+        gone.append(there)
+        gone_on.append(forward)
         landed[k, z] = leaving[k, z]
 
     leave(0)
     pair_x(0)
     leave(1)
+    gone_on[0]()
     for n, off in enumerate(offsets):
         if n:
             homes.append(send(back_bf.at[n], home_out.at[x], at_x(off)))
     for copy in over_x[0]:
         copy.wait_recv()
-    for piece in forward_pieces(pair_block(0), into, twist, across, z_ref, spec_p):
+    pieces = forward_pieces(pair_block(0), into, twist, across, z_ref, spec_p)
+    for piece in pieces[:2]:
+        piece()
+    gone_on[1]()
+    for piece in pieces[2:]:
         piece()
     leave(2)
     turn_x(0)
     leave(3)
+    gone_on[2]()
     turn_x(1)
+    gone_on[3]()
     turn_x(2)
     turn_x(3)
     for copy in homes + turns:
@@ -415,7 +474,7 @@
     spec_rows = cos.shape[0]
     split = (XS, ZS, width, inner)
     parts = inner // CHUNK
-    count = 139
+    count = 164
 
     def vmem(shape, dtype=BF):
         return pltpu.VMEM(shape, dtype)
@@ -462,6 +521,9 @@
             spec,
             vmem((2 * parts, ZS, XS, width, CHUNK)),
             vmem((2 * parts, ZS, XS, width, CHUNK)),
+            vmem((2, 2, XS // 2, width, inner)),
+            vmem((XS, 2, width, inner)),
+            vmem((2 * parts, 2, XS // 2, width, CHUNK)),
             pltpu.SemaphoreType.DMA((count,)),
             pltpu.SemaphoreType.DMA((count,)),
             pltpu.SemaphoreType.DMA((14,)),

time: 111 us -> 117 us (1.054)
  Pallas kernels: 107 us -> 112 us
    pallas_call x1, Pallas kernels: 107 us -> 112 us  [layer(): pl.pallas_call(layer_kernel, out_shape=[jax.ShapeDtypeStruct((XS, deep, i...]
where the time goes in v7:
time: 117 us
  Pallas kernels  112 us (96%)
  other arithmetic  3.79 us (3%)
    pallas_call x1, Pallas kernels, layer(): pl.pallas_call(layer_kernel, out_shape=[jax.ShapeDtypeStruct((XS, deep, i...  112 us
    convert_element_type x1, other arithmetic, shards(): grad_values = (wide(mixed) * wide(gate_in)).astype(BF)  2.65 us

profile of v7, /device:TPU:1, one launch (start us, length us, event | category | flops | bytes accessed | tf_op | source)
XLA Modules:
  0.0 116.9 jit_solution(4081778505462311824)
XLA Ops:
  0.6 0.0 copy-start.1
  0.6 0.0 copy-start.2
  0.7 0.0 copy-start.3
  0.7 112.4 %shard_map.183 = (bf16[4,128,512]{2,1,0:T(8,128)(2,1)}, bf16[4,8,16,512]{3,2,1,0:T(8,128)(2,1)}, bf16[4,8,16,512]{3,2,1,0:T(8,128)(2,1)}) custom-call(bf16[128,512]{1,0:T(8,128)(2,1)} %w_hbm.1, bf16[512,512]{1,0:T(8,128)(2,1)} %g_hbm.1, bf16[4,8,16,512]{3,2,1,0:T(8,128)(2,1)} %bitcast.15, bf16[4,8,16,512]{3,2,1,0:T(8,128)(2,1)} %bitcast.16, ...), custom_call_target="tpu_custom_call" | custom-call | flops 20000000000 | bytes 20000000 | tf_op jit(solution)/shard_map/pallas_call | solution.py:483
  113.0 0.0 copy-done.1
  113.0 0.0 copy-done.2
  113.0 0.0 copy-done.3
  113.1 0.0 copy-start
  113.1 2.6 %fusion.1 = (bf16[512,512]{1,0:T(8,128)(2,1)}, bf16[512,512]{1,0:T(8,128)(2,1)}, bf16[512,512]{1,0:T(8,128)(2,1)}) fusion(bf16[512,512]{1,0:T(8,128)(2,1)S(1)} %copy-done.1, bf16[4,8,16,512]{3,2,1,0:T(8,128)(2,1)} %get-tuple-element.7, bf16[512,512]{1,0:T(8,128)(2,1)S(1)} %copy-done.2, bf16[512,512]{1,0:T(8,128)(2,1)S(1)} %copy-done.3, ...), kind=kLoop, calls=%fused_computation.3 | loop fusion | flops 2883584 | bytes 4194304 | tf_op jit(solution)/shard_map/convert_element_type | solution.py:558
  115.7 0.0 copy-done
  115.7 1.1 bitcast_convert_fusion
Async XLA Ops:
  0.6 112.4 %copy-start.1 = (bf16[512,512]{1,0:T(8,128)(2,1)S(1)}, bf16[512,512]{1,0:T(8,128)(2,1)}, u32[]{:S(2)}) copy-start(bf16[512,512]{1,0:T(8,128)(2,1)} %param.18) | copy-start | bytes 1572868
  0.6 112.4 %copy-start.2 = (bf16[512,512]{1,0:T(8,128)(2,1)S(1)}, bf16[512,512]{1,0:T(8,128)(2,1)}, u32[]{:S(2)}) copy-start(bf16[512,512]{1,0:T(8,128)(2,1)} %param.20) | copy-start | bytes 1572868
  0.7 112.4 %copy-start.3 = (bf16[512,512]{1,0:T(8,128)(2,1)S(1)}, bf16[512,512]{1,0:T(8,128)(2,1)}, u32[]{:S(2)}) copy-start(bf16[512,512]{1,0:T(8,128)(2,1)} %param.21) | copy-start | bytes 1572868
  113.1 2.7 %copy-start = (bf16[4,8,16,512]{3,2,1,0:T(8,128)(2,1)S(1)}, bf16[4,8,16,512]{3,2,1,0:T(8,128)(2,1)}, u32[]{:S(2)}) copy-start(bf16[4,8,16,512]{3,2,1,0:T(8,128)(2,1)} %get-tuple-element.9) | copy-start | bytes 1572868

commit v8 on v6

--- a/solution.py
+++ b/solution.py
@@ -1,5 +1,3 @@
-import functools
-
 import jax
 import jax.numpy as jnp
 import ml_dtypes
@@ -11,6 +9,7 @@
 
 OUTER = 64
 CHUNK = 256
+STEP = 16
 
 
 def split_pair(table):
@@ -39,7 +38,11 @@
     out_of = np.concatenate([back_cos, back_sin], 1)
     turn = 2.0 * np.pi * (np.outer(k, b) % total) / total
     turn = np.repeat(turn, width, axis=0)
-    second = 2.0 * np.pi * (np.outer(b, b) % inner) / inner
+    quarter = inner // 4
+    c = np.arange(quarter)
+    second = 2.0 * np.pi * (np.outer(c, c) % quarter) / quarter
+    fourth = 2.0 * np.pi * np.outer(np.arange(4), c) / inner
+    fourth = np.concatenate([np.cos(fourth), np.sin(fourth)], 0)
     c, s = np.cos(second), np.sin(second)
     across = np.concatenate([np.concatenate([c, -s], 1), np.concatenate([s, c], 1)], 0)
     return (
@@ -48,6 +51,7 @@
         np.cos(turn).astype(np.float32),
         np.sin(turn).astype(np.float32),
         split_pair(across),
+        fourth.astype(np.float32),
     )
 
 
@@ -65,47 +69,101 @@
 BF = jnp.bfloat16
 
 
-def forward_pieces(block_of, into, twist, across, z_ref, out_ref):
-    rows = z_ref.shape[0]
-    inner = z_ref.shape[1] // 2
-
-    def spread(c):
+def four_way(parts):
+    (re0, im0), (re1, im1), (re2, im2), (re3, im3) = parts
+    sum_re, sum_im, dif_re, dif_im = re0 + re2, im0 + im2, re0 - re2, im0 - im2
+    odd_re, odd_im, gap_re, gap_im = re1 + re3, im1 + im3, re1 - re3, im1 - im3
+    return (
+        (sum_re + odd_re, sum_im + odd_im),
+        (dif_re + gap_im, dif_im - gap_re),
+        (sum_re - odd_re, sum_im - odd_im),
+        (dif_re - gap_im, dif_im + gap_re),
+    )
+
+
+def by_rows(rows, body):
+    @pl.loop(0, rows // STEP, unroll=3)
+    def _(i):
+        body(pl.ds(pl.multiple_of(i * STEP, STEP), STEP), i * STEP)
+
+
+def turn_fourth(part, fourth, r):
+    if r == 0:
+        return part
+    return turned(*part, fourth[pl.ds(r, 1), :], fourth[pl.ds(4 + r, 1), :])
+
+
+def forward(block_of, into, twist, fourth, across, y_ref, z_ref, out_ref):
+    rows = z_ref.shape[1]
+    quarter = z_ref.shape[2] // 2
+
+    for c in range(y_ref.shape[1] // CHUNK):
         at = pl.ds(c * CHUNK, CHUNK)
         block = block_of(at)
-        y = sum(dot(table[...], block) for table in into)
-        real, imag = turned(y[:rows], y[rows:], twist[0][:, at], twist[1][:, at])
-        z_ref[:, at] = real.astype(BF)
-        z_ref[:, pl.ds(inner + c * CHUNK, CHUNK)] = imag.astype(BF)
-
-    def columns(c):
-        at = pl.ds(c * CHUNK, CHUNK)
-        z = z_ref[...]
-        out_ref[:, at] = sum(dot(z, table[:, at]) for table in across)
-
-    pieces = [functools.partial(spread, c) for c in range(inner // CHUNK)]
-    pieces += [functools.partial(columns, c) for c in range(2 * inner // CHUNK)]
-    return pieces
-
-
-def combine(grad_ref, other_ref, z_ref, inner):
-    @pl.loop(0, inner // CHUNK)
-    def _(i):
-        at = pl.ds(pl.multiple_of(i * CHUNK, CHUNK), CHUNK)
-        far = pl.ds(pl.multiple_of(inner + i * CHUNK, CHUNK), CHUNK)
-        g_re, g_im = grad_ref[:, at], grad_ref[:, far]
-        o_re, o_im = other_ref[:, at], other_ref[:, far]
-        z_ref[:, at] = (g_re * o_re + g_im * o_im).astype(BF)
-        z_ref[:, far] = (g_re * o_im - g_im * o_re).astype(BF)
+        y_ref[:, at] = sum(dot(table[...], block) for table in into)
+
+    def body(at, start):
+        far = pl.ds(pl.multiple_of(rows + start, STEP), STEP)
+        parts = []
+        for q in range(4):
+            col = pl.ds(q * quarter, quarter)
+            parts.append(turned(y_ref[at, col], y_ref[far, col], twist[0][at, col], twist[1][at, col]))
+        for r, part in enumerate(four_way(parts)):
+            real, imag = turn_fourth(part, fourth, r)
+            z_ref[r, at, :quarter] = real.astype(BF)
+            z_ref[r, at, quarter:] = imag.astype(BF)
+
+    by_rows(rows, body)
+    columns(z_ref, across, out_ref)
+
+
+def columns(z_ref, across, out_ref):
+    for r in range(4):
+        z = z_ref[r]
+        out_ref[r] = sum(dot(z, table[...]) for table in across)
+
+
+def combine(grad_ref, other_ref, z_ref):
+    rows = z_ref.shape[1]
+    quarter = z_ref.shape[2] // 2
+
+    def body(at, _):
+        for r in range(4):
+            g_re, g_im = grad_ref[r, at, :quarter], grad_ref[r, at, quarter:]
+            o_re, o_im = other_ref[r, at, :quarter], other_ref[r, at, quarter:]
+            z_ref[r, at, :quarter] = (g_re * o_re + g_im * o_im).astype(BF)
+            z_ref[r, at, quarter:] = (g_re * o_im - g_im * o_re).astype(BF)
+
+    by_rows(rows, body)
+
+
+def unfold(spec_ref, twist, fourth, u_ref):
+    rows = spec_ref.shape[1]
+    quarter = spec_ref.shape[2] // 2
+
+    def body(at, start):
+        far = pl.ds(pl.multiple_of(rows + start, STEP), STEP)
+        parts = [
+            turn_fourth((spec_ref[r, at, :quarter], spec_ref[r, at, quarter:]), fourth, r)
+            for r in range(4)
+        ]
+        for q, part in enumerate(four_way(parts)):
+            col = pl.ds(q * quarter, quarter)
+            real, imag = turned(*part, twist[0][at, col], twist[1][at, col])
+            u_ref[at, col] = real.astype(BF)
+            u_ref[far, col] = imag.astype(BF)
+
+    by_rows(rows, body)
 
 
 def layer_kernel(
     w_hbm, g_hbm, gate_in_hbm, values_hbm, gate_out_hbm, filters_hbm, skip_ref,
-    in_hi_h, in_lo_h, of_hi_h, of_lo_h, cos_h, sin_h, ac_hi_h, ac_lo_h,
+    in_hi_h, in_lo_h, of_hi_h, of_lo_h, cos_h, sin_h, ac_hi_h, ac_lo_h, fourth_h,
     home_out, filters_out, mixed_out,
-    gate_in, values, filters, in_hi, in_lo, of_hi, of_lo, cos, sin, ac_hi, ac_lo,
+    gate_in, values, filters, in_hi, in_lo, of_hi, of_lo, cos, sin, ac_hi, ac_lo, fourth,
     w_ring, w_mine, w_other, g_ring, g_other, own, hold, part, inbox, relay, final,
     near_gate, back_bf, gated, gated_in, stage, crossed, pair_in,
-    z_ref, u_ref, spec_g, spec_p, spec_f, leaving, landed,
+    y_ref, z_ref, u_ref, spec_r, spec_g, spec_p, spec_f, leaving, landed,
     send_sems, recv_sems, local_sems,
 ):
     s, h = lax.axis_index("seq"), lax.axis_index("ch")
@@ -151,7 +209,7 @@
         load(src, dst)
         for src, dst in (
             (in_hi_h, in_hi), (in_lo_h, in_lo), (ac_hi_h, ac_hi), (ac_lo_h, ac_lo),
-            (cos_h, cos), (sin_h, sin), (of_hi_h, of_hi), (of_lo_h, of_lo),
+            (cos_h, cos), (sin_h, sin), (fourth_h, fourth), (of_hi_h, of_hi), (of_lo_h, of_lo),
         )
     ]
     pl.semaphore_wait(barrier, len(peers))
@@ -331,15 +389,14 @@
         copy.wait()
     for copy in over_x[1]:
         copy.wait_recv()
-    for piece in forward_pieces(pair_block(1), into, twist, across, z_ref, spec_f):
-        piece()
+    forward(pair_block(1), into, twist, fourth, across, y_ref, z_ref, spec_f)
     home_out[x] = back_bf[0]
     for copy in arrivals:
         copy.wait_recv()
-    for piece in forward_pieces(
-        lambda at: gated_in[:, :, :, at].reshape(rows, CHUNK), into, twist, across[:1], z_ref, spec_g
-    ):
-        piece()
+    forward(
+        lambda at: gated_in[:, :, :, at].reshape(rows, CHUNK),
+        into, twist, fourth, across, y_ref, z_ref, spec_g,
+    )
 
     width = gated_in.shape[2]
     lanes = skip_ref.shape[1]
@@ -347,7 +404,6 @@
         jnp.int32, (width, lanes), 0
     )
     scale = jnp.sum(jnp.where(pick, skip_ref[pl.ds(x, 1), :], 0.0), axis=1, keepdims=True)
-    spec_rows = z_ref.shape[0]
     gone = []
     turns = []
 
@@ -366,15 +422,11 @@
     def leave(k):
         which, c = divmod(k, 2)
         if c == 0:
-            combine(spec_g, (spec_f, spec_p)[which], z_ref, inner)
-        at, far = pl.ds(c * CHUNK, CHUNK), pl.ds(inner + c * CHUNK, CHUNK)
-        values_z = z_ref[...]
-        real = dot(values_z, ac_hi[:, at]) + dot(values_z, ac_lo[:, at])
-        imag = dot(values_z, ac_hi[:, far]) + dot(values_z, ac_lo[:, far])
-        real, imag = turned(real, imag, cos[:, at], sin[:, at])
-        u_ref[:spec_rows, :] = real.astype(BF)
-        u_ref[spec_rows:, :] = imag.astype(BF)
-        u = u_ref[...]
+            combine(spec_g, (spec_f, spec_p)[which], z_ref)
+            columns(z_ref, across, spec_r)
+            unfold(spec_r, twist, fourth, u_ref)
+        at = pl.ds(c * CHUNK, CHUNK)
+        u = u_ref[:, at]
         out = (dot(of_hi[...], u) + dot(of_lo[...], u)).reshape(leaving.shape[1:])
         if which == 0:
             out = out + scale * gated_in[:, :, :, at].astype(jnp.float32)
@@ -392,8 +444,7 @@
             homes.append(send(back_bf.at[n], home_out.at[x], at_x(off)))
     for copy in over_x[0]:
         copy.wait_recv()
-    for piece in forward_pieces(pair_block(0), into, twist, across, z_ref, spec_p):
-        piece()
+    forward(pair_block(0), into, twist, fourth, across, y_ref, z_ref, spec_p)
     leave(2)
     turn_x(0)
     leave(3)
@@ -410,8 +461,8 @@
     rows, inner = gate_in.shape
     deep, wide = out_weight.shape
     width = rows // (ZS * XS)
-    into, out_of, cos, sin, across = make_tables(ZS * XS, width, inner)
-    tables = (*into, *out_of, cos, sin, *across)
+    into, out_of, cos, sin, across, fourth = make_tables(ZS * XS, width, inner)
+    tables = (*into, *out_of, cos, sin, *across, fourth)
     spec_rows = cos.shape[0]
     split = (XS, ZS, width, inner)
     parts = inner // CHUNK
@@ -420,7 +471,7 @@
     def vmem(shape, dtype=BF):
         return pltpu.VMEM(shape, dtype)
 
-    spec = vmem((spec_rows, 2 * inner), jnp.float32)
+    spec = vmem((4, spec_rows, inner // 2), jnp.float32)
     return pl.pallas_call(
         layer_kernel,
         out_shape=[
@@ -455,8 +506,10 @@
             vmem((2,) + split),
             vmem((2, ZS, XS, width, inner)),
             vmem((2, ZS, XS, width, inner)),
-            vmem((spec_rows, 2 * inner)),
-            vmem((2 * spec_rows, CHUNK)),
+            vmem((2 * spec_rows, inner), jnp.float32),
+            vmem((4, spec_rows, inner // 2)),
+            vmem((2 * spec_rows, inner)),
+            spec,
             spec,
             spec,
             spec,
@@ -464,12 +517,12 @@
             vmem((2 * parts, ZS, XS, width, CHUNK)),
             pltpu.SemaphoreType.DMA((count,)),
             pltpu.SemaphoreType.DMA((count,)),
-            pltpu.SemaphoreType.DMA((14,)),
+            pltpu.SemaphoreType.DMA((15,)),
         ],
         compiler_params=pltpu.CompilerParams(
             collective_id=0, has_side_effects=True, vmem_limit_bytes=58 * 1024 * 1024
         ),
-        cost_estimate=pl.CostEstimate(flops=20 * 10**9, bytes_accessed=20 * 10**6, transcendentals=0),
+        cost_estimate=pl.CostEstimate(flops=10 * 10**9, bytes_accessed=20 * 10**6, transcendentals=0),
     )(
         out_weight,
         grad_out,

time: 111 us -> 108 us (0.973)
  Pallas kernels: 107 us -> 104 us
    pallas_call x1, Pallas kernels: 107 us -> 104 us  [layer(): pl.pallas_call(layer_kernel, out_shape=[jax.ShapeDtypeStruct((XS, deep, i...]
where the time goes in v8:
time: 108 us
  Pallas kernels  104 us (96%)
  other arithmetic  3.79 us (4%)
    pallas_call x1, Pallas kernels, layer(): pl.pallas_call(layer_kernel, out_shape=[jax.ShapeDtypeStruct((XS, deep, i...  104 us
    convert_element_type x1, other arithmetic, shards(): grad_values = (wide(mixed) * wide(gate_in)).astype(BF)  2.65 us

profile of v8, /device:TPU:1, one launch (start us, length us, event | category | flops | bytes accessed | tf_op | source)
XLA Modules:
  0.0 108.1 jit_solution(14304092437215964231)
XLA Ops:
  0.6 0.0 copy-start.1
  0.6 0.0 copy-start.2
  0.7 0.0 copy-start.3
  0.7 103.6 %shard_map.192 = (bf16[4,128,512]{2,1,0:T(8,128)(2,1)}, bf16[4,8,16,512]{3,2,1,0:T(8,128)(2,1)}, bf16[4,8,16,512]{3,2,1,0:T(8,128)(2,1)}) custom-call(bf16[128,512]{1,0:T(8,128)(2,1)} %w_hbm.1, bf16[512,512]{1,0:T(8,128)(2,1)} %g_hbm.1, bf16[4,8,16,512]{3,2,1,0:T(8,128)(2,1)} %bitcast.15, bf16[4,8,16,512]{3,2,1,0:T(8,128)(2,1)} %bitcast.16, ...), custom_call_target="tpu_custom_call" | custom-call | flops 10000000000 | bytes 20000000 | tf_op jit(solution)/shard_map/pallas_call | solution.py:475
  104.2 0.0 copy-done.1
  104.2 0.0 copy-done.2
  104.3 0.0 copy-done.3
  104.3 0.0 copy-start
  104.3 2.6 %fusion.1 = (bf16[512,512]{1,0:T(8,128)(2,1)}, bf16[512,512]{1,0:T(8,128)(2,1)}, bf16[512,512]{1,0:T(8,128)(2,1)}) fusion(bf16[512,512]{1,0:T(8,128)(2,1)S(1)} %copy-done.1, bf16[4,8,16,512]{3,2,1,0:T(8,128)(2,1)} %get-tuple-element.7, bf16[512,512]{1,0:T(8,128)(2,1)S(1)} %copy-done.2, bf16[512,512]{1,0:T(8,128)(2,1)S(1)} %copy-done.3, ...), kind=kLoop, calls=%fused_computation.3 | loop fusion | flops 2883584 | bytes 4194304 | tf_op jit(solution)/shard_map/convert_element_type | solution.py:549
  106.9 0.0 copy-done
  106.9 1.1 %bitcast_convert_fusion = f32[512,512]{1,0:T(8,128)} fusion(bf16[4,8,16,512]{3,2,1,0:T(8,128)(2,1)S(1)} %copy-done), kind=kLoop, calls=%fused_computation.6 | loop fusion | flops 262144 | bytes 1572864 | tf_op jit(solution)/shard_map/convert_element_type | solution.py:545
Async XLA Ops:
  0.6 103.6 %copy-start.1 = (bf16[512,512]{1,0:T(8,128)(2,1)S(1)}, bf16[512,512]{1,0:T(8,128)(2,1)}, u32[]{:S(2)}) copy-start(bf16[512,512]{1,0:T(8,128)(2,1)} %param.19) | copy-start | bytes 1572868
  0.6 103.6 %copy-start.2 = (bf16[512,512]{1,0:T(8,128)(2,1)S(1)}, bf16[512,512]{1,0:T(8,128)(2,1)}, u32[]{:S(2)}) copy-start(bf16[512,512]{1,0:T(8,128)(2,1)} %param.21) | copy-start | bytes 1572868
  0.7 103.6 %copy-start.3 = (bf16[512,512]{1,0:T(8,128)(2,1)S(1)}, bf16[512,512]{1,0:T(8,128)(2,1)}, u32[]{:S(2)}) copy-start(bf16[512,512]{1,0:T(8,128)(2,1)} %param.22) | copy-start | bytes 1572868
  104.3 2.7 %copy-start = (bf16[4,8,16,512]{3,2,1,0:T(8,128)(2,1)S(1)}, bf16[4,8,16,512]{3,2,1,0:T(8,128)(2,1)}, u32[]{:S(2)}) copy-start(bf16[4,8,16,512]{3,2,1,0:T(8,128)(2,1)} %get-tuple-element.9) | copy-start | bytes 1572868

commit v9 on v8

--- a/solution.py
+++ b/solution.py
@@ -226,6 +226,13 @@
         copies.append(copy)
         return copy
 
+    waited = [0]
+
+    def flush(count):
+        for copy in copies[waited[0] : count]:
+            copy.wait_send()
+        waited[0] = count
+
     half_w = w_ring.shape[1] // 2
     half_g = g_ring.shape[1] // 2
     first, second = pl.ds(0, half_w), pl.ds(half_w, half_w)
@@ -350,10 +357,9 @@
     homes = []
 
     def total_up(n):
-        off = offsets[n]
         for copy in passed[2 * n : 2 * n + 2]:
             copy.wait_recv()
-        d = -off % XS
+        d = -offsets[n] % XS
         if d:
             gates[d - 1].wait_recv()
         else:
@@ -363,9 +369,11 @@
         back = jnp.concatenate([upper, lower], 0)
         result = back * near_gate[d].astype(jnp.float32)
         gated[n] = result.astype(BF).reshape(gated.shape[1:])
-        for d in range(1, ZS):
-            arrivals.append(send(gated.at[n, zmod(d)], gated_in.at[z, xmod(off)], at_z(d)))
-        gated_in[z, xmod(off)] = gated[n, z]
+        gated_in[z, n] = gated[n, z]
+        if n % 2:
+            both = pl.ds(n - 1, 2)
+            for d in range(1, ZS):
+                arrivals.append(send(gated.at[both, zmod(d)], gated_in.at[z, both], at_z(d)))
         back_bf[n] = back.astype(BF)
 
     inner = g_ring.shape[2]
@@ -375,6 +383,7 @@
     def pair_block(i):
         return lambda at: pair_in[i, :, :, :, at].reshape(rows, CHUNK)
 
+    early = len(copies)
     pass_on(0)
     pass_on(1)
     pass_on(2)
@@ -390,11 +399,20 @@
     for copy in over_x[1]:
         copy.wait_recv()
     forward(pair_block(1), into, twist, fourth, across, y_ref, z_ref, spec_f)
-    home_out[x] = back_bf[0]
+    stays = [load(back_bf.at[0], home_out.at[x])]
+    flush(early)
+
+    def gated_block(at):
+        blocks = []
+        for i in range(XS):
+            e = lax.rem(i - x + XS, XS)
+            blocks.append(gated_in[:, 2 * e - e // 2 - 4 * (e // 3), :, at])
+        return jnp.stack(blocks, 1).reshape(rows, CHUNK)
+
     for copy in arrivals:
         copy.wait_recv()
     forward(
-        lambda at: gated_in[:, :, :, at].reshape(rows, CHUNK),
+        gated_block,
         into, twist, fourth, across, y_ref, z_ref, spec_g,
     )
 
@@ -408,53 +426,63 @@
     turns = []
 
     def turn_x(k):
+        which, at = groups[k]
+        result = (mixed_out, filters_out)[which]
         for copy in gone[k]:
             copy.wait_recv()
-        which, c = divmod(k, 2)
-        result = (mixed_out, filters_out)[which]
-        at = pl.ds(c * CHUNK, CHUNK)
         turns.extend(
-            send(landed.at[k, :, xmod(d)], result.at[x, :, :, at], at_x(d))
+            send(landed.at[which, :, xmod(d), :, at], result.at[x, :, :, at], at_x(d))
             for d in range(1, XS)
         )
-        result[x, :, :, at] = landed[k, :, x]
-
-    def leave(k):
-        which, c = divmod(k, 2)
-        if c == 0:
+        stays.append(load(landed.at[which, :, x, :, at], result.at[x, :, :, at]))
+
+    groups = []
+
+    def leave(which, start, size):
+        if start == 0:
             combine(spec_g, (spec_f, spec_p)[which], z_ref)
             columns(z_ref, across, spec_r)
             unfold(spec_r, twist, fourth, u_ref)
-        at = pl.ds(c * CHUNK, CHUNK)
-        u = u_ref[:, at]
-        out = (dot(of_hi[...], u) + dot(of_lo[...], u)).reshape(leaving.shape[1:])
-        if which == 0:
-            out = out + scale * gated_in[:, :, :, at].astype(jnp.float32)
-        leaving[k] = out.astype(BF)
+        for c in range(start, start + size, CHUNK):
+            at = pl.ds(c, CHUNK)
+            u = u_ref[:, at]
+            out = dot(of_hi[...], u) + dot(of_lo[...], u)
+            if which == 0:
+                out = out.reshape(ZS * XS, width, CHUNK)
+                out = out + scale * gated_block(at).reshape(out.shape).astype(jnp.float32)
+            leaving[which, :, :, :, at] = out.astype(BF).reshape(ZS, XS, width, CHUNK)
+        at = pl.ds(start, size)
+        groups.append((which, at))
         gone.append(
-            [send(leaving.at[k, zmod(d)], landed.at[k, z], at_z(d)) for d in range(1, ZS)]
+            [
+                send(leaving.at[which, zmod(d), :, :, at], landed.at[which, z, :, :, at], at_z(d))
+                for d in range(1, ZS)
+            ]
         )
-        landed[k, z] = leaving[k, z]
-
-    leave(0)
+        landed[which, z, :, :, at] = leaving[which, z, :, :, at]
+
+    leave(0, 0, inner)
     pair_x(0)
-    leave(1)
     for n, off in enumerate(offsets):
         if n:
             homes.append(send(back_bf.at[n], home_out.at[x], at_x(off)))
     for copy in over_x[0]:
         copy.wait_recv()
     forward(pair_block(0), into, twist, fourth, across, y_ref, z_ref, spec_p)
-    leave(2)
+    middle = len(copies)
+    leave(1, 0, CHUNK)
+    leave(1, CHUNK, CHUNK)
     turn_x(0)
-    leave(3)
+    flush(middle)
     turn_x(1)
     turn_x(2)
-    turn_x(3)
+    for copy in stays:
+        copy.wait()
     for copy in homes + turns:
         copy.wait_recv()
-    for copy in copies:
-        copy.wait_send()
+    flush(len(copies))
+    assert len(copies) == send_sems.shape[0]
+    assert len(loads) == local_sems.shape[0]
 
 
 def layer(grad_out, out_weight, gate_in, gate_out, values, filters, skip_scale):
@@ -465,8 +493,7 @@
     tables = (*into, *out_of, cos, sin, *across, fourth)
     spec_rows = cos.shape[0]
     split = (XS, ZS, width, inner)
-    parts = inner // CHUNK
-    count = 139
+    count = 115
 
     def vmem(shape, dtype=BF):
         return pltpu.VMEM(shape, dtype)
@@ -482,7 +509,7 @@
         in_specs=[pl.BlockSpec(memory_space=pl.ANY)] * 6
         + [VMEM]
         + [pl.BlockSpec(memory_space=pl.ANY)] * len(tables),
-        out_specs=[VMEM] * 3,
+        out_specs=[pl.BlockSpec(memory_space=pl.ANY)] * 3,
         scratch_shapes=[
             vmem(split),
             vmem(split),
@@ -513,11 +540,11 @@
             spec,
             spec,
             spec,
-            vmem((2 * parts, ZS, XS, width, CHUNK)),
-            vmem((2 * parts, ZS, XS, width, CHUNK)),
+            vmem((2, ZS, XS, width, inner)),
+            vmem((2, ZS, XS, width, inner)),
             pltpu.SemaphoreType.DMA((count,)),
             pltpu.SemaphoreType.DMA((count,)),
-            pltpu.SemaphoreType.DMA((15,)),
+            pltpu.SemaphoreType.DMA((19,)),
         ],
         compiler_params=pltpu.CompilerParams(
             collective_id=0, has_side_effects=True, vmem_limit_bytes=58 * 1024 * 1024

time: 108 us -> 107 us (level)
  no operation moved by 1% of the time
where the time goes in v9:
time: 107 us
  Pallas kernels  103 us (96%)
  other arithmetic  3.79 us (4%)
    pallas_call x1, Pallas kernels, layer(): pl.pallas_call(layer_kernel, out_shape=[jax.ShapeDtypeStruct((XS, deep, i...  103 us
    convert_element_type x1, other arithmetic, shards(): grad_values = (wide(mixed) * wide(gate_in)).astype(BF)  2.65 us

profile of v9, /device:TPU:1, one launch (start us, length us, event | category | flops | bytes accessed | tf_op | source)
XLA Modules:
  0.0 107.1 jit_solution(2170468645852376760)
XLA Ops:
  0.6 0.0 copy-start.1
  0.6 0.0 copy-start.2
  0.7 0.0 copy-start.3
  0.7 102.6 %shard_map.192 = (bf16[4,128,512]{2,1,0:T(8,128)(2,1)}, bf16[4,8,16,512]{3,2,1,0:T(8,128)(2,1)}, bf16[4,8,16,512]{3,2,1,0:T(8,128)(2,1)}) custom-call(bf16[128,512]{1,0:T(8,128)(2,1)} %w_hbm.1, bf16[512,512]{1,0:T(8,128)(2,1)} %g_hbm.1, bf16[4,8,16,512]{3,2,1,0:T(8,128)(2,1)} %bitcast.15, bf16[4,8,16,512]{3,2,1,0:T(8,128)(2,1)} %bitcast.16, ...), custom_call_target="tpu_custom_call" | custom-call | flops 10000000000 | bytes 20000000 | tf_op jit(solution)/shard_map/pallas_call | solution.py:502
  103.3 0.0 copy-done.1
  103.3 0.0 copy-done.2
  103.3 0.0 copy-done.3
  103.3 0.0 copy-start
  103.3 2.6 %fusion.1 = (bf16[512,512]{1,0:T(8,128)(2,1)}, bf16[512,512]{1,0:T(8,128)(2,1)}, bf16[512,512]{1,0:T(8,128)(2,1)}) fusion(bf16[512,512]{1,0:T(8,128)(2,1)S(1)} %copy-done.1, bf16[4,8,16,512]{3,2,1,0:T(8,128)(2,1)} %get-tuple-element.7, bf16[512,512]{1,0:T(8,128)(2,1)S(1)} %copy-done.2, bf16[512,512]{1,0:T(8,128)(2,1)S(1)} %copy-done.3, ...), kind=kLoop, calls=%fused_computation.3 | loop fusion | flops 2883584 | bytes 4194304 | tf_op jit(solution)/shard_map/convert_element_type | solution.py:576
  106.0 0.0 copy-done
  106.0 1.1 %bitcast_convert_fusion = f32[512,512]{1,0:T(8,128)} fusion(bf16[4,8,16,512]{3,2,1,0:T(8,128)(2,1)S(1)} %copy-done), kind=kLoop, calls=%fused_computation.6 | loop fusion | flops 262144 | bytes 1572864 | tf_op jit(solution)/shard_map/convert_element_type | solution.py:572
Async XLA Ops:
  0.6 102.7 %copy-start.1 = (bf16[512,512]{1,0:T(8,128)(2,1)S(1)}, bf16[512,512]{1,0:T(8,128)(2,1)}, u32[]{:S(2)}) copy-start(bf16[512,512]{1,0:T(8,128)(2,1)} %param.19) | copy-start | bytes 1572868
  0.6 102.7 %copy-start.2 = (bf16[512,512]{1,0:T(8,128)(2,1)S(1)}, bf16[512,512]{1,0:T(8,128)(2,1)}, u32[]{:S(2)}) copy-start(bf16[512,512]{1,0:T(8,128)(2,1)} %param.21) | copy-start | bytes 1572868
  0.7 102.7 %copy-start.3 = (bf16[512,512]{1,0:T(8,128)(2,1)S(1)}, bf16[512,512]{1,0:T(8,128)(2,1)}, u32[]{:S(2)}) copy-start(bf16[512,512]{1,0:T(8,128)(2,1)} %param.22) | copy-start | bytes 1572868
  103.3 2.7 %copy-start = (bf16[4,8,16,512]{3,2,1,0:T(8,128)(2,1)S(1)}, bf16[4,8,16,512]{3,2,1,0:T(8,128)(2,1)}, u32[]{:S(2)}) copy-start(bf16[4,8,16,512]{3,2,1,0:T(8,128)(2,1)} %get-tuple-element.9) | copy-start | bytes 1572868

commit v10 on v9

--- a/solution.py
+++ b/solution.py
@@ -238,13 +238,18 @@
     first, second = pl.ds(0, half_w), pl.ds(half_w, half_w)
     top, low = pl.ds(0, half_g), pl.ds(half_g, half_g)
 
-    up = send(w_hbm, w_ring.at[z], at_z(1))
-    down = send(w_hbm, w_ring.at[z], at_z(-1))
+    halves = (first, second)
+    ring = {}
+    for side in (0, 1):
+        for way in (1, -1):
+            rows = halves[side if way == 1 else 1 - side]
+            ring[way, side] = send(w_hbm.at[rows], w_ring.at[z, rows], at_z(way))
     right_top = send(g_hbm.at[top], g_ring.at[x, top], at_x(1))
     left_low = send(g_hbm.at[low], g_ring.at[x, low], at_x(-1))
     right_low = send(g_hbm.at[low], g_ring.at[x, low], at_x(1))
     left_top = send(g_hbm.at[top], g_ring.at[x, top], at_x(-1))
     shared = [send(g_hbm, g_other.at[0], sibling)]
+    w_load.wait()
     for copy in pair_loads:
         copy.wait()
     for i in range(XS):
@@ -252,18 +257,30 @@
         stage[0, i] = product.astype(BF)
         stage[1, i] = filters[i].astype(BF)
 
-    up.wait_recv()
-    up = send(w_ring.at[zmod(-1)], w_ring.at[zmod(-1)], at_z(1))
-    down.wait_recv()
-    down = send(w_ring.at[zmod(1)], w_ring.at[zmod(1)], at_z(-1))
+    w_shared = []
+
+    def step(r):
+        for side in (0, 1):
+            for way in (1, -1):
+                if r == ZS // 2 and side:
+                    continue
+                ring[way, side].wait_recv()
+                if r == ZS // 2 or (r == ZS // 2 - 1 and side):
+                    continue
+                block = w_ring.at[zmod(-r * way), halves[side if way == 1 else 1 - side]]
+                ring[way, side] = send(block, block, at_z(way))
+        even, odd = (0, 2, -2, 4)[r - 1], (1, -1, 3, -3)[r - 1]
+        e = lax.rem(1 - core + z, 2)
+        row = zmod(even + e * (odd - even))
+        w_shared.append(send(w_ring.at[row], w_other.at[lax.rem(row // 2 - y + YS, YS)], sibling))
+
+    step(1)
     right_top.wait_recv()
     far_top = send(g_ring.at[xmod(-1), top], g_ring.at[xmod(-1), top], at_x(1))
     left_low.wait_recv()
     far_low = send(g_ring.at[xmod(1), low], g_ring.at[xmod(1), low], at_x(-1))
-    up.wait_recv()
-    up = send(w_ring.at[zmod(-2)], w_ring.at[zmod(-2)], at_z(1))
-    down.wait_recv()
-    down = send(w_ring.at[zmod(2)], w_ring.at[zmod(2)], at_z(-1))
+    step(2)
+    step(3)
     over_z = {}
     over_x = {}
 
@@ -282,27 +299,18 @@
         ]
         pair_in[i, :, x] = crossed[i, :, x]
 
-    up.wait_recv()
-    up = send(w_ring.at[zmod(-3), first], w_ring.at[zmod(-3), first], at_z(1))
-    down.wait_recv()
-    down = send(w_ring.at[zmod(3), second], w_ring.at[zmod(3), second], at_z(-1))
     pair_z(1, 0, XS)
     right_low.wait_recv()
     shared.append(send(g_ring.at[xmod(-1)], g_other.at[1], sibling))
     left_top.wait_recv()
     shared.append(send(g_ring.at[xmod(1)], g_other.at[2], sibling))
-    w_load.wait()
     g_load.wait()
-    up.wait_recv()
-    down.wait_recv()
-    pair_z(0, 0, XS // 2)
+    step(4)
+    pair_z(0, 0, XS)
 
     def rows_for(d, of_core):
         return lax.rem(y + d, YS) * 2 + of_core
 
-    w_shared = [
-        send(w_ring.at[rows_for(d, 1 - core)], w_other.at[d], sibling) for d in range(YS)
-    ]
     for d in range(YS):
         w_mine[d] = w_ring[rows_for(d, core)]
     for copy in w_shared:
@@ -370,10 +378,10 @@
         result = back * near_gate[d].astype(jnp.float32)
         gated[n] = result.astype(BF).reshape(gated.shape[1:])
         gated_in[z, n] = gated[n, z]
-        if n % 2:
-            both = pl.ds(n - 1, 2)
+        if n:
+            some = pl.ds(0, 2) if n == 1 else pl.ds(n, 1)
             for d in range(1, ZS):
-                arrivals.append(send(gated.at[both, zmod(d)], gated_in.at[z, both], at_z(d)))
+                arrivals.append(send(gated.at[some, zmod(d)], gated_in.at[z, some], at_z(d)))
         back_bf[n] = back.astype(BF)
 
     inner = g_ring.shape[2]
@@ -393,7 +401,7 @@
     total_up(2)
     pair_x(1)
     total_up(3)
-    pair_z(0, XS // 2, XS // 2)
+    pair_x(0)
     for copy in table_loads:
         copy.wait()
     for copy in over_x[1]:
@@ -462,13 +470,12 @@
         landed[which, z, :, :, at] = leaving[which, z, :, :, at]
 
     leave(0, 0, inner)
-    pair_x(0)
+    for copy in over_x[0]:
+        copy.wait_recv()
+    forward(pair_block(0), into, twist, fourth, across, y_ref, z_ref, spec_p)
     for n, off in enumerate(offsets):
         if n:
             homes.append(send(back_bf.at[n], home_out.at[x], at_x(off)))
-    for copy in over_x[0]:
-        copy.wait_recv()
-    forward(pair_block(0), into, twist, fourth, across, y_ref, z_ref, spec_p)
     middle = len(copies)
     leave(1, 0, CHUNK)
     leave(1, CHUNK, CHUNK)
@@ -493,7 +500,7 @@
     tables = (*into, *out_of, cos, sin, *across, fourth)
     spec_rows = cos.shape[0]
     split = (XS, ZS, width, inner)
-    count = 115
+    count = 121
 
     def vmem(shape, dtype=BF):
         return pltpu.VMEM(shape, dtype)

time: 107 us -> 106 us (level); the launches traced: 107 us -> 105 us
  Pallas kernels: 103 us -> 100 us
    pallas_call x1, Pallas kernels: 103 us -> 100 us  [layer(): pl.pallas_call(layer_kernel, out_shape=[jax.ShapeDtypeStruct((XS, deep, i...]
where the time goes in v10:
time: 106 us; the launch traced here: 105 us
  Pallas kernels  100 us (94%)
  other arithmetic  3.79 us (4%)
    pallas_call x1, Pallas kernels, layer(): pl.pallas_call(layer_kernel, out_shape=[jax.ShapeDtypeStruct((XS, deep, i...  100 us
    convert_element_type x1, other arithmetic, shards(): grad_values = (wide(mixed) * wide(gate_in)).astype(BF)  2.65 us

profile of v10, /device:TPU:1, one launch (start us, length us, event | category | flops | bytes accessed | tf_op | source)
XLA Modules:
  0.0 104.7 jit_solution(14281262943940937170)
XLA Ops:
  0.6 0.0 copy-start.1
  0.6 0.0 copy-start.2
  0.7 0.0 copy-start.3
  0.7 100.2 %shard_map.192 = (bf16[4,128,512]{2,1,0:T(8,128)(2,1)}, bf16[4,8,16,512]{3,2,1,0:T(8,128)(2,1)}, bf16[4,8,16,512]{3,2,1,0:T(8,128)(2,1)}) custom-call(bf16[128,512]{1,0:T(8,128)(2,1)} %w_hbm.1, bf16[512,512]{1,0:T(8,128)(2,1)} %g_hbm.1, bf16[4,8,16,512]{3,2,1,0:T(8,128)(2,1)} %bitcast.15, bf16[4,8,16,512]{3,2,1,0:T(8,128)(2,1)} %bitcast.16, ...), custom_call_target="tpu_custom_call" | custom-call | flops 10000000000 | bytes 20000000 | tf_op jit(solution)/shard_map/pallas_call | solution.py:509
  100.9 0.0 copy-done.1
  100.9 0.0 copy-done.2
  100.9 0.0 copy-done.3
  100.9 0.0 copy-start
  100.9 2.6 %fusion.1 = (bf16[512,512]{1,0:T(8,128)(2,1)}, bf16[512,512]{1,0:T(8,128)(2,1)}, bf16[512,512]{1,0:T(8,128)(2,1)}) fusion(bf16[512,512]{1,0:T(8,128)(2,1)S(1)} %copy-done.1, bf16[4,8,16,512]{3,2,1,0:T(8,128)(2,1)} %get-tuple-element.7, bf16[512,512]{1,0:T(8,128)(2,1)S(1)} %copy-done.2, bf16[512,512]{1,0:T(8,128)(2,1)S(1)} %copy-done.3, ...), kind=kLoop, calls=%fused_computation.3 | loop fusion | flops 2883584 | bytes 4194304 | tf_op jit(solution)/shard_map/convert_element_type | solution.py:583
  103.5 0.0 copy-done
  103.5 1.1 %bitcast_convert_fusion = f32[512,512]{1,0:T(8,128)} fusion(bf16[4,8,16,512]{3,2,1,0:T(8,128)(2,1)S(1)} %copy-done), kind=kLoop, calls=%fused_computation.6 | loop fusion | flops 262144 | bytes 1572864 | tf_op jit(solution)/shard_map/convert_element_type | solution.py:579
Async XLA Ops:
  0.6 100.2 %copy-start.1 = (bf16[512,512]{1,0:T(8,128)(2,1)S(1)}, bf16[512,512]{1,0:T(8,128)(2,1)}, u32[]{:S(2)}) copy-start(bf16[512,512]{1,0:T(8,128)(2,1)} %param.19) | copy-start | bytes 1572868
  0.6 100.2 %copy-start.2 = (bf16[512,512]{1,0:T(8,128)(2,1)S(1)}, bf16[512,512]{1,0:T(8,128)(2,1)}, u32[]{:S(2)}) copy-start(bf16[512,512]{1,0:T(8,128)(2,1)} %param.21) | copy-start | bytes 1572868
  0.7 100.2 %copy-start.3 = (bf16[512,512]{1,0:T(8,128)(2,1)S(1)}, bf16[512,512]{1,0:T(8,128)(2,1)}, u32[]{:S(2)}) copy-start(bf16[512,512]{1,0:T(8,128)(2,1)} %param.22) | copy-start | bytes 1572868
  100.9 2.7 %copy-start = (bf16[4,8,16,512]{3,2,1,0:T(8,128)(2,1)S(1)}, bf16[4,8,16,512]{3,2,1,0:T(8,128)(2,1)}, u32[]{:S(2)}) copy-start(bf16[4,8,16,512]{3,2,1,0:T(8,128)(2,1)} %get-tuple-element.9) | copy-start | bytes 1572868

commit v11 on v10

--- a/solution.py
+++ b/solution.py
@@ -163,7 +163,7 @@
     gate_in, values, filters, in_hi, in_lo, of_hi, of_lo, cos, sin, ac_hi, ac_lo, fourth,
     w_ring, w_mine, w_other, g_ring, g_other, own, hold, part, inbox, relay, final,
     near_gate, back_bf, gated, gated_in, stage, crossed, pair_in,
-    y_ref, z_ref, u_ref, spec_r, spec_g, spec_p, spec_f, leaving, landed,
+    y_ref, z_ref, u_ref, spec_r, spec_g, spec_p, spec_f, leaving, landed, held,
     send_sems, recv_sems, local_sems,
 ):
     s, h = lax.axis_index("seq"), lax.axis_index("ch")
@@ -284,12 +284,32 @@
     over_z = {}
     over_x = {}
 
-    def pair_z(i, start, size):
-        at = pl.ds(start, size)
-        over_z.setdefault(i, []).extend(
-            send(stage.at[i, at, zmod(d)], crossed.at[i, z, at], at_z(d)) for d in range(1, ZS)
+    def ring_z(source, target, held):
+        turns = (2, -2)
+        hops = [send(source(4, n), held(n), at_z(turn)) for n, turn in enumerate(turns)]
+        there = [send(source(d, None), target(z, None), at_z(d)) for d in (3, -3, 2, -2, 1, -1)]
+
+        def forward_on():
+            for n, turn in enumerate(turns):
+                hops[n].wait_recv()
+                there.append(send(held(n), target(zmod(-turn), n), at_z(turn)))
+
+        return there, forward_on
+
+    half = XS // 2
+
+    def half_at(n):
+        return pl.ds(0, XS) if n is None else pl.ds(n * half, half)
+
+    def pair_z(i):
+        there, forward_on = ring_z(
+            lambda d, n: stage.at[i, half_at(n), zmod(d)],
+            lambda origin, n: crossed.at[i, origin, half_at(n)],
+            lambda n: held.at[i, n],
         )
-        crossed[i, z, at] = stage[i, at, z]
+        over_z[i] = there
+        crossed[i, z] = stage[i, :, z]
+        return forward_on
 
     def pair_x(i):
         for copy in over_z[i]:
@@ -299,14 +319,14 @@
         ]
         pair_in[i, :, x] = crossed[i, :, x]
 
-    pair_z(1, 0, XS)
+    filters_on = pair_z(1)
     right_low.wait_recv()
     shared.append(send(g_ring.at[xmod(-1)], g_other.at[1], sibling))
     left_top.wait_recv()
     shared.append(send(g_ring.at[xmod(1)], g_other.at[2], sibling))
     g_load.wait()
     step(4)
-    pair_z(0, 0, XS)
+    product_on = pair_z(0)
 
     def rows_for(d, of_core):
         return lax.rem(y + d, YS) * 2 + of_core
@@ -362,6 +382,7 @@
         parts.append([send(part.at[n, side], inbox.at[n, side], at_y(1 - 2 * side)) for side in range(2)])
 
     arrivals = []
+    gated_on = []
     homes = []
 
     def total_up(n):
@@ -378,10 +399,23 @@
         result = back * near_gate[d].astype(jnp.float32)
         gated[n] = result.astype(BF).reshape(gated.shape[1:])
         gated_in[z, n] = gated[n, z]
-        if n:
-            some = pl.ds(0, 2) if n == 1 else pl.ds(n, 1)
+        if n == 1:
+
+            def pick(part):
+                return pl.ds(0, 2) if part is None else pl.ds(part, 1)
+
+            there, forward_on = ring_z(
+                lambda d, part: gated.at[pick(part), zmod(d)],
+                lambda origin, part: gated_in.at[origin, pick(part)],
+                lambda part: held.at[2, part, pl.ds(0, 1)],
+            )
+            arrivals.append(there)
+            gated_on.append(forward_on)
+        if n > 1:
+            some = pl.ds(n, 1)
+            arrivals.append([])
             for d in range(1, ZS):
-                arrivals.append(send(gated.at[some, zmod(d)], gated_in.at[z, some], at_z(d)))
+                arrivals[-1].append(send(gated.at[some, zmod(d)], gated_in.at[z, some], at_z(d)))
         back_bf[n] = back.astype(BF)
 
     inner = g_ring.shape[2]
@@ -392,6 +426,7 @@
         return lambda at: pair_in[i, :, :, :, at].reshape(rows, CHUNK)
 
     early = len(copies)
+    filters_on()
     pass_on(0)
     pass_on(1)
     pass_on(2)
@@ -399,8 +434,10 @@
     pass_on(3)
     total_up(1)
     total_up(2)
+    product_on()
+    total_up(3)
+    gated_on[0]()
     pair_x(1)
-    total_up(3)
     pair_x(0)
     for copy in table_loads:
         copy.wait()
@@ -417,7 +454,7 @@
             blocks.append(gated_in[:, 2 * e - e // 2 - 4 * (e // 3), :, at])
         return jnp.stack(blocks, 1).reshape(rows, CHUNK)
 
-    for copy in arrivals:
+    for copy in sum(arrivals, []):
         copy.wait_recv()
     forward(
         gated_block,
@@ -431,6 +468,7 @@
     )
     scale = jnp.sum(jnp.where(pick, skip_ref[pl.ds(x, 1), :], 0.0), axis=1, keepdims=True)
     gone = []
+    gone_on = []
     turns = []
 
     def turn_x(k):
@@ -461,12 +499,21 @@
             leaving[which, :, :, :, at] = out.astype(BF).reshape(ZS, XS, width, CHUNK)
         at = pl.ds(start, size)
         groups.append((which, at))
-        gone.append(
-            [
-                send(leaving.at[which, zmod(d), :, :, at], landed.at[which, z, :, :, at], at_z(d))
-                for d in range(1, ZS)
-            ]
-        )
+        if which and start:
+            gone.append(
+                [
+                    send(leaving.at[which, zmod(d), :, :, at], landed.at[which, z, :, :, at], at_z(d))
+                    for d in range(1, ZS)
+                ]
+            )
+        else:
+            there, forward_on = ring_z(
+                lambda d, n: leaving.at[which, zmod(d), half_at(n), :, at],
+                lambda origin, n: landed.at[which, origin, half_at(n), :, at],
+                lambda n: held.at[3 + which, n, :, :, at],
+            )
+            gone.append(there)
+            gone_on.append(forward_on)
         landed[which, z, :, :, at] = leaving[which, z, :, :, at]
 
     leave(0, 0, inner)
@@ -476,9 +523,11 @@
     for n, off in enumerate(offsets):
         if n:
             homes.append(send(back_bf.at[n], home_out.at[x], at_x(off)))
+    gone_on[0]()
     middle = len(copies)
     leave(1, 0, CHUNK)
     leave(1, CHUNK, CHUNK)
+    gone_on[1]()
     turn_x(0)
     flush(middle)
     turn_x(1)
@@ -500,7 +549,7 @@
     tables = (*into, *out_of, cos, sin, *across, fourth)
     spec_rows = cos.shape[0]
     split = (XS, ZS, width, inner)
-    count = 121
+    count = 136
 
     def vmem(shape, dtype=BF):
         return pltpu.VMEM(shape, dtype)
@@ -549,6 +598,7 @@
             spec,
             vmem((2, ZS, XS, width, inner)),
             vmem((2, ZS, XS, width, inner)),
+            vmem((5, 2, XS // 2, width, inner)),
             pltpu.SemaphoreType.DMA((count,)),
             pltpu.SemaphoreType.DMA((count,)),
             pltpu.SemaphoreType.DMA((19,)),

time: 106 us -> 109 us (1.028); the launches traced: 105 us -> 109 us
  Pallas kernels: 100 us -> 105 us
    pallas_call x1, Pallas kernels: 100 us -> 105 us  [layer(): pl.pallas_call(layer_kernel, out_shape=[jax.ShapeDtypeStruct((XS, deep, i...]
where the time goes in v11:
time: 109 us
  Pallas kernels  105 us (96%)
  other arithmetic  3.79 us (3%)
    pallas_call x1, Pallas kernels, layer(): pl.pallas_call(layer_kernel, out_shape=[jax.ShapeDtypeStruct((XS, deep, i...  105 us
    convert_element_type x1, other arithmetic, shards(): grad_values = (wide(mixed) * wide(gate_in)).astype(BF)  2.65 us

profile of v11, /device:TPU:1, one launch (start us, length us, event | category | flops | bytes accessed | tf_op | source)
XLA Modules:
  0.0 109.3 jit_solution(3713982124642182111)
XLA Ops:
  0.6 0.0 copy-start.1
  0.6 0.0 copy-start.2
  0.7 0.0 copy-start.3
  0.7 104.8 %shard_map.192 = (bf16[4,128,512]{2,1,0:T(8,128)(2,1)}, bf16[4,8,16,512]{3,2,1,0:T(8,128)(2,1)}, bf16[4,8,16,512]{3,2,1,0:T(8,128)(2,1)}) custom-call(bf16[128,512]{1,0:T(8,128)(2,1)} %w_hbm.1, bf16[512,512]{1,0:T(8,128)(2,1)} %g_hbm.1, bf16[4,8,16,512]{3,2,1,0:T(8,128)(2,1)} %bitcast.15, bf16[4,8,16,512]{3,2,1,0:T(8,128)(2,1)} %bitcast.16, ...), custom_call_target="tpu_custom_call" | custom-call | flops 10000000000 | bytes 20000000 | tf_op jit(solution)/shard_map/pallas_call | solution.py:558
  105.5 0.0 copy-done.1
  105.5 0.0 copy-done.2
  105.5 0.0 copy-done.3
  105.5 0.0 copy-start
  105.5 2.6 %fusion.1 = (bf16[512,512]{1,0:T(8,128)(2,1)}, bf16[512,512]{1,0:T(8,128)(2,1)}, bf16[512,512]{1,0:T(8,128)(2,1)}) fusion(bf16[512,512]{1,0:T(8,128)(2,1)S(1)} %copy-done.1, bf16[4,8,16,512]{3,2,1,0:T(8,128)(2,1)} %get-tuple-element.7, bf16[512,512]{1,0:T(8,128)(2,1)S(1)} %copy-done.2, bf16[512,512]{1,0:T(8,128)(2,1)S(1)} %copy-done.3, ...), kind=kLoop, calls=%fused_computation.3 | loop fusion | flops 2883584 | bytes 4194304 | tf_op jit(solution)/shard_map/convert_element_type | solution.py:633
  108.2 0.0 copy-done
  108.2 1.1 %bitcast_convert_fusion = f32[512,512]{1,0:T(8,128)} fusion(bf16[4,8,16,512]{3,2,1,0:T(8,128)(2,1)S(1)} %copy-done), kind=kLoop, calls=%fused_computation.6 | loop fusion | flops 262144 | bytes 1572864 | tf_op jit(solution)/shard_map/convert_element_type | solution.py:629
Async XLA Ops:
  0.6 104.9 %copy-start.1 = (bf16[512,512]{1,0:T(8,128)(2,1)S(1)}, bf16[512,512]{1,0:T(8,128)(2,1)}, u32[]{:S(2)}) copy-start(bf16[512,512]{1,0:T(8,128)(2,1)} %param.19) | copy-start | bytes 1572868
  0.6 104.9 %copy-start.2 = (bf16[512,512]{1,0:T(8,128)(2,1)S(1)}, bf16[512,512]{1,0:T(8,128)(2,1)}, u32[]{:S(2)}) copy-start(bf16[512,512]{1,0:T(8,128)(2,1)} %param.21) | copy-start | bytes 1572868
  0.7 104.9 %copy-start.3 = (bf16[512,512]{1,0:T(8,128)(2,1)S(1)}, bf16[512,512]{1,0:T(8,128)(2,1)}, u32[]{:S(2)}) copy-start(bf16[512,512]{1,0:T(8,128)(2,1)} %param.22) | copy-start | bytes 1572868
  105.5 2.7 %copy-start = (bf16[4,8,16,512]{3,2,1,0:T(8,128)(2,1)S(1)}, bf16[4,8,16,512]{3,2,1,0:T(8,128)(2,1)}, u32[]{:S(2)}) copy-start(bf16[4,8,16,512]{3,2,1,0:T(8,128)(2,1)} %get-tuple-element.9) | copy-start | bytes 1572868

commit v12 on v10

--- a/solution.py
+++ b/solution.py
@@ -433,18 +433,23 @@
     gone = []
     turns = []
 
-    def turn_x(k):
-        which, at = groups[k]
-        result = (mixed_out, filters_out)[which]
+    def mixed_over_x():
+        for copy in gone[0]:
+            copy.wait_recv()
+        turns.extend(
+            send(landed.at[0, :, xmod(d)], mixed_out.at[x], at_x(d)) for d in range(1, XS)
+        )
+        stays.append(load(landed.at[0, :, x], mixed_out.at[x]))
+
+    def filters_over_z(k):
+        at = pl.ds((k - 1) * CHUNK, CHUNK)
         for copy in gone[k]:
             copy.wait_recv()
         turns.extend(
-            send(landed.at[which, :, xmod(d), :, at], result.at[x, :, :, at], at_x(d))
-            for d in range(1, XS)
+            send(landed.at[1, zmod(d), :, :, at], filters_out.at[:, z, :, at], at_z(d))
+            for d in range(1, ZS)
         )
-        stays.append(load(landed.at[which, :, x, :, at], result.at[x, :, :, at]))
-
-    groups = []
+        stays.append(load(landed.at[1, z, :, :, at], filters_out.at[:, z, :, at]))
 
     def leave(which, start, size):
         if start == 0:
@@ -460,29 +465,34 @@
                 out = out + scale * gated_block(at).reshape(out.shape).astype(jnp.float32)
             leaving[which, :, :, :, at] = out.astype(BF).reshape(ZS, XS, width, CHUNK)
         at = pl.ds(start, size)
-        groups.append((which, at))
-        gone.append(
-            [
-                send(leaving.at[which, zmod(d), :, :, at], landed.at[which, z, :, :, at], at_z(d))
-                for d in range(1, ZS)
-            ]
-        )
-        landed[which, z, :, :, at] = leaving[which, z, :, :, at]
+        if which == 0:
+            gone.append(
+                [send(leaving.at[0, zmod(d)], landed.at[0, z], at_z(d)) for d in range(1, ZS)]
+            )
+            landed[0, z] = leaving[0, z]
+        else:
+            gone.append(
+                [
+                    send(leaving.at[1, :, xmod(d), :, at], landed.at[1, :, x, :, at], at_x(d))
+                    for d in range(1, XS)
+                ]
+            )
+            landed[1, :, x, :, at] = leaving[1, :, x, :, at]
 
     leave(0, 0, inner)
     for copy in over_x[0]:
         copy.wait_recv()
     forward(pair_block(0), into, twist, fourth, across, y_ref, z_ref, spec_p)
+    middle = len(copies)
+    leave(1, 0, CHUNK)
+    leave(1, CHUNK, CHUNK)
+    filters_over_z(1)
+    filters_over_z(2)
     for n, off in enumerate(offsets):
         if n:
             homes.append(send(back_bf.at[n], home_out.at[x], at_x(off)))
-    middle = len(copies)
-    leave(1, 0, CHUNK)
-    leave(1, CHUNK, CHUNK)
-    turn_x(0)
+    mixed_over_x()
     flush(middle)
-    turn_x(1)
-    turn_x(2)
     for copy in stays:
         copy.wait()
     for copy in homes + turns:

time: 106 us -> 104 us (0.981); the launches traced: 105 us -> 104 us
  no operation moved by 1% of the time
where the time goes in v12:
time: 104 us
  Pallas kernels  99.6 us (96%)
  other arithmetic  3.79 us (4%)
    pallas_call x1, Pallas kernels, layer(): pl.pallas_call(layer_kernel, out_shape=[jax.ShapeDtypeStruct((XS, deep, i...  99.6 us
    convert_element_type x1, other arithmetic, shards(): grad_values = (wide(mixed) * wide(gate_in)).astype(BF)  2.65 us

profile of v12, /device:TPU:1, one launch (start us, length us, event | category | flops | bytes accessed | tf_op | source)
XLA Modules:
  0.0 104.1 jit_solution(5559594979137567151)
XLA Ops:
  0.6 0.0 copy-start.1
  0.6 0.0 copy-start.2
  0.7 0.0 copy-start.3
  0.7 99.6 %shard_map.192 = (bf16[4,128,512]{2,1,0:T(8,128)(2,1)}, bf16[4,8,16,512]{3,2,1,0:T(8,128)(2,1)}, bf16[4,8,16,512]{3,2,1,0:T(8,128)(2,1)}) custom-call(bf16[128,512]{1,0:T(8,128)(2,1)} %w_hbm.1, bf16[512,512]{1,0:T(8,128)(2,1)} %g_hbm.1, bf16[4,8,16,512]{3,2,1,0:T(8,128)(2,1)} %bitcast.15, bf16[4,8,16,512]{3,2,1,0:T(8,128)(2,1)} %bitcast.16, ...), custom_call_target="tpu_custom_call" | custom-call | flops 10000000000 | bytes 20000000 | tf_op jit(solution)/shard_map/pallas_call | solution.py:519
  100.3 0.0 copy-done.1
  100.3 0.0 copy-done.2
  100.3 0.0 copy-done.3
  100.3 0.0 copy-start
  100.4 2.6 %fusion.1 = (bf16[512,512]{1,0:T(8,128)(2,1)}, bf16[512,512]{1,0:T(8,128)(2,1)}, bf16[512,512]{1,0:T(8,128)(2,1)}) fusion(bf16[512,512]{1,0:T(8,128)(2,1)S(1)} %copy-done.1, bf16[4,8,16,512]{3,2,1,0:T(8,128)(2,1)} %get-tuple-element.7, bf16[512,512]{1,0:T(8,128)(2,1)S(1)} %copy-done.2, bf16[512,512]{1,0:T(8,128)(2,1)S(1)} %copy-done.3, ...), kind=kLoop, calls=%fused_computation.3 | loop fusion | flops 2883584 | bytes 4194304 | tf_op jit(solution)/shard_map/convert_element_type | solution.py:593
  103.0 0.0 copy-done
  103.0 1.1 %bitcast_convert_fusion = f32[512,512]{1,0:T(8,128)} fusion(bf16[4,8,16,512]{3,2,1,0:T(8,128)(2,1)S(1)} %copy-done), kind=kLoop, calls=%fused_computation.6 | loop fusion | flops 262144 | bytes 1572864 | tf_op jit(solution)/shard_map/convert_element_type | solution.py:589
Async XLA Ops:
  0.6 99.7 %copy-start.1 = (bf16[512,512]{1,0:T(8,128)(2,1)S(1)}, bf16[512,512]{1,0:T(8,128)(2,1)}, u32[]{:S(2)}) copy-start(bf16[512,512]{1,0:T(8,128)(2,1)} %param.19) | copy-start | bytes 1572868
  0.6 99.7 %copy-start.2 = (bf16[512,512]{1,0:T(8,128)(2,1)S(1)}, bf16[512,512]{1,0:T(8,128)(2,1)}, u32[]{:S(2)}) copy-start(bf16[512,512]{1,0:T(8,128)(2,1)} %param.21) | copy-start | bytes 1572868
  0.7 99.7 %copy-start.3 = (bf16[512,512]{1,0:T(8,128)(2,1)S(1)}, bf16[512,512]{1,0:T(8,128)(2,1)}, u32[]{:S(2)}) copy-start(bf16[512,512]{1,0:T(8,128)(2,1)} %param.22) | copy-start | bytes 1572868
  100.3 2.7 %copy-start = (bf16[4,8,16,512]{3,2,1,0:T(8,128)(2,1)S(1)}, bf16[4,8,16,512]{3,2,1,0:T(8,128)(2,1)}, u32[]{:S(2)}) copy-start(bf16[4,8,16,512]{3,2,1,0:T(8,128)(2,1)} %get-tuple-element.9) | copy-start | bytes 1572868

commit v13 on v12

--- a/solution.py
+++ b/solution.py
@@ -281,32 +281,39 @@
     far_low = send(g_ring.at[xmod(1), low], g_ring.at[xmod(1), low], at_x(-1))
     step(2)
     step(3)
-    over_z = {}
-    over_x = {}
-
-    def pair_z(i, start, size):
+    product_x = [
+        send(stage.at[0, xmod(d)], crossed.at[0, :, x], at_x(d)) for d in range(1, XS)
+    ]
+    crossed[0, :, x] = stage[0, x]
+    product_z = []
+
+    def product_over_z(start, size):
         at = pl.ds(start, size)
-        over_z.setdefault(i, []).extend(
-            send(stage.at[i, at, zmod(d)], crossed.at[i, z, at], at_z(d)) for d in range(1, ZS)
+        product_z.extend(
+            send(crossed.at[0, zmod(d), at], pair_in.at[0, z, at], at_z(d)) for d in range(1, ZS)
         )
-        crossed[i, z, at] = stage[i, at, z]
-
-    def pair_x(i):
-        for copy in over_z[i]:
+        pair_in[0, z, at] = crossed[0, z, at]
+
+    filters_z = [
+        send(stage.at[1, :, zmod(d)], crossed.at[1, z], at_z(d)) for d in range(1, ZS)
+    ]
+    crossed[1, z] = stage[1, :, z]
+    filters_x = []
+
+    def filters_over_x():
+        for copy in filters_z:
             copy.wait_recv()
-        over_x[i] = [
-            send(crossed.at[i, :, xmod(d)], pair_in.at[i, :, x], at_x(d)) for d in range(1, XS)
-        ]
-        pair_in[i, :, x] = crossed[i, :, x]
-
-    pair_z(1, 0, XS)
+        filters_x.extend(
+            send(crossed.at[1, :, xmod(d)], pair_in.at[1, :, x], at_x(d)) for d in range(1, XS)
+        )
+        pair_in[1, :, x] = crossed[1, :, x]
+
     right_low.wait_recv()
     shared.append(send(g_ring.at[xmod(-1)], g_other.at[1], sibling))
     left_top.wait_recv()
     shared.append(send(g_ring.at[xmod(1)], g_other.at[2], sibling))
     g_load.wait()
     step(4)
-    pair_z(0, 0, XS)
 
     def rows_for(d, of_core):
         return lax.rem(y + d, YS) * 2 + of_core
@@ -392,6 +399,9 @@
         return lambda at: pair_in[i, :, :, :, at].reshape(rows, CHUNK)
 
     early = len(copies)
+    for copy in product_x:
+        copy.wait_recv()
+    product_over_z(0, XS // 2)
     pass_on(0)
     pass_on(1)
     pass_on(2)
@@ -399,12 +409,12 @@
     pass_on(3)
     total_up(1)
     total_up(2)
-    pair_x(1)
+    filters_over_x()
     total_up(3)
-    pair_x(0)
+    product_over_z(XS // 2, XS // 2)
     for copy in table_loads:
         copy.wait()
-    for copy in over_x[1]:
+    for copy in filters_x:
         copy.wait_recv()
     forward(pair_block(1), into, twist, fourth, across, y_ref, z_ref, spec_f)
     stays = [load(back_bf.at[0], home_out.at[x])]
@@ -480,7 +490,7 @@
             landed[1, :, x, :, at] = leaving[1, :, x, :, at]
 
     leave(0, 0, inner)
-    for copy in over_x[0]:
+    for copy in product_z:
         copy.wait_recv()
     forward(pair_block(0), into, twist, fourth, across, y_ref, z_ref, spec_p)
     middle = len(copies)
@@ -510,7 +520,7 @@
     tables = (*into, *out_of, cos, sin, *across, fourth)
     spec_rows = cos.shape[0]
     split = (XS, ZS, width, inner)
-    count = 121
+    count = 128
 
     def vmem(shape, dtype=BF):
         return pltpu.VMEM(shape, dtype)

time: 104 us -> 105 us (level)
  no operation moved by 1% of the time
where the time goes in v13:
time: 105 us
  Pallas kernels  100 us (95%)
  other arithmetic  3.79 us (4%)
    pallas_call x1, Pallas kernels, layer(): pl.pallas_call(layer_kernel, out_shape=[jax.ShapeDtypeStruct((XS, deep, i...  100 us
    convert_element_type x1, other arithmetic, shards(): grad_values = (wide(mixed) * wide(gate_in)).astype(BF)  2.65 us

profile of v13, /device:TPU:1, one launch (start us, length us, event | category | flops | bytes accessed | tf_op | source)
XLA Modules:
  0.0 104.6 jit_solution(12305079920168291356)
XLA Ops:
  0.6 0.0 copy-start.1
  0.6 0.0 copy-start.2
  0.7 0.0 copy-start.3
  0.7 100.1 %shard_map.192 = (bf16[4,128,512]{2,1,0:T(8,128)(2,1)}, bf16[4,8,16,512]{3,2,1,0:T(8,128)(2,1)}, bf16[4,8,16,512]{3,2,1,0:T(8,128)(2,1)}) custom-call(bf16[128,512]{1,0:T(8,128)(2,1)} %w_hbm.1, bf16[512,512]{1,0:T(8,128)(2,1)} %g_hbm.1, bf16[4,8,16,512]{3,2,1,0:T(8,128)(2,1)} %bitcast.15, bf16[4,8,16,512]{3,2,1,0:T(8,128)(2,1)} %bitcast.16, ...), custom_call_target="tpu_custom_call" | custom-call | flops 10000000000 | bytes 20000000 | tf_op jit(solution)/shard_map/pallas_call | solution.py:529
  100.7 0.0 copy-done.1
  100.8 0.0 copy-done.2
  100.8 0.0 copy-done.3
  100.8 0.0 copy-start
  100.8 2.6 %fusion.1 = (bf16[512,512]{1,0:T(8,128)(2,1)}, bf16[512,512]{1,0:T(8,128)(2,1)}, bf16[512,512]{1,0:T(8,128)(2,1)}) fusion(bf16[512,512]{1,0:T(8,128)(2,1)S(1)} %copy-done.1, bf16[4,8,16,512]{3,2,1,0:T(8,128)(2,1)} %get-tuple-element.7, bf16[512,512]{1,0:T(8,128)(2,1)S(1)} %copy-done.2, bf16[512,512]{1,0:T(8,128)(2,1)S(1)} %copy-done.3, ...), kind=kLoop, calls=%fused_computation.3 | loop fusion | flops 2883584 | bytes 4194304 | tf_op jit(solution)/shard_map/convert_element_type | solution.py:603
  103.4 0.0 copy-done
  103.4 1.1 %bitcast_convert_fusion = f32[512,512]{1,0:T(8,128)} fusion(bf16[4,8,16,512]{3,2,1,0:T(8,128)(2,1)S(1)} %copy-done), kind=kLoop, calls=%fused_computation.6 | loop fusion | flops 262144 | bytes 1572864 | tf_op jit(solution)/shard_map/convert_element_type | solution.py:599
Async XLA Ops:
  0.6 100.1 %copy-start.1 = (bf16[512,512]{1,0:T(8,128)(2,1)S(1)}, bf16[512,512]{1,0:T(8,128)(2,1)}, u32[]{:S(2)}) copy-start(bf16[512,512]{1,0:T(8,128)(2,1)} %param.19) | copy-start | bytes 1572868
  0.6 100.1 %copy-start.2 = (bf16[512,512]{1,0:T(8,128)(2,1)S(1)}, bf16[512,512]{1,0:T(8,128)(2,1)}, u32[]{:S(2)}) copy-start(bf16[512,512]{1,0:T(8,128)(2,1)} %param.21) | copy-start | bytes 1572868
  0.7 100.1 %copy-start.3 = (bf16[512,512]{1,0:T(8,128)(2,1)S(1)}, bf16[512,512]{1,0:T(8,128)(2,1)}, u32[]{:S(2)}) copy-start(bf16[512,512]{1,0:T(8,128)(2,1)} %param.22) | copy-start | bytes 1572868
  100.8 2.7 %copy-start = (bf16[4,8,16,512]{3,2,1,0:T(8,128)(2,1)S(1)}, bf16[4,8,16,512]{3,2,1,0:T(8,128)(2,1)}, u32[]{:S(2)}) copy-start(bf16[4,8,16,512]{3,2,1,0:T(8,128)(2,1)} %get-tuple-element.9) | copy-start | bytes 1572868

commit v14 on v13

--- a/solution.py
+++ b/solution.py
@@ -161,7 +161,7 @@
     in_hi_h, in_lo_h, of_hi_h, of_lo_h, cos_h, sin_h, ac_hi_h, ac_lo_h, fourth_h,
     home_out, filters_out, mixed_out,
     gate_in, values, filters, in_hi, in_lo, of_hi, of_lo, cos, sin, ac_hi, ac_lo, fourth,
-    w_ring, w_mine, w_other, g_ring, g_other, own, hold, part, inbox, relay, final,
+    w_ring, w_mine, w_other, g_own, g_ring, g_other, own, hold, part, inbox, relay, final,
     near_gate, back_bf, gated, gated_in, stage, crossed, pair_in,
     y_ref, z_ref, u_ref, spec_r, spec_g, spec_p, spec_f, leaving, landed,
     send_sems, recv_sems, local_sems,
@@ -202,7 +202,7 @@
         return copy
 
     w_load = load(w_hbm, w_ring.at[z])
-    g_load = load(g_hbm, g_ring.at[x])
+    g_load = load(g_hbm, g_own)
     pair_loads = [load(gate_in_hbm, gate_in), load(values_hbm, values), load(filters_hbm, filters)]
     gate_load = load(gate_out_hbm.at[x], near_gate.at[0])
     table_loads = [
@@ -244,11 +244,14 @@
         for way in (1, -1):
             rows = halves[side if way == 1 else 1 - side]
             ring[way, side] = send(w_hbm.at[rows], w_ring.at[z, rows], at_z(way))
-    right_top = send(g_hbm.at[top], g_ring.at[x, top], at_x(1))
-    left_low = send(g_hbm.at[low], g_ring.at[x, low], at_x(-1))
-    right_low = send(g_hbm.at[low], g_ring.at[x, low], at_x(1))
-    left_top = send(g_hbm.at[top], g_ring.at[x, top], at_x(-1))
-    shared = [send(g_hbm, g_other.at[0], sibling)]
+    g_load.wait()
+    for part_of in (top, low):
+        g_ring[x, part_of, :] = g_own[:, part_of].astype(jnp.float32).T.astype(BF)
+    right_top = send(g_ring.at[x, top], g_ring.at[x, top], at_x(1))
+    left_low = send(g_ring.at[x, low], g_ring.at[x, low], at_x(-1))
+    right_low = send(g_ring.at[x, low], g_ring.at[x, low], at_x(1))
+    left_top = send(g_ring.at[x, top], g_ring.at[x, top], at_x(-1))
+    shared = [send(g_ring.at[x], g_other.at[0], sibling)]
     w_load.wait()
     for copy in pair_loads:
         copy.wait()
@@ -312,7 +315,6 @@
     shared.append(send(g_ring.at[xmod(-1)], g_other.at[1], sibling))
     left_top.wait_recv()
     shared.append(send(g_ring.at[xmod(1)], g_other.at[2], sibling))
-    g_load.wait()
     step(4)
 
     def rows_for(d, of_core):
@@ -346,17 +348,11 @@
             shared.append(send(g_ring.at[xmod(2)], g_other.at[3], sibling))
         shared[n].wait_recv()
 
-        @pl.loop(0, g_ring.shape[1] // CHUNK)
+        @pl.loop(0, g_ring.shape[2] // CHUNK)
         def _(i, n=n, off=off):
             at = pl.ds(pl.multiple_of(i * CHUNK, CHUNK), CHUNK)
-            form = (((1,), (1,)), ((), ()))
-            total = lax.dot_general(
-                w_mine[...].reshape(wide), g_ring[xmod(off), at, :], form,
-                preferred_element_type=jnp.float32,
-            ) + lax.dot_general(
-                w_other[...].reshape(wide), g_other[n, at, :], form,
-                preferred_element_type=jnp.float32,
-            )
+            total = dot(w_mine[...].reshape(wide), g_ring[xmod(off), :, at])
+            total = total + dot(w_other[...].reshape(wide), g_other[n, :, at])
             total = total.reshape(YS, deep, CHUNK)
             own[n, :, at] = total[0]
             hold[n, 0, :, at] = total[1, :half_w]
@@ -391,8 +387,8 @@
                 arrivals.append(send(gated.at[some, zmod(d)], gated_in.at[z, some], at_z(d)))
         back_bf[n] = back.astype(BF)
 
-    inner = g_ring.shape[2]
-    rows = g_ring.shape[1]
+    inner = own.shape[2]
+    rows = gated_in.shape[0] * gated_in.shape[1] * gated_in.shape[2]
     into, twist, across = (in_hi, in_lo), (cos, sin), (ac_hi, ac_lo)
 
     def pair_block(i):
@@ -545,8 +541,9 @@
             vmem((ZS, deep, wide)),
             vmem((YS, deep, wide)),
             vmem((YS, deep, wide)),
-            vmem((XS,) + grad_out.shape),
-            vmem((XS,) + grad_out.shape),
+            vmem(grad_out.shape),
+            vmem((XS,) + grad_out.shape[::-1]),
+            vmem((XS,) + grad_out.shape[::-1]),
             vmem((XS, deep, inner), jnp.float32),
             vmem((XS, 2, deep // 2, inner), jnp.float32),
             vmem((XS, 2, 2, deep // 2, inner)),

time: 105 us -> 105 us (level)
  no operation moved by 1% of the time
where the time goes in v14:
time: 105 us
  Pallas kernels  100 us (95%)
  other arithmetic  3.79 us (4%)
    pallas_call x1, Pallas kernels, layer(): pl.pallas_call(layer_kernel, out_shape=[jax.ShapeDtypeStruct((XS, deep, i...  100 us
    convert_element_type x1, other arithmetic, shards(): grad_values = (wide(mixed) * wide(gate_in)).astype(BF)  2.65 us

profile of v14, /device:TPU:1, one launch (start us, length us, event | category | flops | bytes accessed | tf_op | source)
XLA Modules:
  0.0 104.8 jit_solution(9024145815683382246)
XLA Ops:
  0.6 0.0 copy-start.1
  0.6 0.0 copy-start.2
  0.7 0.0 copy-start.3
  0.7 100.2 %shard_map.192 = (bf16[4,128,512]{2,1,0:T(8,128)(2,1)}, bf16[4,8,16,512]{3,2,1,0:T(8,128)(2,1)}, bf16[4,8,16,512]{3,2,1,0:T(8,128)(2,1)}) custom-call(bf16[128,512]{1,0:T(8,128)(2,1)} %w_hbm.1, bf16[512,512]{1,0:T(8,128)(2,1)} %g_hbm.1, bf16[4,8,16,512]{3,2,1,0:T(8,128)(2,1)} %bitcast.15, bf16[4,8,16,512]{3,2,1,0:T(8,128)(2,1)} %bitcast.16, ...), custom_call_target="tpu_custom_call" | custom-call | flops 10000000000 | bytes 20000000 | tf_op jit(solution)/shard_map/pallas_call | solution.py:525
  100.9 0.0 copy-done.1
  100.9 0.0 copy-done.2
  100.9 0.0 copy-done.3
  101.0 0.0 copy-start
  101.0 2.6 %fusion.1 = (bf16[512,512]{1,0:T(8,128)(2,1)}, bf16[512,512]{1,0:T(8,128)(2,1)}, bf16[512,512]{1,0:T(8,128)(2,1)}) fusion(bf16[512,512]{1,0:T(8,128)(2,1)S(1)} %copy-done.1, bf16[4,8,16,512]{3,2,1,0:T(8,128)(2,1)} %get-tuple-element.7, bf16[512,512]{1,0:T(8,128)(2,1)S(1)} %copy-done.2, bf16[512,512]{1,0:T(8,128)(2,1)S(1)} %copy-done.3, ...), kind=kLoop, calls=%fused_computation.3 | loop fusion | flops 2883584 | bytes 4194304 | tf_op jit(solution)/shard_map/convert_element_type | solution.py:600
  103.6 0.0 copy-done
  103.6 1.1 %bitcast_convert_fusion = f32[512,512]{1,0:T(8,128)} fusion(bf16[4,8,16,512]{3,2,1,0:T(8,128)(2,1)S(1)} %copy-done), kind=kLoop, calls=%fused_computation.6 | loop fusion | flops 262144 | bytes 1572864 | tf_op jit(solution)/shard_map/convert_element_type | solution.py:596
Async XLA Ops:
  0.6 100.3 %copy-start.1 = (bf16[512,512]{1,0:T(8,128)(2,1)S(1)}, bf16[512,512]{1,0:T(8,128)(2,1)}, u32[]{:S(2)}) copy-start(bf16[512,512]{1,0:T(8,128)(2,1)} %param.19) | copy-start | bytes 1572868
  0.6 100.3 %copy-start.2 = (bf16[512,512]{1,0:T(8,128)(2,1)S(1)}, bf16[512,512]{1,0:T(8,128)(2,1)}, u32[]{:S(2)}) copy-start(bf16[512,512]{1,0:T(8,128)(2,1)} %param.21) | copy-start | bytes 1572868
  0.7 100.3 %copy-start.3 = (bf16[512,512]{1,0:T(8,128)(2,1)S(1)}, bf16[512,512]{1,0:T(8,128)(2,1)}, u32[]{:S(2)}) copy-start(bf16[512,512]{1,0:T(8,128)(2,1)} %param.22) | copy-start | bytes 1572868
  101.0 2.7 %copy-start = (bf16[4,8,16,512]{3,2,1,0:T(8,128)(2,1)S(1)}, bf16[4,8,16,512]{3,2,1,0:T(8,128)(2,1)}, u32[]{:S(2)}) copy-start(bf16[4,8,16,512]{3,2,1,0:T(8,128)(2,1)} %get-tuple-element.9) | copy-start | bytes 1572868

commit v15 on v14

--- a/solution.py
+++ b/solution.py
@@ -414,6 +414,9 @@
         copy.wait_recv()
     forward(pair_block(1), into, twist, fourth, across, y_ref, z_ref, spec_f)
     stays = [load(back_bf.at[0], home_out.at[x])]
+    for n, off in enumerate(offsets):
+        if n:
+            homes.append(send(back_bf.at[n], home_out.at[x], at_x(off)))
     flush(early)
 
     def gated_block(at):
@@ -494,9 +497,6 @@
     leave(1, CHUNK, CHUNK)
     filters_over_z(1)
     filters_over_z(2)
-    for n, off in enumerate(offsets):
-        if n:
-            homes.append(send(back_bf.at[n], home_out.at[x], at_x(off)))
     mixed_over_x()
     flush(middle)
     for copy in stays:
@@ -586,19 +586,68 @@
     )
 
 
+def finish_kernel(*refs):
+    sources, results = refs[:6], refs[6:10]
+    held, done, sems = refs[10:16], refs[16:20], refs[20]
+    mixed, values, gate_in, home, conv_out, filters = held
+    order = (3, 4, 0, 1, 2, 5)
+    loads = {n: pltpu.make_async_copy(sources[n], held[n], sems.at[n]) for n in order}
+    for n in order:
+        loads[n].start()
+    stores = []
+
+    def close(n, needs, left, right):
+        for need in needs:
+            loads[need].wait()
+
+        @pl.loop(0, left.shape[0] // 64)
+        def _(i):
+            at = pl.ds(pl.multiple_of(i * 64, 64), 64)
+            value = left[at, :].astype(jnp.float32)
+            if right is not None:
+                value = value * right[at, :].astype(jnp.float32)
+            done[n][at, :] = value.astype(done[n].dtype)
+
+        stores.append(pltpu.make_async_copy(done[n], results[n], sems.at[6 + n]))
+        stores[-1].start()
+
+    close(2, (3, 4), home, conv_out)
+    close(0, (0, 1), mixed, values)
+    close(1, (2,), mixed, gate_in)
+    close(3, (5,), filters, None)
+    for store in stores:
+        store.wait()
+
+
+def finish(*arrays):
+    shape = arrays[0].shape
+    outs = [jax.ShapeDtypeStruct(shape, t) for t in (BF, BF, BF, jnp.float32)]
+    hbm = pl.BlockSpec(memory_space=pl.ANY)
+    return tuple(
+        pl.pallas_call(
+            finish_kernel,
+            out_shape=outs,
+            in_specs=[hbm] * 6,
+            out_specs=[hbm] * 4,
+            scratch_shapes=[pltpu.VMEM(shape, BF)] * 6
+            + [pltpu.VMEM(o.shape, o.dtype) for o in outs]
+            + [pltpu.SemaphoreType.DMA((10,))],
+            compiler_params=pltpu.CompilerParams(vmem_limit_bytes=62 * 1024 * 1024),
+            cost_estimate=pl.CostEstimate(flops=10**6, bytes_accessed=6 * 10**6, transcendentals=0),
+        )(*arrays)
+    )
+
+
 def shards(grad_out, out_weight, gate_in, gate_out, values, conv_out, filters, skip_scale):
     rows, inner = gate_in.shape
     home, grad_filters, mixed = layer(
         grad_out, out_weight, gate_in, gate_out, values, filters, skip_scale
     )
 
-    def wide(block):
-        return block.reshape(rows, inner).astype(jnp.float32)
-
-    grad_gate_out = (wide(home) * wide(conv_out)).astype(BF)
-    grad_gate_in = (wide(mixed) * wide(values)).astype(BF)
-    grad_values = (wide(mixed) * wide(gate_in)).astype(BF)
-    return (grad_gate_in, grad_values, grad_gate_out, wide(grad_filters))
+    return finish(
+        mixed.reshape(rows, inner), values, gate_in, home.reshape(rows, inner), conv_out,
+        grad_filters.reshape(rows, inner),
+    )
 
 
 def solution(mesh):

time: 105 us -> 103 us (0.981)
  other arithmetic: 3.79 us -> 0 us
  Pallas kernels: 100 us -> 102 us
    convert_element_type x2 -> x0, other arithmetic: 3.79 us -> none  [the longest x1 2.65 us: shards(): grad_values = (wide(mixed) * wide(gate_in)).astype(BF)]
    pallas_call x0 -> x1, Pallas kernels: none -> 3.08 us  [finish(): pl.pallas_call(finish_kernel, out_shape=outs, in_specs=[hbm] * 6, out_spe...]
    pallas_call x1, Pallas kernels: 100 us -> 98.8 us  [layer(): pl.pallas_call(layer_kernel, out_shape=[jax.ShapeDtypeStruct((XS, deep, i...]
where the time goes in v15:
time: 103 us
  Pallas kernels  102 us (99%)
    pallas_call x1, Pallas kernels, layer(): pl.pallas_call(layer_kernel, out_shape=[jax.ShapeDtypeStruct((XS, deep, i...  98.8 us
    pallas_call x1, Pallas kernels, finish(): pl.pallas_call(finish_kernel, out_shape=outs, in_specs=[hbm] * 6, out_spe...  3.08 us

profile of v15, /device:TPU:1, one launch (start us, length us, event | category | flops | bytes accessed | tf_op | source)
XLA Modules:
  0.0 102.5 jit_solution(3220852526921103358)
XLA Ops:
  0.6 98.8 %shard_map.192 = (bf16[4,128,512]{2,1,0:T(8,128)(2,1)}, bf16[4,8,16,512]{3,2,1,0:T(8,128)(2,1)}, bf16[4,8,16,512]{3,2,1,0:T(8,128)(2,1)}) custom-call(bf16[128,512]{1,0:T(8,128)(2,1)} %w_hbm.1, bf16[512,512]{1,0:T(8,128)(2,1)} %g_hbm.1, bf16[4,8,16,512]{3,2,1,0:T(8,128)(2,1)} %bitcast.8, bf16[4,8,16,512]{3,2,1,0:T(8,128)(2,1)} %bitcast.9, ...), custom_call_target="tpu_custom_call" | custom-call | flops 10000000000 | bytes 20000000 | tf_op jit(solution)/shard_map/pallas_call | solution.py:525
  99.4 3.1 %shard_map.193 = (bf16[512,512]{1,0:T(8,128)(2,1)}, bf16[512,512]{1,0:T(8,128)(2,1)}, bf16[512,512]{1,0:T(8,128)(2,1)}, f32[512,512]{1,0:T(8,128)}) custom-call(bf16[512,512]{1,0:T(8,128)(2,1)} %bitcast.12, bf16[512,512]{1,0:T(8,128)(2,1)} %refs_1_.1, bf16[512,512]{1,0:T(8,128)(2,1)} %refs_2_.1, bf16[512,512]{1,0:T(8,128)(2,1)} %bitcast.10, ...), custom_call_target="tpu_custom_call" | custom-call | flops 1000000 | bytes 6000000 | tf_op jit(solution)/shard_map/pallas_call | solution.py:627

commit v16 on v15

--- a/solution.py
+++ b/solution.py
@@ -284,9 +284,7 @@
     far_low = send(g_ring.at[xmod(1), low], g_ring.at[xmod(1), low], at_x(-1))
     step(2)
     step(3)
-    product_x = [
-        send(stage.at[0, xmod(d)], crossed.at[0, :, x], at_x(d)) for d in range(1, XS)
-    ]
+    product_x = []
     crossed[0, :, x] = stage[0, x]
     product_z = []
 
@@ -344,6 +342,9 @@
             far_low.wait_recv()
             gates.extend(
                 send(gate_out_hbm.at[xmod(d)], near_gate.at[d], at_x(d)) for d in range(1, XS)
+            )
+            product_x.extend(
+                send(stage.at[0, xmod(d)], crossed.at[0, :, x], at_x(d)) for d in range(1, XS)
             )
             shared.append(send(g_ring.at[xmod(2)], g_other.at[3], sibling))
         shared[n].wait_recv()
@@ -395,15 +396,15 @@
         return lambda at: pair_in[i, :, :, :, at].reshape(rows, CHUNK)
 
     early = len(copies)
-    for copy in product_x:
-        copy.wait_recv()
-    product_over_z(0, XS // 2)
     pass_on(0)
     pass_on(1)
     pass_on(2)
     total_up(0)
     pass_on(3)
     total_up(1)
+    for copy in product_x:
+        copy.wait_recv()
+    product_over_z(0, XS // 2)
     total_up(2)
     filters_over_x()
     total_up(3)

time: 103 us -> 108 us (1.049)
  Pallas kernels: 102 us -> 108 us
    pallas_call x1, Pallas kernels: 98.8 us -> 104 us  [layer(): pl.pallas_call(layer_kernel, out_shape=[jax.ShapeDtypeStruct((XS, deep, i...]
where the time goes in v16:
time: 108 us
  Pallas kernels  108 us (100%)
    pallas_call x1, Pallas kernels, layer(): pl.pallas_call(layer_kernel, out_shape=[jax.ShapeDtypeStruct((XS, deep, i...  104 us
    pallas_call x1, Pallas kernels, finish(): pl.pallas_call(finish_kernel, out_shape=outs, in_specs=[hbm] * 6, out_spe...  3.08 us

profile of v16, /device:TPU:1, one launch (start us, length us, event | category | flops | bytes accessed | tf_op | source)
XLA Modules:
  0.0 108.2 jit_solution(12094983251772503958)
XLA Ops:
  0.6 104.4 %shard_map.192 = (bf16[4,128,512]{2,1,0:T(8,128)(2,1)}, bf16[4,8,16,512]{3,2,1,0:T(8,128)(2,1)}, bf16[4,8,16,512]{3,2,1,0:T(8,128)(2,1)}) custom-call(bf16[128,512]{1,0:T(8,128)(2,1)} %w_hbm.1, bf16[512,512]{1,0:T(8,128)(2,1)} %g_hbm.1, bf16[4,8,16,512]{3,2,1,0:T(8,128)(2,1)} %bitcast.8, bf16[4,8,16,512]{3,2,1,0:T(8,128)(2,1)} %bitcast.9, ...), custom_call_target="tpu_custom_call" | custom-call | flops 10000000000 | bytes 20000000 | tf_op jit(solution)/shard_map/pallas_call | solution.py:526
  105.1 3.1 %shard_map.193 = (bf16[512,512]{1,0:T(8,128)(2,1)}, bf16[512,512]{1,0:T(8,128)(2,1)}, bf16[512,512]{1,0:T(8,128)(2,1)}, f32[512,512]{1,0:T(8,128)}) custom-call(bf16[512,512]{1,0:T(8,128)(2,1)} %bitcast.12, bf16[512,512]{1,0:T(8,128)(2,1)} %refs_1_.1, bf16[512,512]{1,0:T(8,128)(2,1)} %refs_2_.1, bf16[512,512]{1,0:T(8,128)(2,1)} %bitcast.10, ...), custom_call_target="tpu_custom_call" | custom-call | flops 1000000 | bytes 6000000 | tf_op jit(solution)/shard_map/pallas_call | solution.py:628
